TPU v7x, 32 devices: a whole 2x2x4 slice. The times are simulated.
32 devices in a mesh: row: 8 (over z, x), col: 4 (over y, core).
Axes of the slice: x: 2, y: 2, z: 4, core: 2. Of those that a mesh axis runs over, the one named last changes fastest.
Arguments:
- amp_tiles: bfloat16 [2, 4, 32, 256, 256], P(None, 'col', 'row'), may hold values from -6 to 6
- amp_rows: int32 [2, 4, 32], P(None, 'col', 'row'), may hold values from -1 to 3, as said below
- int_tiles: bfloat16 [2, 8, 8, 256, 256], P(None, 'col', 'row'), may hold values from -0.1875 to 0.1875
- int_codes: int32 [2, 8, 8], P(None, 'col', 'row'), may hold values from -1 to 11, as said below
Outputs:
- ladder: float32 [4096, 12288], P('col', 'row')
Inputs may be any that keep to these rules, and one draw needn't show every extreme that they name: `amp_rows`: the live tile rows among one device's 4 amplitude slots of a panel are distinct; -1 marks an empty slot. `int_codes`: the live codes among one device's 2 integral slots of a panel are distinct; -1 marks an empty slot.
All inputs are finite; a program needn't handle non-finite values.
Results may differ from a plain program's by a relative error of at most 0.0003.
Values may be sent and summed in bfloat16 or wider, within the bound.
No kernel may reach another device: no remote copies, remote signals or barrier semaphores. Data moves between devices by JAX's collectives and lax.ppermute only.
A program may use at most 192 MiB of HBM per device.

v0:
```python
import jax
import jax.numpy as jnp
from jax import lax
from jax.sharding import PartitionSpec as P

MI = 4
NJ = 6
SA = 4


def densify(tiles, codes, per_dev, rows_held, panel_tiles, cols_tiles, width):
    slot_ids = jnp.arange(codes.shape[0], dtype=jnp.int32)
    living = codes >= 0
    k_index = jnp.where(
        living, slot_ids // per_dev * rows_held + codes // cols_tiles, panel_tiles
    ).astype(jnp.int32)
    j_index = jnp.where(living, codes % cols_tiles, 0).astype(jnp.int32)
    dense = jnp.zeros((panel_tiles, width, cols_tiles, width), jnp.bfloat16)
    dense = dense.at[k_index, :, j_index, :].set(tiles, mode="drop")
    return dense.reshape(panel_tiles, width, cols_tiles * width)


def accumulate(carry, tiles, rows, panel, per_dev):
    count = tiles.shape[0]
    groups = count // per_dev
    width = tiles.shape[1]
    row_count = carry.shape[0]
    grouped = tiles.reshape(groups, per_dev, width, width)
    slot_rows = rows.reshape(groups, per_dev)
    target = jnp.where(slot_rows >= 0, slot_rows, row_count).astype(jnp.int32)
    group_ids = jnp.broadcast_to(jnp.arange(groups, dtype=jnp.int32)[:, None], (groups, per_dev))
    placed = jnp.zeros((row_count, groups, width, width), jnp.bfloat16)
    placed = placed.at[target, group_ids].set(grouped, mode="drop")
    return carry + jnp.einsum("mgxy,gyz->mxz", placed, panel, preferred_element_type=jnp.float32)


def body(amp_tiles, amp_rows, int_tiles, int_codes):
    rows_held = lax.axis_size("row") // lax.axis_size("col")
    panel_tiles = lax.axis_size("row")
    per_amp = SA
    per_int = int_tiles.shape[1]
    width = amp_tiles.shape[3]
    total = jnp.zeros((MI, width, NJ * width), jnp.float32)
    for step in range(amp_tiles.shape[0]):
        got_tiles, got_codes = (
            lax.all_gather(int_tiles[step], "col", axis=0, tiled=True),
            lax.all_gather(int_codes[step], "col", axis=0, tiled=True),
        )
        panel = densify(
            got_tiles[:, 0], got_codes[:, 0], per_int, rows_held, panel_tiles, NJ, width
        )

        def fold_step(carry, piece, start, panel=panel):
            return accumulate(carry, piece[0][0], piece[1][0], panel, per_amp)

        total = fold_step(
            total,
            (
                lax.all_gather(amp_tiles[step], "row", axis=1, tiled=True),
                lax.all_gather(amp_rows[step], "row", axis=1, tiled=True),
            ),
            jnp.int32(0),
        )
    return total.reshape(MI * width, NJ * width)


def solution(mesh):
    return jax.shard_map(
        body,
        mesh=mesh,
        in_specs=(
            P(None, "col", "row", None, None),
            P(None, "col", "row"),
            P(None, "col", "row", None, None),
            P(None, "col", "row"),
        ),
        out_specs=P("col", "row"),
        check_vma=False,
    )
```

profile of v0, /device:TPU:0, one launch (start us, length us, event | category | flops | bytes accessed | tf_op | source)
XLA Modules:
  0.0 228.9 jit_solution(15348008958194104837)
XLA Ops:
  6.5 1.9 slice_bitcast_fusion.2
  8.4 0.0 all-gather.19.cloned.1.call-start
  8.5 0.7 all-gather.19.cloned.1.call-update
  9.2 2.3 %slice_bitcast_fusion = (bf16[1,1,4,256,256]{4,3,1,0,2:T(8,128)(2,1)}, bf16[1,1,4,256,256]{4,3,1,0,2:T(8,128)(2,1)}) fusion(bf16[2,1,4,256,256]{4,3,2,1,0:T(8,128)(2,1)} %param.4), kind=kLoop, calls=%fused_computation.5 | loop fusion | bytes 2097152
  11.6 0.0 all-gather.17.cloned.1.call-start
  11.6 0.5 all-gather.17.cloned.1.call-update
  12.1 1.3 dynamic-slice.1
  14.2 0.8 bitcast_dynamic-update-slice_fusion.2
  14.9 0.7 bitcast_dynamic-update-slice_fusion
  15.7 6.4 %all-reduce.5 = (s32[8]{0:T(128)S(1)}, s32[8]{0:T(128)S(1)}) all-reduce(s32[8]{0:T(128)S(1)} %bitcast_dynamic-update-slice_fusion.2, s32[8]{0:T(128)S(1)} %bitcast_dynamic-update-slice_fusion), channel_id=4, replica_groups=mesh['row'=8,'col'=4] {'col'}, use_global_device_ids=true, to_apply=%add.1 | all-reduce | flops 16 | bytes 128
  22.0 1.3 dynamic-slice
  24.1 0.8 bitcast_dynamic-update-slice_fusion.3
  24.8 0.7 bitcast_dynamic-update-slice_fusion.1
  25.6 11.6 %all-reduce.4 = (s32[32]{0:T(128)S(1)}, s32[32]{0:T(128)S(1)}) all-reduce(s32[32]{0:T(128)S(1)} %bitcast_dynamic-update-slice_fusion.3, s32[32]{0:T(128)S(1)} %bitcast_dynamic-update-slice_fusion.1), channel_id=2, replica_groups=mesh['row'=8,'col'=4] {'row'}, use_global_device_ids=true, to_apply=%add | all-reduce | flops 64 | bytes 512
  37.2 0.1 reshape_squeeze.12
  37.3 0.1 reshape.118
  37.3 0.1 reshape_squeeze.14
  37.4 0.1 reshape.130
  37.6 3.4 %broadcast.204.clone = bf16[8,256,6,256]{3,1,2,0:T(8,128)(2,1)} broadcast(bf16[]{:T(256)} %constant.50.clone.1), dimensions={} | broadcast | bytes 6291458 | tf_op jit(solution)/shard_map/broadcast.21
  41.1 2.8 %scatter_fusion.1 = bf16[8,256,6,256]{3,1,2,0:T(8,128)(2,1)} fusion(bf16[8,256,6,256]{3,1,2,0:T(8,128)(2,1)} %broadcast.204.clone, s32[8]{0:T(128)S(1)} %fusion.14, bf16[8,256,256]{2,1,0:T(8,128)(2,1)S(1)} %bitcast.131), kind=kCustom, calls=%fused_computation.1 | custom fusion | bytes 3145792 | tf_op jit(solution)/shard_map/scatter | solution.py:19
  43.8 8.6 %copy.11 = bf16[8,256,6,256]{1,3,2,0:T(8,128)(2,1)} copy(bf16[8,256,6,256]{3,1,2,0:T(8,128)(2,1)} %scatter_fusion.1) | data formatting | bytes 12582912 | tf_op jit(solution)/shard_map/scatter | solution.py:19
  52.5 3.4 %broadcast.204.clone.1 = bf16[8,256,6,256]{3,1,2,0:T(8,128)(2,1)} broadcast(bf16[]{:T(256)} %constant.50.clone.1), dimensions={} | broadcast | bytes 6291458 | tf_op jit(solution)/shard_map/broadcast.21
  55.9 2.8 %scatter_fusion.3 = bf16[8,256,6,256]{3,1,2,0:T(8,128)(2,1)} fusion(bf16[8,256,6,256]{3,1,2,0:T(8,128)(2,1)} %broadcast.204.clone.1, s32[8]{0:T(128)S(1)} %fusion.15, bf16[8,256,256]{2,1,0:T(8,128)(2,1)S(1)} %bitcast.132), kind=kCustom, calls=%fused_computation.3 | custom fusion | bytes 3145792 | tf_op jit(solution)/shard_map/scatter | solution.py:19
  58.8 8.6 %copy.15 = bf16[8,256,6,256]{1,3,2,0:T(8,128)(2,1)} copy(bf16[8,256,6,256]{3,1,2,0:T(8,128)(2,1)} %scatter_fusion.3) | data formatting | bytes 12582912 | tf_op jit(solution)/shard_map/scatter | solution.py:19
  67.4 55.0 %all-gather.13.cloned.1.call-done = bf16[1,1,32,256,256]{4,3,1,0,2:T(8,128)(2,1)} async-done(((bf16[1,1,4,256,256]{4,3,1,0,2:T(8,128)(2,1)}), bf16[1,1,32,256,256]{4,3,1,0,2:T(8,128)(2,1)}) %all-gather.13.cloned.1.call-update) | async-done | bytes 4194320 | tf_op jit(solution)/shard_map/all_gather | solution.py:59
  122.3 2.4 %broadcast.202.clone = bf16[4,8,256,256]{3,2,1,0:T(8,128)(2,1)} broadcast(bf16[]{:T(256)} %constant.50.clone.1), dimensions={} | broadcast | bytes 4194306 | tf_op jit(solution)/shard_map/broadcast.17
  124.8 11.2 %scatter_fusion = bf16[4,8,256,256]{3,2,1,0:T(8,128)(2,1)} fusion(bf16[4,8,256,256]{3,2,1,0:T(8,128)(2,1)} %broadcast.202.clone, s32[32]{0:T(128)S(1)} %reshape.118, bf16[32,256,256]{2,1,0:T(8,128)(2,1)} %bitcast.130), kind=kCustom, calls=%fused_computation | custom fusion | bytes 12583168 | tf_op jit(solution)/shard_map/scatter | solution.py:33
  135.9 11.7 %fusion.16 = f32[4,256,1536,1]{2,1,3,0:T(8,128)} fusion(bf16[4,8,256,256]{3,2,1,0:T(8,128)(2,1)} %scatter_fusion, bf16[8,256,1536,1]{1,2,0,3:T(8,128)(2,1)} %bitcast.128), kind=kOutput, calls=%fused_computation.61 | convolution fusion | flops 6442450944 | bytes 16777216 | tf_op jit(solution)/shard_map/mgxy,gyz->mxz/dot_general | solution.py:34
  147.7 48.4 %all-gather.17.cloned.1.call-done = bf16[1,1,32,256,256]{4,3,1,0,2:T(8,128)(2,1)} async-done(((bf16[1,1,4,256,256]{4,3,1,0,2:T(8,128)(2,1)}), bf16[1,1,32,256,256]{4,3,1,0,2:T(8,128)(2,1)}) %all-gather.17.cloned.1.call-update) | async-done | bytes 4194320 | tf_op jit(solution)/shard_map/all_gather | solution.py:59
  196.0 2.5 %broadcast.202.clone.1 = bf16[4,8,256,256]{3,2,1,0:T(8,128)(2,1)} broadcast(bf16[]{:T(256)} %constant.50.clone.1), dimensions={} | broadcast | bytes 4194306 | tf_op jit(solution)/shard_map/broadcast.17
  198.5 11.2 %scatter_fusion.2 = bf16[4,8,256,256]{3,2,1,0:T(8,128)(2,1)} fusion(bf16[4,8,256,256]{3,2,1,0:T(8,128)(2,1)} %broadcast.202.clone.1, s32[32]{0:T(128)S(1)} %reshape.130, bf16[32,256,256]{2,1,0:T(8,128)(2,1)} %bitcast.129), kind=kCustom, calls=%fused_computation.2 | custom fusion | bytes 12583168 | tf_op jit(solution)/shard_map/scatter | solution.py:33
  209.7 12.6 %bitcast_add_fusion = f32[4,256,1536]{2,1,0:T(8,128)} fusion(f32[4,256,1536,1]{2,1,3,0:T(8,128)} %fusion.16, bf16[4,8,256,256]{3,2,1,0:T(8,128)(2,1)} %scatter_fusion.2, bf16[8,256,1536,1]{1,2,0,3:T(8,128)(2,1)} %bitcast.127), kind=kOutput, calls=%fused_computation.4 | convolution fusion | flops 6444023808 | bytes 23068672 | tf_op jit(solution)/shard_map/mgxy,gyz->mxz/dot_general | solution.py:34
  (18 shorter events, 0.2 us)
Async XLA Ops:
  6.5 31.1 %all-gather.15.cloned.1.call-start = ((), (), s32[]{:S(2)}) async-start(), calls=%async_computation.1 | async-start | bytes 1310720 | tf_op jit(solution)/shard_map/all_gather | solution.py:46
  8.4 44.1 %all-gather.19.cloned.1.call-start = ((), (), s32[]{:S(2)}) async-start(), calls=%async_computation.3 | async-start | bytes 1310720 | tf_op jit(solution)/shard_map/all_gather | solution.py:46
  9.2 113.2 %all-gather.13.cloned.1.call-start = ((), (), s32[]{:S(2)}) async-start(), calls=%async_computation | async-start | bytes 4718592 | tf_op jit(solution)/shard_map/all_gather | solution.py:59
  11.6 184.5 %all-gather.17.cloned.1.call-start = ((), (), s32[]{:S(2)}) async-start(), calls=%async_computation.2 | async-start | bytes 4718592 | tf_op jit(solution)/shard_map/all_gather | solution.py:59
  37.6 3.5 %copy-start = (bf16[1,8,1,256,256]{4,3,2,0,1:T(8,128)(2,1)S(1)}, bf16[1,8,1,256,256]{4,3,2,0,1:T(8,128)(2,1)}, u32[]{:S(2)}) copy-start(bf16[1,8,1,256,256]{4,3,2,0,1:T(8,128)(2,1)} %all-gather.15.cloned.1.call-done) | copy-start | bytes 3145732
  52.5 3.5 %copy-start.1 = (bf16[1,8,1,256,256]{4,3,2,0,1:T(8,128)(2,1)S(1)}, bf16[1,8,1,256,256]{4,3,2,0,1:T(8,128)(2,1)}, u32[]{:S(2)}) copy-start(bf16[1,8,1,256,256]{4,3,2,0,1:T(8,128)(2,1)} %all-gather.19.cloned.1.call-done) | copy-start | bytes 3145732
Sparse Core Ops, SparseCore 0:
  8.9 19.5 all-gather.14
  30.0 16.7 all-gather.18
  48.9 73.3 all-gather.12
  124.3 71.6 all-gather.16
where the time goes:
time: 230 us; the launch traced here: 229 us
  waiting for transfers between devices  105 us (46%)
  local copies, waits for them, and re-layouts  67.1 us (29%)
  matrix products  24.4 us (11%)
  blocking collectives  18 us (8%)
  between operations  14.6 us (6%)
    all_gather x2, waiting for transfers between devices, body(): lax.all_gather(amp_tiles[step], 'row', axis=1, tiled=True)  103 us
    dot_general x2, matrix products, accumulate(): jnp.einsum('mgxy,gyz->mxz', placed, panel, preferred_element_type=jnp.flo...  24.4 us
    scatter x4, local copies, waits for them, and re-layouts, densify(): dense = dense.at[k_index, :, j_index, :].set(tiles, mode='drop')  22.9 us
    scatter x2, local copies, waits for them, and re-layouts, accumulate(): placed = placed.at[target, group_ids].set(grouped, mode='drop')  22.3 us
    unnamed x2, blocking collectives  18 us
    another operation x4, local copies, waits for them, and re-layouts  11.8 us
    unnamed x16, local copies, waits for them, and re-layouts  9.81 us
  transfers between devices with their start and end apart: 4, of which 2 were waited for; matrix products, arithmetic and copies ran while one was open for 28% of the time, Pallas kernels for 0%

commit v1 on v0

v1 whole, which is shorter than its diff:
```python
import functools

import jax
import jax.numpy as jnp
from jax import lax
from jax.experimental import pallas as pl
from jax.experimental.pallas import tpu as pltpu
from jax.sharding import PartitionSpec as P

MI = 4
NJ = 6
CORES = 2
GROUPS = ((0, 2), (2, 4))
VMEM_LIMIT = 8 * 1024 * 1024


def grid_cycle(depth, across):
    order = [z * across for z in range(depth)]
    for turn, z in enumerate(reversed(range(depth))):
        xs = range(1, across) if turn % 2 == 0 else range(across - 1, 0, -1)
        order += [z * across + x for x in xs]
    return order


def pick(table, index):
    value = jnp.int32(table[0])
    for at in range(1, len(table)):
        value = jnp.where(index == at, jnp.int32(table[at]), value)
    return value


def place_kernel(rows_ref, tiles_ref, *rest):
    placed, sem = rest[:-1], rest[-1]
    panels, slots, width = tiles_ref.shape[0], tiles_ref.shape[2], tiles_ref.shape[3]
    jobs = []
    for group, (first, last) in enumerate(GROUPS):
        for panel in range(panels):
            ref = placed[group * panels + panel]
            for row in range(first, last):
                slot = jnp.int32(-1)
                for at in range(slots):
                    slot = jnp.where(rows_ref[panel, 0, at] == row, at, slot)
                spot = ref.at[pl.ds((row - first) * width, width)]
                copy = pltpu.make_async_copy(
                    tiles_ref.at[panel, 0, jnp.maximum(slot, 0)], spot, sem.at[panel, row]
                )
                jobs.append((slot, spot, copy))
    for slot, spot, copy in jobs:

        @pl.when(slot >= 0)
        def _():
            copy.start()

        @pl.when(slot < 0)
        def _():
            spot[...] = jnp.zeros(spot.shape, spot.dtype)

    for slot, spot, copy in jobs:

        @pl.when(slot >= 0)
        def _():
            copy.wait()


def place(amp_tiles, amp_rows):
    panels, width = amp_tiles.shape[0], amp_tiles.shape[3]
    shapes = [
        pltpu.VMEM(((last - first) * width, width), amp_tiles.dtype)
        for first, last in GROUPS
        for _ in range(panels)
    ]
    return pl.pallas_call(
        place_kernel,
        out_shape=shapes,
        in_specs=[pl.BlockSpec(memory_space=pltpu.SMEM), pl.BlockSpec(memory_space=pl.ANY)],
        out_specs=[pl.BlockSpec(memory_space=pltpu.VMEM)] * len(shapes),
        scratch_shapes=[pltpu.SemaphoreType.DMA((panels, MI))],
        compiler_params=pltpu.CompilerParams(vmem_limit_bytes=VMEM_LIMIT),
        name="place",
    )(amp_rows, amp_tiles)


def collect_kernel(*refs):
    parts, out_ref, sem = refs[:-2], refs[-2], refs[-1]
    panels, slots = parts[0].shape[0], parts[0].shape[1]
    count = len(parts)
    col = lax.axis_index("col")
    y, core = col // CORES, lax.rem(col, CORES)
    depth = count // CORES
    copies = []
    for at, part in enumerate(parts):
        shift, flip = at // CORES, at % CORES
        owner = lax.rem(y + depth - shift, depth) * CORES + lax.rem(core + flip, CORES)
        for panel in range(panels):
            copies.append(
                pltpu.make_async_copy(
                    part.at[panel], out_ref.at[panel, pl.ds(owner * slots, slots)], sem.at[at, panel]
                )
            )
    for copy in copies:
        copy.start()
    for copy in copies:
        copy.wait()


def collect(parts):
    panels, slots, width, _ = parts[0].shape
    return pl.pallas_call(
        collect_kernel,
        out_shape=pltpu.VMEM((panels, slots * len(parts), width, width), parts[0].dtype),
        in_specs=[pl.BlockSpec(memory_space=pl.ANY)] * len(parts),
        out_specs=pl.BlockSpec(memory_space=pltpu.VMEM),
        scratch_shapes=[pltpu.SemaphoreType.DMA((len(parts), panels))],
        compiler_params=pltpu.CompilerParams(vmem_limit_bytes=VMEM_LIMIT),
        name="collect",
    )(*parts)


def chunk_updates(codes_ref, hops, order, rows_held, slots):
    me = lax.axis_index("row")
    inverse = [order.index(at) for at in range(len(order))]
    here = pick(inverse, me)
    found = []
    for panel, hop in hops:
        way = hop if panel % 2 == 0 else len(order) - hop
        source = pick(order, lax.rem(here + len(order) - way, len(order)))
        owner, held = source // rows_held, lax.rem(source, rows_held)
        for at in range(slots):
            slot = owner * slots + at
            code = codes_ref[panel, slot, 0]
            live = (code >= 0) & (code // NJ == held)
            found.append((live, slot, lax.rem(jnp.maximum(code, 0), NJ)))
    return found


def fold_kernel(first, last, hops, order, rows_held, slots, band, codes_ref, ints_ref, *refs):
    chunks = refs[: len(hops)]
    width = ints_ref.shape[2]
    if first:
        total_ref = refs[len(hops)]
        total_ref[...] = jnp.zeros(total_ref.shape, jnp.float32)
    elif last:
        total_ref, out_ref, sem = refs[len(hops)], refs[-2], refs[-1]
    else:
        total_ref = refs[-1]
    found = chunk_updates(codes_ref, hops, order, rows_held, slots)

    def send(column):
        cols = pl.ds(column * width, width)
        return pltpu.make_async_copy(
            total_ref.at[:, cols],
            out_ref.at[pl.ds(band[0], band[1]), cols],
            sem.at[column],
        )

    touched = []
    if last:
        for column in range(NJ):
            hit = False
            for live, _, at in found:
                hit = hit | (live & (at == column))
            touched.append(hit)

            @pl.when(jnp.logical_not(hit))
            def _():
                send(column).start()

    for index, (live, slot, column) in enumerate(found):
        panel, chunk = hops[index // slots][0], chunks[index // slots]

        @pl.when(live)
        def _():
            cols = pl.ds(pl.multiple_of(column * width, width), width)
            total_ref[:, cols] += jnp.dot(
                chunk[...], ints_ref[panel, slot], preferred_element_type=jnp.float32
            )

    if last:
        for column in range(NJ):

            @pl.when(touched[column])
            def _():
                send(column).start()

        for column in range(NJ):
            send(column).wait()


def in_vmem(value):
    return pltpu.with_memory_space_constraint(value, pltpu.VMEM)


def fold(codes, ints, chunks, hops, total, order, rows_held, slots, band, out=None, whole=None):
    first, last = total is None, whole is not None
    rows, width = chunks[0].shape
    vmem = pl.BlockSpec(memory_space=pltpu.VMEM)
    anywhere = pl.BlockSpec(memory_space=pl.ANY)
    operands = [codes, in_vmem(ints), *map(in_vmem, chunks)]
    in_specs = [pl.BlockSpec(memory_space=pltpu.SMEM)] + [vmem] * (1 + len(chunks))
    aliases, scratch = {}, []
    if not first:
        operands.append(in_vmem(total))
        in_specs.append(vmem)
    if last:
        out_shape, out_spec = jax.ShapeDtypeStruct(whole, jnp.float32), anywhere
        scratch = [pltpu.SemaphoreType.DMA((NJ,))]
        if out is not None:
            aliases = {len(operands): 0}
            operands.append(out)
            in_specs.append(anywhere)
    else:
        out_shape, out_spec = pltpu.VMEM((rows, NJ * width), jnp.float32), vmem
        if not first:
            aliases = {len(operands) - 1: 0}
    return pl.pallas_call(
        functools.partial(fold_kernel, first, last, hops, order, rows_held, slots, band),
        out_shape=out_shape,
        in_specs=in_specs,
        out_specs=out_spec,
        scratch_shapes=scratch,
        input_output_aliases=aliases,
        compiler_params=pltpu.CompilerParams(vmem_limit_bytes=VMEM_LIMIT),
        cost_estimate=pl.CostEstimate(
            flops=2 * rows * width * width * len(hops) * slots, bytes_accessed=rows * NJ * width * 4, transcendentals=0
        ),
        name="fold",
    )(*operands)


def body(amp_tiles, amp_rows, int_tiles, int_codes):
    n_row, n_col = lax.axis_size("row"), lax.axis_size("col")
    rows_held = n_row // n_col
    panels, slots, width = int_tiles.shape[0], int_tiles.shape[1], int_tiles.shape[3]
    across = n_col // CORES
    order = grid_cycle(n_row // across, across)
    forth = [(order[at], order[(at + 1) % n_row]) for at in range(n_row)]
    ways = [forth if panel % 2 == 0 else [(b, a) for a, b in forth] for panel in range(panels)]

    streams = place(amp_tiles, amp_rows)
    rings = []
    held = list(streams)
    rings.append(held)
    for _ in range(1, n_row):
        held = [lax.ppermute(held[at], "row", ways[at % panels]) for at in range(len(held))]
        rings.append(held)

    codes = lax.all_gather(int_codes, "col", axis=1, tiled=True)
    own = int_tiles.reshape(panels, slots, width, width)
    flip = [(c, c // CORES * CORES + (c + 1) % CORES) for c in range(n_col)]
    parts = []
    for shift in range(n_col // CORES):
        moved = own
        if shift:
            moved = lax.ppermute(own, "col", [(c, (c + shift * CORES) % n_col) for c in range(n_col)])
        parts += [moved, lax.ppermute(moved, "col", flip)]
    ints = collect(parts)

    whole = (MI * width, NJ * width)
    cuts = [0, n_row // 2, n_row - 1, n_row]
    totals = [None] * len(GROUPS)
    out = None
    for begin, end in zip(cuts[:-1], cuts[1:]):
        hops = [(panel, hop) for hop in range(begin, end) for panel in range(panels)]
        for group, (top, bottom) in enumerate(GROUPS):
            chunks = [rings[hop][group * panels + panel] for panel, hop in hops]
            band = (top * width, (bottom - top) * width)
            made = fold(
                codes, ints, chunks, hops, totals[group], order, rows_held, slots, band,
                out, whole if end == n_row else None,
            )
            if end == n_row:
                out = made
            else:
                totals[group] = made
    return out


def solution(mesh):
    return jax.shard_map(
        body,
        mesh=mesh,
        in_specs=(
            P(None, "col", "row", None, None),
            P(None, "col", "row"),
            P(None, "col", "row", None, None),
            P(None, "col", "row"),
        ),
        out_specs=P("col", "row"),
        check_vma=False,
    )
```

time: 230 us -> 95.7 us (0.42)
  waiting for transfers between devices: 105 us -> 28.5 us
  local copies, waits for them, and re-layouts: 67.1 us -> 13.1 us
  starting transfers between devices: 0.12 us -> 31.4 us
  matrix products: 24.4 us -> 0 us
  Pallas kernels: 0 us -> 17 us
  between operations: 14.6 us -> 0.28 us
  blocking collectives: 18 us -> 5.06 us
    all_gather x4 -> x0, waiting for transfers between devices: 103 us -> none  [the longest x2 103 us: body(): lax.all_gather(amp_tiles[step], 'row', axis=1, tiled=True)]
    scatter x6 -> x0, local copies, waits for them, and re-layouts: 45.2 us -> none  [the longest x4 22.9 us: densify(): dense = dense.at[k_index, :, j_index, :].set(tiles, mode='drop')]
    ppermute x0 -> x31, starting transfers between devices: none -> 31.4 us  [the longest x28 28.4 us: body(): lax.ppermute(held[at], 'row', ways[at % panels])]
    ppermute x0 -> x31, waiting for transfers between devices: none -> 28.5 us  [the longest x28 28.4 us: body(): lax.ppermute(held[at], 'row', ways[at % panels])]
    dot_general x2 -> x0, matrix products: 24.4 us -> none  [accumulate(): jnp.einsum('mgxy,gyz->mxz', placed, panel, preferred_element_type=jnp.flo...]
    unnamed x2 -> x0, blocking collectives: 18 us -> none
    pallas_call x0 -> x8, Pallas kernels: none -> 17 us  [the longest x6 15.2 us: fold(): pl.pallas_call(functools.partial(fold_kernel, first, last, hops, order, r...]
    another operation x6 -> x0, local copies, waits for them, and re-layouts: 12 us -> none
  transfers between devices with their start and end apart: 4 -> 31, of which waited for: 2 -> 10; matrix products, arithmetic and copies ran while one was open for 28% -> 1% of each run, Pallas kernels for 0% -> 15%
where the time goes in v1:
time: 95.7 us; the launch traced here: 95.3 us
  starting transfers between devices  31.4 us (33%)
  waiting for transfers between devices  28.5 us (30%)
  Pallas kernels  17 us (18%)
  local copies, waits for them, and re-layouts  13.1 us (14%)
  blocking collectives  5.06 us (5%)
    ppermute x28, starting transfers between devices, body(): lax.ppermute(held[at], 'row', ways[at % panels])  28.4 us
    ppermute x28, waiting for transfers between devices, body(): lax.ppermute(held[at], 'row', ways[at % panels])  28.4 us
    pallas_call x6, Pallas kernels, fold(): pl.pallas_call(functools.partial(fold_kernel, first, last, hops, order, r...  15.2 us
    unnamed x59, local copies, waits for them, and re-layouts  13 us
    all_gather x1, blocking collectives, body(): codes = lax.all_gather(int_codes, 'col', axis=1, tiled=True)  5.06 us
    ppermute x1, starting transfers between devices, body(): lax.ppermute(own, 'col', [(c, (c + shift * CORES) % n_col) for c in range...  2.97 us
  transfers between devices with their start and end apart: 31, of which 10 were waited for; matrix products, arithmetic and copies ran while one was open for 1% of the time, Pallas kernels for 15%

profile of v1, /device:TPU:0, one launch (start us, length us, event | category | flops | bytes accessed | tf_op | source)
XLA Modules:
  0.0 95.3 jit_solution(425077662354866178)
XLA Ops:
  0.0 3.0 %collective-permute-start.1 = (bf16[2,2,256,256]{3,2,1,0:T(8,128)(2,1)}, bf16[2,2,256,256]{3,2,1,0:T(8,128)(2,1)S(1)}, u32[]{:S(2)}, u32[]{:S(2)}) collective-permute-start(bf16[2,2,256,256]{3,2,1,0:T(8,128)(2,1)} %bitcast.1), channel_id=1, source_target_pairs={{0,2},{1,3},{2,0},{3,1},{4,6},{5,7},{6,4},{7,5},{8,10},{9,11},{10,... | collective-permute-start | bytes 1572872 | tf_op jit(solution)/shard_map/ppermute | solution.py:254
  4.9 1.6 %place.1 = (bf16[512,256]{1,0:T(8,128)(2,1)S(1)}, bf16[512,256]{1,0:T(8,128)(2,1)S(1)}, bf16[512,256]{1,0:T(8,128)(2,1)S(1)}, bf16[512,256]{1,0:T(8,128)(2,1)S(1)}) custom-call(s32[2,1,4]{2,1,0:T(1,128)S(1)} %copy-done.28, bf16[2,1,4,256,256]{4,3,2,1,0:T(8,128)(2,1)S(1)} %copy-done), custom_call_target="tpu_custom_call" | custom-call | tf_op jit(solution)/shard_map/place/pallas_call | solution.py:72
  6.5 1.8 %collective-permute-start.17 = (bf16[512,256]{1,0:T(8,128)(2,1)S(1)}, bf16[512,256]{1,0:T(8,128)(2,1)S(1)}, u32[]{:S(2)}, u32[]{:S(2)}) collective-permute-start(bf16[512,256]{1,0:T(8,128)(2,1)S(1)} %get-tuple-element.11.refs_0_), channel_id=1, source_target_pairs={{0,8},{8,16},{16,24},{24,28},{28,20},{20,12},{12,4},{4,0},{1,9},{9... | collective-permute-start | bytes 786440 | tf_op jit(solution)/shard_map/ppermute | solution.py:244
  8.5 1.7 %collective-permute-start.3 = (bf16[512,256]{1,0:T(8,128)(2,1)S(1)}, bf16[512,256]{1,0:T(8,128)(2,1)S(1)}, u32[]{:S(2)}, u32[]{:S(2)}) collective-permute-start(bf16[512,256]{1,0:T(8,128)(2,1)S(1)} %get-tuple-element.9.refs_0_), channel_id=1, source_target_pairs={{0,8},{8,16},{16,24},{24,28},{28,20},{20,12},{12,4},{4,0},{1,9},{9... | collective-permute-start | bytes 786440 | tf_op jit(solution)/shard_map/ppermute | solution.py:244
  10.6 5.2 %collective-permute-done.17.refs_2_ = bf16[512,256]{1,0:T(8,128)(2,1)S(1)} collective-permute-done((bf16[512,256]{1,0:T(8,128)(2,1)S(1)}, bf16[512,256]{1,0:T(8,128)(2,1)S(1)}, u32[]{:S(2)}, u32[]{:S(2)}) %collective-permute-start.17) | collective-permute-done | bytes 262176 | tf_op jit(solution)/shard_map/ppermute | solution.py:244
  15.8 1.7 %collective-permute-start.18 = (bf16[512,256]{1,0:T(8,128)(2,1)S(1)}, bf16[512,256]{1,0:T(8,128)(2,1)S(1)}, u32[]{:S(2)}, u32[]{:S(2)}) collective-permute-start(bf16[512,256]{1,0:T(8,128)(2,1)S(1)} %collective-permute-done.17.refs_2_), channel_id=1, source_target_pairs={{0,8},{8,16},{16,24},{24,28},{28,20},{20,12},{12,4},{4,0},{1,9},{9... | collective-permute-start | bytes 786440 | tf_op jit(solution)/shard_map/ppermute | solution.py:244
  18.5 2.9 %collective-permute-done.3.refs_2_ = bf16[512,256]{1,0:T(8,128)(2,1)S(1)} collective-permute-done((bf16[512,256]{1,0:T(8,128)(2,1)S(1)}, bf16[512,256]{1,0:T(8,128)(2,1)S(1)}, u32[]{:S(2)}, u32[]{:S(2)}) %collective-permute-start.3) | collective-permute-done | bytes 262176 | tf_op jit(solution)/shard_map/ppermute | solution.py:244
  21.4 1.7 %collective-permute-start.4 = (bf16[512,256]{1,0:T(8,128)(2,1)S(1)}, bf16[512,256]{1,0:T(8,128)(2,1)S(1)}, u32[]{:S(2)}, u32[]{:S(2)}) collective-permute-start(bf16[512,256]{1,0:T(8,128)(2,1)S(1)} %collective-permute-done.3.refs_2_), channel_id=1, source_target_pairs={{0,8},{8,16},{16,24},{24,28},{28,20},{20,12},{12,4},{4,0},{1,9},{9... | collective-permute-start | bytes 786440 | tf_op jit(solution)/shard_map/ppermute | solution.py:244
  23.4 3.6 %collective-permute-done.18.refs_4_ = bf16[512,256]{1,0:T(8,128)(2,1)S(1)} collective-permute-done((bf16[512,256]{1,0:T(8,128)(2,1)S(1)}, bf16[512,256]{1,0:T(8,128)(2,1)S(1)}, u32[]{:S(2)}, u32[]{:S(2)}) %collective-permute-start.18) | collective-permute-done | bytes 262176 | tf_op jit(solution)/shard_map/ppermute | solution.py:244
  27.0 1.7 %collective-permute-start.19 = (bf16[512,256]{1,0:T(8,128)(2,1)S(1)}, bf16[512,256]{1,0:T(8,128)(2,1)S(1)}, u32[]{:S(2)}, u32[]{:S(2)}) collective-permute-start(bf16[512,256]{1,0:T(8,128)(2,1)S(1)} %collective-permute-done.18.refs_4_), channel_id=1, source_target_pairs={{0,8},{8,16},{16,24},{24,28},{28,20},{20,12},{12,4},{4,0},{1,9},{9... | collective-permute-start | bytes 786440 | tf_op jit(solution)/shard_map/ppermute | solution.py:244
  30.4 2.2 %collective-permute-done.4.refs_4_ = bf16[512,256]{1,0:T(8,128)(2,1)S(1)} collective-permute-done((bf16[512,256]{1,0:T(8,128)(2,1)S(1)}, bf16[512,256]{1,0:T(8,128)(2,1)S(1)}, u32[]{:S(2)}, u32[]{:S(2)}) %collective-permute-start.4) | collective-permute-done | bytes 262176 | tf_op jit(solution)/shard_map/ppermute | solution.py:244
  32.6 1.7 %collective-permute-start.5 = (bf16[512,256]{1,0:T(8,128)(2,1)S(1)}, bf16[512,256]{1,0:T(8,128)(2,1)S(1)}, u32[]{:S(2)}, u32[]{:S(2)}) collective-permute-start(bf16[512,256]{1,0:T(8,128)(2,1)S(1)} %collective-permute-done.4.refs_4_), channel_id=1, source_target_pairs={{0,8},{8,16},{16,24},{24,28},{28,20},{20,12},{12,4},{4,0},{1,9},{9... | collective-permute-start | bytes 786440 | tf_op jit(solution)/shard_map/ppermute | solution.py:244
  36.1 2.2 %collective-permute-done.19.refs_6_ = bf16[512,256]{1,0:T(8,128)(2,1)S(1)} collective-permute-done((bf16[512,256]{1,0:T(8,128)(2,1)S(1)}, bf16[512,256]{1,0:T(8,128)(2,1)S(1)}, u32[]{:S(2)}, u32[]{:S(2)}) %collective-permute-start.19) | collective-permute-done | bytes 262176 | tf_op jit(solution)/shard_map/ppermute | solution.py:244
  38.2 1.7 %collective-permute-start.20 = (bf16[512,256]{1,0:T(8,128)(2,1)S(1)}, bf16[512,256]{1,0:T(8,128)(2,1)S(1)}, u32[]{:S(2)}, u32[]{:S(2)}) collective-permute-start(bf16[512,256]{1,0:T(8,128)(2,1)S(1)} %collective-permute-done.19.refs_6_), channel_id=1, source_target_pairs={{0,8},{8,16},{16,24},{24,28},{28,20},{20,12},{12,4},{4,0},{1,9},{9... | collective-permute-start | bytes 786440 | tf_op jit(solution)/shard_map/ppermute | solution.py:244
  41.7 2.2 %collective-permute-done.5.refs_6_ = bf16[512,256]{1,0:T(8,128)(2,1)S(1)} collective-permute-done((bf16[512,256]{1,0:T(8,128)(2,1)S(1)}, bf16[512,256]{1,0:T(8,128)(2,1)S(1)}, u32[]{:S(2)}, u32[]{:S(2)}) %collective-permute-start.5) | collective-permute-done | bytes 262176 | tf_op jit(solution)/shard_map/ppermute | solution.py:244
  43.8 1.7 %collective-permute-start.6 = (bf16[512,256]{1,0:T(8,128)(2,1)S(1)}, bf16[512,256]{1,0:T(8,128)(2,1)S(1)}, u32[]{:S(2)}, u32[]{:S(2)}) collective-permute-start(bf16[512,256]{1,0:T(8,128)(2,1)S(1)} %collective-permute-done.5.refs_6_), channel_id=1, source_target_pairs={{0,8},{8,16},{16,24},{24,28},{28,20},{20,12},{12,4},{4,0},{1,9},{9... | collective-permute-start | bytes 786440 | tf_op jit(solution)/shard_map/ppermute | solution.py:244
  47.3 2.1 %collective-permute-done.20.refs_0_ = bf16[512,256]{1,0:T(8,128)(2,1)S(1)} collective-permute-done((bf16[512,256]{1,0:T(8,128)(2,1)S(1)}, bf16[512,256]{1,0:T(8,128)(2,1)S(1)}, u32[]{:S(2)}, u32[]{:S(2)}) %collective-permute-start.20) | collective-permute-done | bytes 262176 | tf_op jit(solution)/shard_map/ppermute | solution.py:244
  49.5 1.7 %collective-permute-start.21 = (bf16[512,256]{1,0:T(8,128)(2,1)S(1)}, bf16[512,256]{1,0:T(8,128)(2,1)}, u32[]{:S(2)}, u32[]{:S(2)}) collective-permute-start(bf16[512,256]{1,0:T(8,128)(2,1)S(1)} %collective-permute-done.20.refs_0_), channel_id=1, source_target_pairs={{0,8},{8,16},{16,24},{24,28},{28,20},{20,12},{12,4},{4,0},{1,9},{9... | collective-permute-start | bytes 786440 | tf_op jit(solution)/shard_map/ppermute | solution.py:244
  52.9 2.1 %collective-permute-done.6.refs_0_ = bf16[512,256]{1,0:T(8,128)(2,1)S(1)} collective-permute-done((bf16[512,256]{1,0:T(8,128)(2,1)S(1)}, bf16[512,256]{1,0:T(8,128)(2,1)S(1)}, u32[]{:S(2)}, u32[]{:S(2)}) %collective-permute-start.6) | collective-permute-done | bytes 262176 | tf_op jit(solution)/shard_map/ppermute | solution.py:244
  55.1 1.7 %collective-permute-start.7 = (bf16[512,256]{1,0:T(8,128)(2,1)S(1)}, bf16[512,256]{1,0:T(8,128)(2,1)}, u32[]{:S(2)}, u32[]{:S(2)}) collective-permute-start(bf16[512,256]{1,0:T(8,128)(2,1)S(1)} %collective-permute-done.6.refs_0_), channel_id=1, source_target_pairs={{0,8},{8,16},{16,24},{24,28},{28,20},{20,12},{12,4},{4,0},{1,9},{9... | collective-permute-start | bytes 786440 | tf_op jit(solution)/shard_map/ppermute | solution.py:244
  58.5 2.3 %collective-permute-done.21.refs_2_ = bf16[512,256]{1,0:T(8,128)(2,1)} collective-permute-done((bf16[512,256]{1,0:T(8,128)(2,1)S(1)}, bf16[512,256]{1,0:T(8,128)(2,1)}, u32[]{:S(2)}, u32[]{:S(2)}) %collective-permute-start.21) | collective-permute-done | bytes 262176 | tf_op jit(solution)/shard_map/ppermute | solution.py:244
  60.8 1.7 %collective-permute-start.22 = (bf16[512,256]{1,0:T(8,128)(2,1)}, bf16[512,256]{1,0:T(8,128)(2,1)}, u32[]{:S(2)}, u32[]{:S(2)}) collective-permute-start(bf16[512,256]{1,0:T(8,128)(2,1)} %collective-permute-done.21.refs_2_), channel_id=1, source_target_pairs={{0,8},{8,16},{16,24},{24,28},{28,20},{20,12},{12,4},{4,0},{1,9},{9... | collective-permute-start | bytes 786440 | tf_op jit(solution)/shard_map/ppermute | solution.py:244
  62.8 3.6 %collective-permute-done.7.refs_2_ = bf16[512,256]{1,0:T(8,128)(2,1)} collective-permute-done((bf16[512,256]{1,0:T(8,128)(2,1)S(1)}, bf16[512,256]{1,0:T(8,128)(2,1)}, u32[]{:S(2)}, u32[]{:S(2)}) %collective-permute-start.7) | collective-permute-done | bytes 262176 | tf_op jit(solution)/shard_map/ppermute | solution.py:244
  66.4 1.7 %collective-permute-start.8 = (bf16[512,256]{1,0:T(8,128)(2,1)}, bf16[512,256]{1,0:T(8,128)(2,1)}, u32[]{:S(2)}, u32[]{:S(2)}) collective-permute-start(bf16[512,256]{1,0:T(8,128)(2,1)} %collective-permute-done.7.refs_2_), channel_id=1, source_target_pairs={{0,8},{8,16},{16,24},{24,28},{28,20},{20,12},{12,4},{4,0},{1,9},{9... | collective-permute-start | bytes 786440 | tf_op jit(solution)/shard_map/ppermute | solution.py:244
  69.2 5.1 %all_gather.3 = s32[2,8,1]{0,2,1:T(1,128)S(1)} all-gather(s32[2,2,1]{0,2,1:T(1,128)S(1)} %copy.9), channel_id=1, replica_groups=mesh['row'=8,'col'=4] {'col'}, dimensions={1}, use_global_device_ids=true | all-gather | bytes 80 | tf_op jit(solution)/shard_map/all_gather | solution.py:247
  75.8 1.8 %collective-permute-start.23 = (bf16[512,256]{1,0:T(8,128)(2,1)}, bf16[512,256]{1,0:T(8,128)(2,1)S(1)}, u32[]{:S(2)}, u32[]{:S(2)}) collective-permute-start(bf16[512,256]{1,0:T(8,128)(2,1)} %collective-permute-done.22.refs_4_), channel_id=1, source_target_pairs={{0,8},{8,16},{16,24},{24,28},{28,20},{20,12},{12,4},{4,0},{1,9},{9... | collective-permute-start | bytes 786440 | tf_op jit(solution)/shard_map/ppermute | solution.py:244
  77.9 2.5 %fold.8.refs_6_ = f32[512,1536]{1,0:T(8,128)S(1)} custom-call(s32[2,8,1]{2,1,0:T(8,128)S(1)} %copy.15.codes_ref, bf16[2,8,256,256]{3,2,1,0:T(8,128)(2,1)S(1)} %collect.1.ints_ref, bf16[512,256]{1,0:T(8,128)(2,1)S(1)} %get-tuple-element.11.refs_0_, bf16[512,256]{1,0:T(8,128)(2,1)S(1)} %get-tuple-element.12.refs_1_, ...), custom_call_target="tpu_custom_call" | custom-call | flops 1073741824 | bytes 3145728 | tf_op jit(solution)/shard_map/fold/pallas_call | solution.py:215
  82.6 2.5 %fold.6.refs_6_ = f32[512,1536]{1,0:T(8,128)S(1)} custom-call(s32[2,8,1]{2,1,0:T(8,128)S(1)} %copy.15.codes_ref, bf16[2,8,256,256]{3,2,1,0:T(8,128)(2,1)S(1)} %collect.1.ints_ref, bf16[512,256]{1,0:T(8,128)(2,1)S(1)} %get-tuple-element.9.refs_0_, bf16[512,256]{1,0:T(8,128)(2,1)S(1)} %get-tuple-element.10.refs_1_, ...), custom_call_target="tpu_custom_call" | custom-call | flops 1073741824 | bytes 3145728 | tf_op jit(solution)/shard_map/fold/pallas_call | solution.py:215
  85.2 2.6 %fold.9.refs_2_ = f32[512,1536]{1,0:T(8,128)S(1)} custom-call(s32[2,8,1]{2,1,0:T(8,128)S(1)} %copy.15.codes_ref, bf16[2,8,256,256]{3,2,1,0:T(8,128)(2,1)S(1)} %collect.1.ints_ref, bf16[512,256]{1,0:T(8,128)(2,1)S(1)} %copy-done.19, bf16[512,256]{1,0:T(8,128)(2,1)S(1)} %copy-done.23, ...), custom_call_target="tpu_custom_call", output_to_operand_aliasing={{}: (8, {})} | custom-call | flops 805306368 | bytes 3145728 | tf_op jit(solution)/shard_map/fold/pallas_call | solution.py:215
  87.8 2.5 %fold.7.refs_2_ = f32[512,1536]{1,0:T(8,128)S(1)} custom-call(s32[2,8,1]{2,1,0:T(8,128)S(1)} %copy.15.codes_ref, bf16[2,8,256,256]{3,2,1,0:T(8,128)(2,1)S(1)} %collect.1.ints_ref, bf16[512,256]{1,0:T(8,128)(2,1)S(1)} %copy-done.25, bf16[512,256]{1,0:T(8,128)(2,1)S(1)} %copy-done.27, ...), custom_call_target="tpu_custom_call", output_to_operand_aliasing={{}: (8, {})} | custom-call | flops 805306368 | bytes 3145728 | tf_op jit(solution)/shard_map/fold/pallas_call | solution.py:215
  90.4 2.5 %fold.10.refs_3_ = f32[1024,1536]{1,0:T(8,128)} custom-call(s32[2,8,1]{2,1,0:T(8,128)S(1)} %copy.15.codes_ref, bf16[2,8,256,256]{3,2,1,0:T(8,128)(2,1)S(1)} %collect.1.ints_ref, bf16[512,256]{1,0:T(8,128)(2,1)S(1)} %collective-permute-done.23.refs_0_, bf16[512,256]{1,0:T(8,128)(2,1)S(1)} %collective-permute-done.30.refs_1_, f32[512,1536]{1,0:T(8,128)S(1)} %fold.9.refs_2_), custom_call_target="tpu_custom_call" | custom-call | flops 268435456 | bytes 3145728 | tf_op jit(solution)/shard_map/fold/pallas_call | solution.py:215
  92.9 2.5 %fold.11 = f32[1024,1536]{1,0:T(8,128)} custom-call(s32[2,8,1]{2,1,0:T(8,128)S(1)} %copy.15.codes_ref, bf16[2,8,256,256]{3,2,1,0:T(8,128)(2,1)S(1)} %collect.1.ints_ref, bf16[512,256]{1,0:T(8,128)(2,1)S(1)} %collective-permute-done.9.refs_0_, bf16[512,256]{1,0:T(8,128)(2,1)S(1)} %collective-permute-done.16.refs_1_, ...), custom_call_target="tpu_custom_call", output_to_operand_aliasing={{}: (5, {})} | custom-call | flops 268435456 | bytes 3145728 | tf_op jit(solution)/shard_map/fold/pallas_call | solution.py:215
  (99 shorter events, 19.5 us)
Async XLA Ops:
  0.0 23.4 %collective-permute-start.1 = (bf16[2,2,256,256]{3,2,1,0:T(8,128)(2,1)}, bf16[2,2,256,256]{3,2,1,0:T(8,128)(2,1)S(1)}, u32[]{:S(2)}, u32[]{:S(2)}) collective-permute-start(bf16[2,2,256,256]{3,2,1,0:T(8,128)(2,1)} %bitcast.1), channel_id=1, source_target_pairs={{0,2},{1,3},{2,0},{3,1},{4,6},{5,7},{6,4},{7,5},{8,10},{9,11},{10,... | collective-permute-start | bytes 1572872 | tf_op jit(solution)/shard_map/ppermute | solution.py:254
  6.5 9.3 %collective-permute-start.17 = (bf16[512,256]{1,0:T(8,128)(2,1)S(1)}, bf16[512,256]{1,0:T(8,128)(2,1)S(1)}, u32[]{:S(2)}, u32[]{:S(2)}) collective-permute-start(bf16[512,256]{1,0:T(8,128)(2,1)S(1)} %get-tuple-element.11.refs_0_), channel_id=1, source_target_pairs={{0,8},{8,16},{16,24},{24,28},{28,20},{20,12},{12,4},{4,0},{1,9},{9... | collective-permute-start | bytes 786440 | tf_op jit(solution)/shard_map/ppermute | solution.py:244
  8.3 9.2 %collective-permute-start.24 = (bf16[512,256]{1,0:T(8,128)(2,1)S(1)}, bf16[512,256]{1,0:T(8,128)(2,1)S(1)}, u32[]{:S(2)}, u32[]{:S(2)}) collective-permute-start(bf16[512,256]{1,0:T(8,128)(2,1)S(1)} %get-tuple-element.12.refs_1_), channel_id=1, source_target_pairs={{8,0},{16,8},{24,16},{28,24},{20,28},{12,20},{4,12},{0,4},{9,1},{1... | collective-permute-start | bytes 786440 | tf_op jit(solution)/shard_map/ppermute | solution.py:244
  8.5 12.8 %collective-permute-start.3 = (bf16[512,256]{1,0:T(8,128)(2,1)S(1)}, bf16[512,256]{1,0:T(8,128)(2,1)S(1)}, u32[]{:S(2)}, u32[]{:S(2)}) collective-permute-start(bf16[512,256]{1,0:T(8,128)(2,1)S(1)} %get-tuple-element.9.refs_0_), channel_id=1, source_target_pairs={{0,8},{8,16},{16,24},{24,28},{28,20},{20,12},{12,4},{4,0},{1,9},{9... | collective-permute-start | bytes 786440 | tf_op jit(solution)/shard_map/ppermute | solution.py:244
  10.3 12.8 %collective-permute-start.10 = (bf16[512,256]{1,0:T(8,128)(2,1)S(1)}, bf16[512,256]{1,0:T(8,128)(2,1)S(1)}, u32[]{:S(2)}, u32[]{:S(2)}) collective-permute-start(bf16[512,256]{1,0:T(8,128)(2,1)S(1)} %get-tuple-element.10.refs_1_), channel_id=1, source_target_pairs={{8,0},{16,8},{24,16},{28,24},{20,28},{12,20},{4,12},{0,4},{9,1},{1... | collective-permute-start | bytes 786440 | tf_op jit(solution)/shard_map/ppermute | solution.py:244
  15.8 11.2 %collective-permute-start.18 = (bf16[512,256]{1,0:T(8,128)(2,1)S(1)}, bf16[512,256]{1,0:T(8,128)(2,1)S(1)}, u32[]{:S(2)}, u32[]{:S(2)}) collective-permute-start(bf16[512,256]{1,0:T(8,128)(2,1)S(1)} %collective-permute-done.17.refs_2_), channel_id=1, source_target_pairs={{0,8},{8,16},{16,24},{24,28},{28,20},{20,12},{12,4},{4,0},{1,9},{9... | collective-permute-start | bytes 786440 | tf_op jit(solution)/shard_map/ppermute | solution.py:244
  17.5 11.9 %collective-permute-start.25 = (bf16[512,256]{1,0:T(8,128)(2,1)S(1)}, bf16[512,256]{1,0:T(8,128)(2,1)S(1)}, u32[]{:S(2)}, u32[]{:S(2)}) collective-permute-start(bf16[512,256]{1,0:T(8,128)(2,1)S(1)} %collective-permute-done.24.refs_3_), channel_id=1, source_target_pairs={{8,0},{16,8},{24,16},{28,24},{20,28},{12,20},{4,12},{0,4},{9,1},{1... | collective-permute-start | bytes 786440 | tf_op jit(solution)/shard_map/ppermute | solution.py:244
  21.4 11.2 %collective-permute-start.4 = (bf16[512,256]{1,0:T(8,128)(2,1)S(1)}, bf16[512,256]{1,0:T(8,128)(2,1)S(1)}, u32[]{:S(2)}, u32[]{:S(2)}) collective-permute-start(bf16[512,256]{1,0:T(8,128)(2,1)S(1)} %collective-permute-done.3.refs_2_), channel_id=1, source_target_pairs={{0,8},{8,16},{16,24},{24,28},{28,20},{20,12},{12,4},{4,0},{1,9},{9... | collective-permute-start | bytes 786440 | tf_op jit(solution)/shard_map/ppermute | solution.py:244
  23.1 11.9 %collective-permute-start.11 = (bf16[512,256]{1,0:T(8,128)(2,1)S(1)}, bf16[512,256]{1,0:T(8,128)(2,1)S(1)}, u32[]{:S(2)}, u32[]{:S(2)}) collective-permute-start(bf16[512,256]{1,0:T(8,128)(2,1)S(1)} %collective-permute-done.10.refs_3_), channel_id=1, source_target_pairs={{8,0},{16,8},{24,16},{28,24},{20,28},{12,20},{4,12},{0,4},{9,1},{1... | collective-permute-start | bytes 786440 | tf_op jit(solution)/shard_map/ppermute | solution.py:244
  23.4 23.9 %collective-permute-start = (bf16[2,2,256,256]{3,2,1,0:T(8,128)(2,1)}, bf16[2,2,256,256]{3,2,1,0:T(8,128)(2,1)S(1)}, u32[]{:S(2)}, u32[]{:S(2)}) collective-permute-start(bf16[2,2,256,256]{3,2,1,0:T(8,128)(2,1)} %bitcast.2), channel_id=1, source_target_pairs={{0,1},{1,0},{2,3},{3,2},{4,5},{5,4},{6,7},{7,6},{8,9},{9,8},{10,11... | collective-permute-start | bytes 1572872 | tf_op jit(solution)/shard_map/ppermute | solution.py:255
  27.0 11.2 %collective-permute-start.19 = (bf16[512,256]{1,0:T(8,128)(2,1)S(1)}, bf16[512,256]{1,0:T(8,128)(2,1)S(1)}, u32[]{:S(2)}, u32[]{:S(2)}) collective-permute-start(bf16[512,256]{1,0:T(8,128)(2,1)S(1)} %collective-permute-done.18.refs_4_), channel_id=1, source_target_pairs={{0,8},{8,16},{16,24},{24,28},{28,20},{20,12},{12,4},{4,0},{1,9},{9... | collective-permute-start | bytes 786440 | tf_op jit(solution)/shard_map/ppermute | solution.py:244
  29.4 11.3 %collective-permute-start.26 = (bf16[512,256]{1,0:T(8,128)(2,1)S(1)}, bf16[512,256]{1,0:T(8,128)(2,1)S(1)}, u32[]{:S(2)}, u32[]{:S(2)}) collective-permute-start(bf16[512,256]{1,0:T(8,128)(2,1)S(1)} %collective-permute-done.25.refs_5_), channel_id=1, source_target_pairs={{8,0},{16,8},{24,16},{28,24},{20,28},{12,20},{4,12},{0,4},{9,1},{1... | collective-permute-start | bytes 786440 | tf_op jit(solution)/shard_map/ppermute | solution.py:244
  32.6 11.2 %collective-permute-start.5 = (bf16[512,256]{1,0:T(8,128)(2,1)S(1)}, bf16[512,256]{1,0:T(8,128)(2,1)S(1)}, u32[]{:S(2)}, u32[]{:S(2)}) collective-permute-start(bf16[512,256]{1,0:T(8,128)(2,1)S(1)} %collective-permute-done.4.refs_4_), channel_id=1, source_target_pairs={{0,8},{8,16},{16,24},{24,28},{28,20},{20,12},{12,4},{4,0},{1,9},{9... | collective-permute-start | bytes 786440 | tf_op jit(solution)/shard_map/ppermute | solution.py:244
  35.0 11.3 %collective-permute-start.12 = (bf16[512,256]{1,0:T(8,128)(2,1)S(1)}, bf16[512,256]{1,0:T(8,128)(2,1)S(1)}, u32[]{:S(2)}, u32[]{:S(2)}) collective-permute-start(bf16[512,256]{1,0:T(8,128)(2,1)S(1)} %collective-permute-done.11.refs_5_), channel_id=1, source_target_pairs={{8,0},{16,8},{24,16},{28,24},{20,28},{12,20},{4,12},{0,4},{9,1},{1... | collective-permute-start | bytes 786440 | tf_op jit(solution)/shard_map/ppermute | solution.py:244
  38.2 11.2 %collective-permute-start.20 = (bf16[512,256]{1,0:T(8,128)(2,1)S(1)}, bf16[512,256]{1,0:T(8,128)(2,1)S(1)}, u32[]{:S(2)}, u32[]{:S(2)}) collective-permute-start(bf16[512,256]{1,0:T(8,128)(2,1)S(1)} %collective-permute-done.19.refs_6_), channel_id=1, source_target_pairs={{0,8},{8,16},{16,24},{24,28},{28,20},{20,12},{12,4},{4,0},{1,9},{9... | collective-permute-start | bytes 786440 | tf_op jit(solution)/shard_map/ppermute | solution.py:244
  40.7 11.2 %collective-permute-start.27 = (bf16[512,256]{1,0:T(8,128)(2,1)S(1)}, bf16[512,256]{1,0:T(8,128)(2,1)S(1)}, u32[]{:S(2)}, u32[]{:S(2)}) collective-permute-start(bf16[512,256]{1,0:T(8,128)(2,1)S(1)} %collective-permute-done.26.refs_7_), channel_id=1, source_target_pairs={{8,0},{16,8},{24,16},{28,24},{20,28},{12,20},{4,12},{0,4},{9,1},{1... | collective-permute-start | bytes 786440 | tf_op jit(solution)/shard_map/ppermute | solution.py:244
  43.8 11.2 %collective-permute-start.6 = (bf16[512,256]{1,0:T(8,128)(2,1)S(1)}, bf16[512,256]{1,0:T(8,128)(2,1)S(1)}, u32[]{:S(2)}, u32[]{:S(2)}) collective-permute-start(bf16[512,256]{1,0:T(8,128)(2,1)S(1)} %collective-permute-done.5.refs_6_), channel_id=1, source_target_pairs={{0,8},{8,16},{16,24},{24,28},{28,20},{20,12},{12,4},{4,0},{1,9},{9... | collective-permute-start | bytes 786440 | tf_op jit(solution)/shard_map/ppermute | solution.py:244
  46.3 11.2 %collective-permute-start.13 = (bf16[512,256]{1,0:T(8,128)(2,1)S(1)}, bf16[512,256]{1,0:T(8,128)(2,1)S(1)}, u32[]{:S(2)}, u32[]{:S(2)}) collective-permute-start(bf16[512,256]{1,0:T(8,128)(2,1)S(1)} %collective-permute-done.12.refs_7_), channel_id=1, source_target_pairs={{8,0},{16,8},{24,16},{28,24},{20,28},{12,20},{4,12},{0,4},{9,1},{1... | collective-permute-start | bytes 786440 | tf_op jit(solution)/shard_map/ppermute | solution.py:244
  47.3 27.1 %collective-permute-start.2 = (bf16[2,2,256,256]{3,2,1,0:T(8,128)(2,1)S(1)}, bf16[2,2,256,256]{3,2,1,0:T(8,128)(2,1)S(1)}, u32[]{:S(2)}, u32[]{:S(2)}) collective-permute-start(bf16[2,2,256,256]{3,2,1,0:T(8,128)(2,1)S(1)} %collective-permute-done.1.refs_2_), channel_id=1, source_target_pairs={{0,1},{1,0},{2,3},{3,2},{4,5},{5,4},{6,7},{7,6},{8,9},{9,8},{10,11... | collective-permute-start | bytes 1572872 | tf_op jit(solution)/shard_map/ppermute | solution.py:255
  49.5 11.3 %collective-permute-start.21 = (bf16[512,256]{1,0:T(8,128)(2,1)S(1)}, bf16[512,256]{1,0:T(8,128)(2,1)}, u32[]{:S(2)}, u32[]{:S(2)}) collective-permute-start(bf16[512,256]{1,0:T(8,128)(2,1)S(1)} %collective-permute-done.20.refs_0_), channel_id=1, source_target_pairs={{0,8},{8,16},{16,24},{24,28},{28,20},{20,12},{12,4},{4,0},{1,9},{9... | collective-permute-start | bytes 786440 | tf_op jit(solution)/shard_map/ppermute | solution.py:244
  51.9 10.6 %collective-permute-start.28 = (bf16[512,256]{1,0:T(8,128)(2,1)S(1)}, bf16[512,256]{1,0:T(8,128)(2,1)}, u32[]{:S(2)}, u32[]{:S(2)}) collective-permute-start(bf16[512,256]{1,0:T(8,128)(2,1)S(1)} %collective-permute-done.27.refs_1_), channel_id=1, source_target_pairs={{8,0},{16,8},{24,16},{28,24},{20,28},{12,20},{4,12},{0,4},{9,1},{1... | collective-permute-start | bytes 786440 | tf_op jit(solution)/shard_map/ppermute | solution.py:244
  55.1 11.3 %collective-permute-start.7 = (bf16[512,256]{1,0:T(8,128)(2,1)S(1)}, bf16[512,256]{1,0:T(8,128)(2,1)}, u32[]{:S(2)}, u32[]{:S(2)}) collective-permute-start(bf16[512,256]{1,0:T(8,128)(2,1)S(1)} %collective-permute-done.6.refs_0_), channel_id=1, source_target_pairs={{0,8},{8,16},{16,24},{24,28},{28,20},{20,12},{12,4},{4,0},{1,9},{9... | collective-permute-start | bytes 786440 | tf_op jit(solution)/shard_map/ppermute | solution.py:244
  57.5 10.7 %collective-permute-start.14 = (bf16[512,256]{1,0:T(8,128)(2,1)S(1)}, bf16[512,256]{1,0:T(8,128)(2,1)}, u32[]{:S(2)}, u32[]{:S(2)}) collective-permute-start(bf16[512,256]{1,0:T(8,128)(2,1)S(1)} %collective-permute-done.13.refs_1_), channel_id=1, source_target_pairs={{8,0},{16,8},{24,16},{28,24},{20,28},{12,20},{4,12},{0,4},{9,1},{1... | collective-permute-start | bytes 786440 | tf_op jit(solution)/shard_map/ppermute | solution.py:244
  60.8 15.0 %collective-permute-start.22 = (bf16[512,256]{1,0:T(8,128)(2,1)}, bf16[512,256]{1,0:T(8,128)(2,1)}, u32[]{:S(2)}, u32[]{:S(2)}) collective-permute-start(bf16[512,256]{1,0:T(8,128)(2,1)} %collective-permute-done.21.refs_2_), channel_id=1, source_target_pairs={{0,8},{8,16},{16,24},{24,28},{28,20},{20,12},{12,4},{4,0},{1,9},{9... | collective-permute-start | bytes 786440 | tf_op jit(solution)/shard_map/ppermute | solution.py:244
  62.5 15.0 %collective-permute-start.29 = (bf16[512,256]{1,0:T(8,128)(2,1)}, bf16[512,256]{1,0:T(8,128)(2,1)}, u32[]{:S(2)}, u32[]{:S(2)}) collective-permute-start(bf16[512,256]{1,0:T(8,128)(2,1)} %collective-permute-done.28.refs_3_), channel_id=1, source_target_pairs={{8,0},{16,8},{24,16},{28,24},{20,28},{12,20},{4,12},{0,4},{9,1},{1... | collective-permute-start | bytes 786440 | tf_op jit(solution)/shard_map/ppermute | solution.py:244
  66.4 14.1 %collective-permute-start.8 = (bf16[512,256]{1,0:T(8,128)(2,1)}, bf16[512,256]{1,0:T(8,128)(2,1)}, u32[]{:S(2)}, u32[]{:S(2)}) collective-permute-start(bf16[512,256]{1,0:T(8,128)(2,1)} %collective-permute-done.7.refs_2_), channel_id=1, source_target_pairs={{0,8},{8,16},{16,24},{24,28},{28,20},{20,12},{12,4},{4,0},{1,9},{9... | collective-permute-start | bytes 786440 | tf_op jit(solution)/shard_map/ppermute | solution.py:244
  68.2 13.6 %collective-permute-start.15 = (bf16[512,256]{1,0:T(8,128)(2,1)}, bf16[512,256]{1,0:T(8,128)(2,1)}, u32[]{:S(2)}, u32[]{:S(2)}) collective-permute-start(bf16[512,256]{1,0:T(8,128)(2,1)} %collective-permute-done.14.refs_3_), channel_id=1, source_target_pairs={{8,0},{16,8},{24,16},{28,24},{20,28},{12,20},{4,12},{0,4},{9,1},{1... | collective-permute-start | bytes 786440 | tf_op jit(solution)/shard_map/ppermute | solution.py:244
  75.7 6.8 %copy-start.5 = (bf16[512,256]{1,0:T(8,128)(2,1)S(1)}, bf16[512,256]{1,0:T(8,128)(2,1)}, u32[]{:S(2)}) copy-start(bf16[512,256]{1,0:T(8,128)(2,1)} %copy-done.4) | copy-start | bytes 786436
  75.8 14.5 %collective-permute-start.23 = (bf16[512,256]{1,0:T(8,128)(2,1)}, bf16[512,256]{1,0:T(8,128)(2,1)S(1)}, u32[]{:S(2)}, u32[]{:S(2)}) collective-permute-start(bf16[512,256]{1,0:T(8,128)(2,1)} %collective-permute-done.22.refs_4_), channel_id=1, source_target_pairs={{0,8},{8,16},{16,24},{24,28},{28,20},{20,12},{12,4},{4,0},{1,9},{9... | collective-permute-start | bytes 786440 | tf_op jit(solution)/shard_map/ppermute | solution.py:244
  77.6 12.8 %collective-permute-start.30 = (bf16[512,256]{1,0:T(8,128)(2,1)}, bf16[512,256]{1,0:T(8,128)(2,1)S(1)}, u32[]{:S(2)}, u32[]{:S(2)}) collective-permute-start(bf16[512,256]{1,0:T(8,128)(2,1)} %collective-permute-done.29.refs_5_), channel_id=1, source_target_pairs={{8,0},{16,8},{24,16},{28,24},{20,28},{12,20},{4,12},{0,4},{9,1},{1... | collective-permute-start | bytes 786440 | tf_op jit(solution)/shard_map/ppermute | solution.py:244
  80.5 12.4 %collective-permute-start.9 = (bf16[512,256]{1,0:T(8,128)(2,1)}, bf16[512,256]{1,0:T(8,128)(2,1)S(1)}, u32[]{:S(2)}, u32[]{:S(2)}) collective-permute-start(bf16[512,256]{1,0:T(8,128)(2,1)} %collective-permute-done.8.refs_4_), channel_id=1, source_target_pairs={{0,8},{8,16},{16,24},{24,28},{28,20},{20,12},{12,4},{4,0},{1,9},{9... | collective-permute-start | bytes 786440 | tf_op jit(solution)/shard_map/ppermute | solution.py:244
  81.8 11.0 %collective-permute-start.16 = (bf16[512,256]{1,0:T(8,128)(2,1)}, bf16[512,256]{1,0:T(8,128)(2,1)S(1)}, u32[]{:S(2)}, u32[]{:S(2)}) collective-permute-start(bf16[512,256]{1,0:T(8,128)(2,1)} %collective-permute-done.15.refs_5_), channel_id=1, source_target_pairs={{8,0},{16,8},{24,16},{28,24},{20,28},{12,20},{4,12},{0,4},{9,1},{1... | collective-permute-start | bytes 786440 | tf_op jit(solution)/shard_map/ppermute | solution.py:244
  (28 other events, 59.3 us)

commit v2 on v1

v2 whole, which is shorter than its diff:
```python
import functools

import jax
import jax.numpy as jnp
from jax import lax
from jax.experimental import pallas as pl
from jax.experimental.pallas import tpu as pltpu
from jax.sharding import PartitionSpec as P

MI = 4
NJ = 6
CORES = 2
GROUPS = ((0, 2), (2, 4))
LINES = 16
VMEM_LIMIT = 8 * 1024 * 1024


def grid_cycle(depth, across):
    order = [z * across for z in range(depth)]
    for turn, z in enumerate(reversed(range(depth))):
        xs = range(1, across) if turn % 2 == 0 else range(across - 1, 0, -1)
        order += [z * across + x for x in xs]
    return order


def pick(table, index):
    value = jnp.int32(table[0])
    for at in range(1, len(table)):
        value = jnp.where(index == at, jnp.int32(table[at]), value)
    return value


def in_vmem(value):
    return pltpu.with_memory_space_constraint(value, pltpu.VMEM)


def in_hbm(value):
    return pltpu.with_memory_space_constraint(value, pltpu.HBM)


def place_kernel(rows_hbm, codes_hbm, tiles_hbm, ints_hbm, *rest):
    placed, parcel_ref = rest[: -1 - 6], rest[-1 - 6]
    rows_ref, codes_ref, tiles_ref, small_sem, tiles_sem, ints_sem = rest[-6:]
    panels, slots, width = tiles_ref.shape[0], tiles_ref.shape[1], tiles_ref.shape[2]
    held = ints_hbm.shape[1]
    small = [
        pltpu.make_async_copy(rows_hbm, rows_ref, small_sem.at[0]),
        pltpu.make_async_copy(codes_hbm, codes_ref, small_sem.at[1]),
    ]
    tiles = [
        pltpu.make_async_copy(tiles_hbm.at[panel, 0], tiles_ref.at[panel], tiles_sem.at[panel])
        for panel in range(panels)
    ]
    parcels = [
        pltpu.make_async_copy(
            ints_hbm.at[panel, at, 0],
            parcel_ref.at[pl.ds((panel * held + at) * width, width)],
            ints_sem.at[panel, at],
        )
        for panel in range(panels)
        for at in range(held)
    ]
    for copy in small + tiles + parcels:
        copy.start()
    for copy in small:
        copy.wait()
    lines = lax.broadcasted_iota(jnp.int32, (LINES, width), 0)
    labels = jnp.zeros((LINES, width), jnp.float32)
    for panel in range(panels):
        for at in range(held):
            code = codes_ref[panel, 0, at].astype(jnp.float32)
            labels = jnp.where(lines == panel * held + at, code, labels)
    parcel_ref[pl.ds(panels * held * width, LINES)] = labels.astype(parcel_ref.dtype)
    for panel in range(panels):
        tiles[panel].wait()
        for group, (first, last) in enumerate(GROUPS):
            for row in range(first, last):
                slot = jnp.int32(-1)
                for at in range(slots):
                    slot = jnp.where(rows_ref[panel, 0, at] == row, at, slot)
                spot = placed[group * panels + panel].at[pl.ds((row - first) * width, width)]

                @pl.when(slot >= 0)
                def _():
                    spot[...] = tiles_ref[panel, jnp.maximum(slot, 0)]

                @pl.when(slot < 0)
                def _():
                    spot[...] = jnp.zeros(spot.shape, spot.dtype)

    for copy in parcels:
        copy.wait()


def place(amp_tiles, amp_rows, int_tiles, int_codes):
    panels, held, slots, width = amp_tiles.shape[0], int_tiles.shape[1], amp_tiles.shape[2], amp_tiles.shape[3]
    codes = jnp.transpose(int_codes, (0, 2, 1))
    shapes = [
        pltpu.VMEM(((last - first) * width, width), amp_tiles.dtype)
        for first, last in GROUPS
        for _ in range(panels)
    ]
    shapes.append(pltpu.VMEM((panels * held * width + LINES, width), int_tiles.dtype))
    return pl.pallas_call(
        place_kernel,
        out_shape=shapes,
        in_specs=[pl.BlockSpec(memory_space=pl.ANY)] * 4,
        out_specs=[pl.BlockSpec(memory_space=pltpu.VMEM)] * len(shapes),
        scratch_shapes=[
            pltpu.SMEM(amp_rows.shape, jnp.int32),
            pltpu.SMEM(codes.shape, jnp.int32),
            pltpu.VMEM((panels, slots, width, width), amp_tiles.dtype),
            pltpu.SemaphoreType.DMA((2,)),
            pltpu.SemaphoreType.DMA((panels,)),
            pltpu.SemaphoreType.DMA((panels, held)),
        ],
        compiler_params=pltpu.CompilerParams(vmem_limit_bytes=VMEM_LIMIT),
        name="place",
    )(in_hbm(amp_rows), in_hbm(codes), in_hbm(amp_tiles), in_hbm(int_tiles))


def collect_kernel(panels, slots, base, *refs):
    parts, codes_ref, out_ref = refs[:-2], refs[-2], refs[-1]
    width = parts[0].shape[1]
    col = lax.axis_index("col")
    y, core = col // CORES, lax.rem(col, CORES)
    depth = len(parts) // CORES
    owners = []
    for at, part in enumerate(parts):
        shift, flip = at // CORES, at % CORES
        owner = lax.rem(y + depth - shift, depth) * CORES + lax.rem(core + flip, CORES)
        owners.append(owner)
        for panel in range(panels):
            for slot in range(slots):
                out_ref[panel, owner * slots + slot] = part[pl.ds((panel * slots + slot) * width, width)]
    lines = lax.broadcasted_iota(jnp.int32, (LINES, width), 0)
    scale = jnp.zeros((LINES, width), jnp.float32)
    for at in range(panels * slots):
        scale = jnp.where(lines == at, float(base**at), scale)
    for owner, part in zip(owners, parts):
        labels = part[pl.ds(panels * slots * width, LINES), pl.ds(0, 128)].astype(jnp.float32) + 1.0
        number = jnp.sum(labels * scale[:, :128], axis=0, keepdims=True)
        digits = jnp.max(number).astype(jnp.int32)
        for panel in range(panels):
            for slot in range(slots):
                codes_ref[panel, owner * slots + slot] = lax.rem(digits, base) - 1
                digits = digits // base


def collect(parts, panels, slots, base):
    width = parts[0].shape[1]
    total = slots * len(parts)
    assert base ** (panels * slots) < 2**24
    vmem = pl.BlockSpec(memory_space=pltpu.VMEM)
    return pl.pallas_call(
        functools.partial(collect_kernel, panels, slots, base),
        out_shape=[
            jax.ShapeDtypeStruct((panels, total), jnp.int32),
            pltpu.VMEM((panels, total, width, width), parts[0].dtype),
        ],
        in_specs=[vmem] * len(parts),
        out_specs=[pl.BlockSpec(memory_space=pltpu.SMEM), vmem],
        compiler_params=pltpu.CompilerParams(vmem_limit_bytes=VMEM_LIMIT),
        name="collect",
    )(*map(in_vmem, parts))


def chunk_updates(codes_ref, hops, order, rows_held, slots):
    me = lax.axis_index("row")
    inverse = [order.index(at) for at in range(len(order))]
    here = pick(inverse, me)
    found = []
    for panel, hop in hops:
        way = hop if panel % 2 == 0 else len(order) - hop
        source = pick(order, lax.rem(here + len(order) - way, len(order)))
        owner, held = source // rows_held, lax.rem(source, rows_held)
        for at in range(slots):
            slot = owner * slots + at
            code = codes_ref[panel, slot]
            live = (code >= 0) & (code // NJ == held)
            found.append((live, slot, lax.rem(jnp.maximum(code, 0), NJ)))
    return found


def columns_of(found):
    hits = []
    for column in range(NJ):
        hit = jnp.bool_(False)
        for live, _, at in found:
            hit = hit | (live & (at == column))
        hits.append(hit)
    return hits


def fold_kernel(first, hops, later, order, rows_held, slots, band, codes_ref, ints_ref, *refs):
    chunks, rest = refs[: len(hops)], refs[len(hops) :]
    width = ints_ref.shape[2]
    found = chunk_updates(codes_ref, hops, order, rows_held, slots)
    if later is None:
        total_ref = rest[-1]
    elif later:
        total_ref, out_ref, sem = rest[-3], rest[-2], rest[-1]
        ready = [jnp.logical_not(hit) for hit in columns_of(chunk_updates(codes_ref, later, order, rows_held, slots))]
    else:
        total_ref, out_ref, sem = rest[0], rest[-2], rest[-1]
    def send(column):
        cols = pl.ds(pl.multiple_of(column * width, width), width)
        return pltpu.make_async_copy(
            total_ref.at[:, cols], out_ref.at[pl.ds(band[0], band[1]), cols], sem.at[column]
        )

    if first:
        total_ref[...] = jnp.zeros(total_ref.shape, jnp.float32)
    if later:
        hits = columns_of(found)
        for column in range(NJ):

            @pl.when(ready[column] & jnp.logical_not(hits[column]))
            def _():
                send(column).start()

    final = []
    for index, (live, slot, column) in enumerate(found):
        panel, chunk = hops[index // slots][0], chunks[index // slots]
        again = jnp.bool_(False)
        for other, _, at in found[index + 1 :]:
            again = again | (other & (at == column))
        final.append(live & jnp.logical_not(again))

        @pl.when(live)
        def _():
            cols = pl.ds(pl.multiple_of(column * width, width), width)
            total_ref[:, cols] += jnp.dot(
                chunk[...], ints_ref[panel, slot], preferred_element_type=jnp.float32
            )

        if later is not None and not later:

            @pl.when(final[-1])
            def _():
                send(column).start()

    if later:
        for column in range(NJ):

            @pl.when(ready[column] & hits[column])
            def _():
                send(column).start()

        for column in range(NJ):

            @pl.when(ready[column])
            def _():
                send(column).wait()

    elif later is not None:
        for done, (_, _, column) in zip(final, found):

            @pl.when(done)
            def _():
                send(column).wait()


def fold(codes, ints, chunks, hops, later, total, out, order, rows_held, slots, band, whole):
    first = total is None
    rows, width = chunks[0].shape
    vmem = pl.BlockSpec(memory_space=pltpu.VMEM)
    anywhere = pl.BlockSpec(memory_space=pl.ANY)
    operands = [codes, in_vmem(ints), *map(in_vmem, chunks)]
    in_specs = [pl.BlockSpec(memory_space=pltpu.SMEM)] + [vmem] * (1 + len(chunks))
    aliases, scratch, out_shapes, out_specs = {}, [], [], []
    if not first:
        operands.append(in_vmem(total))
        in_specs.append(vmem)
    if later is None or later:
        if not first:
            aliases[len(operands) - 1] = 0
        out_shapes.append(pltpu.VMEM((rows, NJ * width), jnp.float32))
        out_specs.append(vmem)
    if later is not None:
        if out is not None:
            aliases[len(operands)] = len(out_shapes)
            operands.append(out)
            in_specs.append(anywhere)
        out_shapes.append(jax.ShapeDtypeStruct(whole, jnp.float32))
        out_specs.append(anywhere)
        scratch = [pltpu.SemaphoreType.DMA((NJ,))]
    return pl.pallas_call(
        functools.partial(fold_kernel, first, hops, later, order, rows_held, slots, band),
        out_shape=out_shapes,
        in_specs=in_specs,
        out_specs=out_specs,
        scratch_shapes=scratch,
        input_output_aliases=aliases,
        compiler_params=pltpu.CompilerParams(vmem_limit_bytes=VMEM_LIMIT),
        cost_estimate=pl.CostEstimate(
            flops=2 * rows * width * width * len(hops) * slots,
            bytes_accessed=rows * NJ * width * 4,
            transcendentals=0,
        ),
        name="fold",
    )(*operands)


def body(amp_tiles, amp_rows, int_tiles, int_codes):
    n_row, n_col = lax.axis_size("row"), lax.axis_size("col")
    rows_held = n_row // n_col
    panels, slots, width = int_tiles.shape[0], int_tiles.shape[1], int_tiles.shape[3]
    across = n_col // CORES
    order = grid_cycle(n_row // across, across)
    forth = [(order[at], order[(at + 1) % n_row]) for at in range(n_row)]
    ways = [forth if panel % 2 == 0 else [(b, a) for a, b in forth] for panel in range(panels)]

    swap = [(c, c // CORES * CORES + (c + 1) % CORES) for c in range(n_col)]
    whole = (MI * width, NJ * width)
    cuts = [n_row - 2, n_row - 1, n_row]

    placed = place(amp_tiles, amp_rows, int_tiles, int_codes)
    streams, parcel = placed[:-1], placed[-1]
    parts, last = [], parcel
    for shift in range(1, n_col // CORES):
        moved = lax.optimization_barrier((parcel, last))[0] if shift > 1 else parcel
        moved = lax.ppermute(moved, "col", [(c, (c + shift * CORES) % n_col) for c in range(n_col)])
        last = lax.ppermute(moved, "col", swap)
        parts += [moved, last]
    last = lax.optimization_barrier((parcel, last))[0]
    parts = [parcel, lax.ppermute(last, "col", swap)] + parts

    codes, ints = collect(parts, panels, slots, rows_held * NJ + 1)
    rings = [[list(streams[group * panels : (group + 1) * panels])] for group in range(len(GROUPS))]
    totals, early, out = [None] * len(GROUPS), [None] * len(GROUPS), None
    for at in range(1, n_row):
        for group, (top, bottom) in enumerate(GROUPS):
            held = rings[group][-1]
            if at == n_row - 1:
                held = lax.optimization_barrier((early[group], held))[1]
            rings[group].append([lax.ppermute(held[panel], "row", ways[panel]) for panel in range(panels)])
        if at + 1 not in cuts:
            continue
        which = cuts.index(at + 1)
        begin = cuts[which - 1] if which else 0
        hops = [(panel, step) for step in range(begin, at + 1) for panel in range(panels)]
        later = None
        if which >= len(cuts) - 2:
            later = [(panel, step) for step in range(at + 1, n_row) for panel in range(panels)]
        for group, (top, bottom) in enumerate(GROUPS):
            chunks = [rings[group][step][panel] for panel, step in hops]
            band = (top * width, (bottom - top) * width)
            made = fold(
                codes, ints, chunks, hops, later, totals[group], out, order, rows_held, slots, band, whole
            )
            if later is None:
                totals[group] = early[group] = made[0]
            elif later:
                totals[group], out = made
            else:
                out = made[0]
    return out


def solution(mesh):
    return jax.shard_map(
        body,
        mesh=mesh,
        in_specs=(
            P(None, "col", "row", None, None),
            P(None, "col", "row"),
            P(None, "col", "row", None, None),
            P(None, "col", "row"),
        ),
        out_specs=P("col", "row"),
        check_vma=False,
    )
```

time: 95.7 us -> 88.7 us (0.927)
  local copies, waits for them, and re-layouts: 13.1 us -> 0 us
  waiting for transfers between devices: 28.5 us -> 40.3 us
  blocking collectives: 5.06 us -> 0 us
    unnamed x59 -> x0, local copies, waits for them, and re-layouts: 13 us -> none
    ppermute x31, waiting for transfers between devices: 28.5 us -> 40.3 us  [the longest x28 39.4 us: body(): lax.ppermute(held[panel], 'row', ways[panel])]
    all_gather x1 -> x0, blocking collectives: 5.06 us -> none  [body(): codes = lax.all_gather(int_codes, 'col', axis=1, tiled=True)]
  transfers between devices with their start and end apart: 31 -> 31, of which waited for: 10 -> 14; matrix products, arithmetic and copies ran while one was open for 1% -> 0% of each run, Pallas kernels for 15% -> 15%
where the time goes in v2:
time: 88.7 us; the launch traced here: 88.6 us
  waiting for transfers between devices  40.3 us (45%)
  starting transfers between devices  31.3 us (35%)
  Pallas kernels  16.9 us (19%)
    ppermute x28, waiting for transfers between devices, body(): lax.ppermute(held[panel], 'row', ways[panel])  39.4 us
    ppermute x28, starting transfers between devices, body(): lax.ppermute(held[panel], 'row', ways[panel])  28.3 us
    pallas_call x6, Pallas kernels, fold(): pl.pallas_call(functools.partial(fold_kernel, first, hops, later, order,...  14.4 us
    ppermute x1, starting transfers between devices, body(): lax.ppermute(moved, 'col', [(c, (c + shift * CORES) % n_col) for c in ran...  3.03 us
  transfers between devices with their start and end apart: 31, of which 14 were waited for; matrix products, arithmetic and copies ran while one was open for 0% of the time, Pallas kernels for 15%

profile of v2, /device:TPU:0, one launch (start us, length us, event | category | flops | bytes accessed | tf_op | source)
XLA Modules:
  0.0 88.6 jit_solution(7159302846459436619)
XLA Ops:
  1.5 3.0 %collective-permute-start = (bf16[1040,256]{1,0:T(8,128)(2,1)S(1)}, bf16[1040,256]{1,0:T(8,128)(2,1)S(1)}, u32[]{:S(2)}, u32[]{:S(2)}) collective-permute-start(bf16[1040,256]{1,0:T(8,128)(2,1)S(1)} %get-tuple-element.22.refs_0_), channel_id=1, source_target_pairs={{0,2},{1,3},{2,0},{3,1},{4,6},{5,7},{6,4},{7,5},{8,10},{9,11},{10,... | collective-permute-start | bytes 1597448 | tf_op jit(solution)/shard_map/ppermute | solution.py:323
  4.6 1.6 %collective-permute-start.17 = (bf16[512,256]{1,0:T(8,128)(2,1)S(1)}, bf16[512,256]{1,0:T(8,128)(2,1)S(1)}, u32[]{:S(2)}, u32[]{:S(2)}) collective-permute-start(bf16[512,256]{1,0:T(8,128)(2,1)S(1)} %get-tuple-element.29.refs_0_), channel_id=1, source_target_pairs={{0,8},{8,16},{16,24},{24,28},{28,20},{20,12},{12,4},{4,0},{1,9},{9... | collective-permute-start | bytes 786440 | tf_op jit(solution)/shard_map/ppermute | solution.py:337
  6.6 1.6 %collective-permute-start.3 = (bf16[512,256]{1,0:T(8,128)(2,1)S(1)}, bf16[512,256]{1,0:T(8,128)(2,1)S(1)}, u32[]{:S(2)}, u32[]{:S(2)}) collective-permute-start(bf16[512,256]{1,0:T(8,128)(2,1)S(1)} %get-tuple-element.25.refs_0_), channel_id=1, source_target_pairs={{0,8},{8,16},{16,24},{24,28},{28,20},{20,12},{12,4},{4,0},{1,9},{9... | collective-permute-start | bytes 786440 | tf_op jit(solution)/shard_map/ppermute | solution.py:337
  8.6 5.2 %collective-permute-done.17.refs_2_ = bf16[512,256]{1,0:T(8,128)(2,1)S(1)} collective-permute-done((bf16[512,256]{1,0:T(8,128)(2,1)S(1)}, bf16[512,256]{1,0:T(8,128)(2,1)S(1)}, u32[]{:S(2)}, u32[]{:S(2)}) %collective-permute-start.17) | collective-permute-done | bytes 262176 | tf_op jit(solution)/shard_map/ppermute | solution.py:337
  13.8 1.6 %collective-permute-start.18 = (bf16[512,256]{1,0:T(8,128)(2,1)S(1)}, bf16[512,256]{1,0:T(8,128)(2,1)S(1)}, u32[]{:S(2)}, u32[]{:S(2)}) collective-permute-start(bf16[512,256]{1,0:T(8,128)(2,1)S(1)} %collective-permute-done.17.refs_2_), channel_id=1, source_target_pairs={{0,8},{8,16},{16,24},{24,28},{28,20},{20,12},{12,4},{4,0},{1,9},{9... | collective-permute-start | bytes 786440 | tf_op jit(solution)/shard_map/ppermute | solution.py:337
  16.7 2.8 %collective-permute-done.3.refs_2_ = bf16[512,256]{1,0:T(8,128)(2,1)S(1)} collective-permute-done((bf16[512,256]{1,0:T(8,128)(2,1)S(1)}, bf16[512,256]{1,0:T(8,128)(2,1)S(1)}, u32[]{:S(2)}, u32[]{:S(2)}) %collective-permute-start.3) | collective-permute-done | bytes 262176 | tf_op jit(solution)/shard_map/ppermute | solution.py:337
  19.4 1.6 %collective-permute-start.5 = (bf16[512,256]{1,0:T(8,128)(2,1)S(1)}, bf16[512,256]{1,0:T(8,128)(2,1)S(1)}, u32[]{:S(2)}, u32[]{:S(2)}) collective-permute-start(bf16[512,256]{1,0:T(8,128)(2,1)S(1)} %collective-permute-done.3.refs_2_), channel_id=1, source_target_pairs={{0,8},{8,16},{16,24},{24,28},{28,20},{20,12},{12,4},{4,0},{1,9},{9... | collective-permute-start | bytes 786440 | tf_op jit(solution)/shard_map/ppermute | solution.py:337
  21.4 3.6 %collective-permute-done.18.refs_4_ = bf16[512,256]{1,0:T(8,128)(2,1)S(1)} collective-permute-done((bf16[512,256]{1,0:T(8,128)(2,1)S(1)}, bf16[512,256]{1,0:T(8,128)(2,1)S(1)}, u32[]{:S(2)}, u32[]{:S(2)}) %collective-permute-start.18) | collective-permute-done | bytes 262176 | tf_op jit(solution)/shard_map/ppermute | solution.py:337
  25.0 1.6 %collective-permute-start.19 = (bf16[512,256]{1,0:T(8,128)(2,1)S(1)}, bf16[512,256]{1,0:T(8,128)(2,1)S(1)}, u32[]{:S(2)}, u32[]{:S(2)}) collective-permute-start(bf16[512,256]{1,0:T(8,128)(2,1)S(1)} %collective-permute-done.18.refs_4_), channel_id=1, source_target_pairs={{0,8},{8,16},{16,24},{24,28},{28,20},{20,12},{12,4},{4,0},{1,9},{9... | collective-permute-start | bytes 786440 | tf_op jit(solution)/shard_map/ppermute | solution.py:337
  27.1 3.6 %collective-permute-done.5.refs_4_ = bf16[512,256]{1,0:T(8,128)(2,1)S(1)} collective-permute-done((bf16[512,256]{1,0:T(8,128)(2,1)S(1)}, bf16[512,256]{1,0:T(8,128)(2,1)S(1)}, u32[]{:S(2)}, u32[]{:S(2)}) %collective-permute-start.5) | collective-permute-done | bytes 262176 | tf_op jit(solution)/shard_map/ppermute | solution.py:337
  30.6 1.6 %collective-permute-start.7 = (bf16[512,256]{1,0:T(8,128)(2,1)S(1)}, bf16[512,256]{1,0:T(8,128)(2,1)S(1)}, u32[]{:S(2)}, u32[]{:S(2)}) collective-permute-start(bf16[512,256]{1,0:T(8,128)(2,1)S(1)} %collective-permute-done.5.refs_4_), channel_id=1, source_target_pairs={{0,8},{8,16},{16,24},{24,28},{28,20},{20,12},{12,4},{4,0},{1,9},{9... | collective-permute-start | bytes 786440 | tf_op jit(solution)/shard_map/ppermute | solution.py:337
  32.7 3.6 %collective-permute-done.19.refs_6_ = bf16[512,256]{1,0:T(8,128)(2,1)S(1)} collective-permute-done((bf16[512,256]{1,0:T(8,128)(2,1)S(1)}, bf16[512,256]{1,0:T(8,128)(2,1)S(1)}, u32[]{:S(2)}, u32[]{:S(2)}) %collective-permute-start.19) | collective-permute-done | bytes 262176 | tf_op jit(solution)/shard_map/ppermute | solution.py:337
  36.3 1.6 %collective-permute-start.20 = (bf16[512,256]{1,0:T(8,128)(2,1)S(1)}, bf16[512,256]{1,0:T(8,128)(2,1)S(1)}, u32[]{:S(2)}, u32[]{:S(2)}) collective-permute-start(bf16[512,256]{1,0:T(8,128)(2,1)S(1)} %collective-permute-done.19.refs_6_), channel_id=1, source_target_pairs={{0,8},{8,16},{16,24},{24,28},{28,20},{20,12},{12,4},{4,0},{1,9},{9... | collective-permute-start | bytes 786440 | tf_op jit(solution)/shard_map/ppermute | solution.py:337
  38.3 3.6 %collective-permute-done.7.refs_6_ = bf16[512,256]{1,0:T(8,128)(2,1)S(1)} collective-permute-done((bf16[512,256]{1,0:T(8,128)(2,1)S(1)}, bf16[512,256]{1,0:T(8,128)(2,1)S(1)}, u32[]{:S(2)}, u32[]{:S(2)}) %collective-permute-start.7) | collective-permute-done | bytes 262176 | tf_op jit(solution)/shard_map/ppermute | solution.py:337
  41.9 1.6 %collective-permute-start.9 = (bf16[512,256]{1,0:T(8,128)(2,1)S(1)}, bf16[512,256]{1,0:T(8,128)(2,1)S(1)}, u32[]{:S(2)}, u32[]{:S(2)}) collective-permute-start(bf16[512,256]{1,0:T(8,128)(2,1)S(1)} %collective-permute-done.7.refs_6_), channel_id=1, source_target_pairs={{0,8},{8,16},{16,24},{24,28},{28,20},{20,12},{12,4},{4,0},{1,9},{9... | collective-permute-start | bytes 786440 | tf_op jit(solution)/shard_map/ppermute | solution.py:337
  43.9 3.6 %collective-permute-done.20.refs_8_ = bf16[512,256]{1,0:T(8,128)(2,1)S(1)} collective-permute-done((bf16[512,256]{1,0:T(8,128)(2,1)S(1)}, bf16[512,256]{1,0:T(8,128)(2,1)S(1)}, u32[]{:S(2)}, u32[]{:S(2)}) %collective-permute-start.20) | collective-permute-done | bytes 262176 | tf_op jit(solution)/shard_map/ppermute | solution.py:337
  47.5 1.6 %collective-permute-start.21 = (bf16[512,256]{1,0:T(8,128)(2,1)S(1)}, bf16[512,256]{1,0:T(8,128)(2,1)S(1)}, u32[]{:S(2)}, u32[]{:S(2)}) collective-permute-start(bf16[512,256]{1,0:T(8,128)(2,1)S(1)} %collective-permute-done.20.refs_8_), channel_id=1, source_target_pairs={{0,8},{8,16},{16,24},{24,28},{28,20},{20,12},{12,4},{4,0},{1,9},{9... | collective-permute-start | bytes 786440 | tf_op jit(solution)/shard_map/ppermute | solution.py:337
  49.5 3.6 %collective-permute-done.9.refs_8_ = bf16[512,256]{1,0:T(8,128)(2,1)S(1)} collective-permute-done((bf16[512,256]{1,0:T(8,128)(2,1)S(1)}, bf16[512,256]{1,0:T(8,128)(2,1)S(1)}, u32[]{:S(2)}, u32[]{:S(2)}) %collective-permute-start.9) | collective-permute-done | bytes 262176 | tf_op jit(solution)/shard_map/ppermute | solution.py:337
  53.1 1.6 %collective-permute-start.11 = (bf16[512,256]{1,0:T(8,128)(2,1)S(1)}, bf16[512,256]{1,0:T(8,128)(2,1)S(1)}, u32[]{:S(2)}, u32[]{:S(2)}) collective-permute-start(bf16[512,256]{1,0:T(8,128)(2,1)S(1)} %collective-permute-done.9.refs_8_), channel_id=1, source_target_pairs={{0,8},{8,16},{16,24},{24,28},{28,20},{20,12},{12,4},{4,0},{1,9},{9... | collective-permute-start | bytes 786440 | tf_op jit(solution)/shard_map/ppermute | solution.py:337
  55.2 3.6 %collective-permute-done.21.refs_10_ = bf16[512,256]{1,0:T(8,128)(2,1)S(1)} collective-permute-done((bf16[512,256]{1,0:T(8,128)(2,1)S(1)}, bf16[512,256]{1,0:T(8,128)(2,1)S(1)}, u32[]{:S(2)}, u32[]{:S(2)}) %collective-permute-start.21) | collective-permute-done | bytes 262176 | tf_op jit(solution)/shard_map/ppermute | solution.py:337
  58.7 1.6 %collective-permute-start.22 = (bf16[512,256]{1,0:T(8,128)(2,1)S(1)}, bf16[512,256]{1,0:T(8,128)(2,1)S(1)}, u32[]{:S(2)}, u32[]{:S(2)}) collective-permute-start(bf16[512,256]{1,0:T(8,128)(2,1)S(1)} %collective-permute-done.21.refs_10_), channel_id=1, source_target_pairs={{0,8},{8,16},{16,24},{24,28},{28,20},{20,12},{12,4},{4,0},{1,9},{9... | collective-permute-start | bytes 786440 | tf_op jit(solution)/shard_map/ppermute | solution.py:337
  60.8 3.6 %collective-permute-done.11.refs_10_ = bf16[512,256]{1,0:T(8,128)(2,1)S(1)} collective-permute-done((bf16[512,256]{1,0:T(8,128)(2,1)S(1)}, bf16[512,256]{1,0:T(8,128)(2,1)S(1)}, u32[]{:S(2)}, u32[]{:S(2)}) %collective-permute-start.11) | collective-permute-done | bytes 262176 | tf_op jit(solution)/shard_map/ppermute | solution.py:337
  64.4 1.6 %collective-permute-start.13 = (bf16[512,256]{1,0:T(8,128)(2,1)S(1)}, bf16[512,256]{1,0:T(8,128)(2,1)S(1)}, u32[]{:S(2)}, u32[]{:S(2)}) collective-permute-start(bf16[512,256]{1,0:T(8,128)(2,1)S(1)} %collective-permute-done.11.refs_10_), channel_id=1, source_target_pairs={{0,8},{8,16},{16,24},{24,28},{28,20},{20,12},{12,4},{4,0},{1,9},{9... | collective-permute-start | bytes 786440 | tf_op jit(solution)/shard_map/ppermute | solution.py:337
  67.3 2.6 %fold.7.refs_2_ = f32[512,1536]{1,0:T(8,128)S(1)} custom-call(s32[2,8]{1,0:T(2,128)S(1)} %get-tuple-element.23.codes_ref, bf16[2,8,256,256]{3,2,1,0:T(8,128)(2,1)S(1)} %get-tuple-element.24.ints_ref, bf16[512,256]{1,0:T(8,128)(2,1)S(1)} %get-tuple-element.29.refs_0_, bf16[512,256]{1,0:T(8,128)(2,1)S(1)} %get-tuple-element.30.refs_1_, ...), custom_call_target="tpu_custom_call" | custom-call | flops 1610612736 | bytes 3145728 | tf_op jit(solution)/shard_map/fold/pallas_call | solution.py:288
  70.0 1.6 %collective-permute-done.28.refs_1_ = bf16[512,256]{1,0:T(8,128)(2,1)S(1)} collective-permute-done((bf16[512,256]{1,0:T(8,128)(2,1)S(1)}, bf16[512,256]{1,0:T(8,128)(2,1)S(1)}, u32[]{:S(2)}, u32[]{:S(2)}) %collective-permute-start.28) | collective-permute-done | bytes 262176 | tf_op jit(solution)/shard_map/ppermute | solution.py:337
  71.6 1.6 %collective-permute-start.29 = (bf16[512,256]{1,0:T(8,128)(2,1)S(1)}, bf16[512,256]{1,0:T(8,128)(2,1)S(1)}, u32[]{:S(2)}, u32[]{:S(2)}) collective-permute-start(bf16[512,256]{1,0:T(8,128)(2,1)S(1)} %collective-permute-done.22.refs_0_), channel_id=1, source_target_pairs={{0,8},{8,16},{16,24},{24,28},{28,20},{20,12},{12,4},{4,0},{1,9},{9... | collective-permute-start | bytes 786440 | tf_op jit(solution)/shard_map/ppermute | solution.py:337
  73.6 2.6 %fold.6.refs_2_ = f32[512,1536]{1,0:T(8,128)S(1)} custom-call(s32[2,8]{1,0:T(2,128)S(1)} %get-tuple-element.23.codes_ref, bf16[2,8,256,256]{3,2,1,0:T(8,128)(2,1)S(1)} %get-tuple-element.24.ints_ref, bf16[512,256]{1,0:T(8,128)(2,1)S(1)} %get-tuple-element.25.refs_0_, bf16[512,256]{1,0:T(8,128)(2,1)S(1)} %get-tuple-element.26.refs_1_, ...), custom_call_target="tpu_custom_call" | custom-call | flops 1610612736 | bytes 3145728 | tf_op jit(solution)/shard_map/fold/pallas_call | solution.py:288
  77.2 1.6 %collective-permute-start.15 = (bf16[512,256]{1,0:T(8,128)(2,1)S(1)}, bf16[512,256]{1,0:T(8,128)(2,1)S(1)}, u32[]{:S(2)}, u32[]{:S(2)}) collective-permute-start(bf16[512,256]{1,0:T(8,128)(2,1)S(1)} %collective-permute-done.13.refs_0_), channel_id=1, source_target_pairs={{0,8},{8,16},{16,24},{24,28},{28,20},{20,12},{12,4},{4,0},{1,9},{9... | collective-permute-start | bytes 786440 | tf_op jit(solution)/shard_map/ppermute | solution.py:337
  79.2 2.7 %fold.8 = (f32[512,1536]{1,0:T(8,128)S(1)}, f32[1024,1536]{1,0:T(8,128)}) custom-call(s32[2,8]{1,0:T(2,128)S(1)} %get-tuple-element.23.codes_ref, bf16[2,8,256,256]{3,2,1,0:T(8,128)(2,1)S(1)} %get-tuple-element.24.ints_ref, bf16[512,256]{1,0:T(8,128)(2,1)S(1)} %collective-permute-done.22.refs_0_, ...), custom_call_target="tpu_custom_call", output_to_operand_aliasing={{0}: (4, {})} | custom-call | flops 268435456 | bytes 3145728 | tf_op jit(solution)/shard_map/fold/pallas_call | solution.py:288
  81.9 2.7 %fold.9 = (f32[512,1536]{1,0:T(8,128)S(1)}, f32[1024,1536]{1,0:T(8,128)}) custom-call(s32[2,8]{1,0:T(2,128)S(1)} %get-tuple-element.23.codes_ref, bf16[2,8,256,256]{3,2,1,0:T(8,128)(2,1)S(1)} %get-tuple-element.24.ints_ref, bf16[512,256]{1,0:T(8,128)(2,1)S(1)} %collective-permute-done.13.refs_0_, ...), custom_call_target="tpu_custom_call", output_to_operand_aliasing={{0}: (4, {}), {1}: (5, {})} | custom-call | flops 268435456 | bytes 3145728 | tf_op jit(solution)/shard_map/fold/pallas_call | solution.py:288
  84.7 1.9 %fold.10.refs_3_ = f32[1024,1536]{1,0:T(8,128)} custom-call(s32[2,8]{1,0:T(2,128)S(1)} %get-tuple-element.23.codes_ref, bf16[2,8,256,256]{3,2,1,0:T(8,128)(2,1)S(1)} %get-tuple-element.24.ints_ref, bf16[512,256]{1,0:T(8,128)(2,1)S(1)} %collective-permute-done.29.refs_0_, ...), custom_call_target="tpu_custom_call", output_to_operand_aliasing={{}: (5, {})} | custom-call | flops 268435456 | bytes 3145728 | tf_op jit(solution)/shard_map/fold/pallas_call | solution.py:288
  86.6 1.9 %fold.11 = f32[1024,1536]{1,0:T(8,128)} custom-call(s32[2,8]{1,0:T(2,128)S(1)} %get-tuple-element.23.codes_ref, bf16[2,8,256,256]{3,2,1,0:T(8,128)(2,1)S(1)} %get-tuple-element.24.ints_ref, bf16[512,256]{1,0:T(8,128)(2,1)S(1)} %collective-permute-done.15.refs_0_, ...), custom_call_target="tpu_custom_call", output_to_operand_aliasing={{}: (5, {})} | custom-call | flops 268435456 | bytes 3145728 | tf_op jit(solution)/shard_map/fold/pallas_call | solution.py:288
  (38 shorter events, 10.8 us)
Async XLA Ops:
  1.5 15.1 %collective-permute-start = (bf16[1040,256]{1,0:T(8,128)(2,1)S(1)}, bf16[1040,256]{1,0:T(8,128)(2,1)S(1)}, u32[]{:S(2)}, u32[]{:S(2)}) collective-permute-start(bf16[1040,256]{1,0:T(8,128)(2,1)S(1)} %get-tuple-element.22.refs_0_), channel_id=1, source_target_pairs={{0,2},{1,3},{2,0},{3,1},{4,6},{5,7},{6,4},{7,5},{8,10},{9,11},{10,... | collective-permute-start | bytes 1597448 | tf_op jit(solution)/shard_map/ppermute | solution.py:323
  4.6 9.2 %collective-permute-start.17 = (bf16[512,256]{1,0:T(8,128)(2,1)S(1)}, bf16[512,256]{1,0:T(8,128)(2,1)S(1)}, u32[]{:S(2)}, u32[]{:S(2)}) collective-permute-start(bf16[512,256]{1,0:T(8,128)(2,1)S(1)} %get-tuple-element.29.refs_0_), channel_id=1, source_target_pairs={{0,8},{8,16},{16,24},{24,28},{28,20},{20,12},{12,4},{4,0},{1,9},{9... | collective-permute-start | bytes 786440 | tf_op jit(solution)/shard_map/ppermute | solution.py:337
  6.1 9.2 %collective-permute-start.23 = (bf16[512,256]{1,0:T(8,128)(2,1)S(1)}, bf16[512,256]{1,0:T(8,128)(2,1)S(1)}, u32[]{:S(2)}, u32[]{:S(2)}) collective-permute-start(bf16[512,256]{1,0:T(8,128)(2,1)S(1)} %get-tuple-element.30.refs_1_), channel_id=1, source_target_pairs={{8,0},{16,8},{24,16},{28,24},{20,28},{12,20},{4,12},{0,4},{9,1},{1... | collective-permute-start | bytes 786440 | tf_op jit(solution)/shard_map/ppermute | solution.py:337
  6.6 12.8 %collective-permute-start.3 = (bf16[512,256]{1,0:T(8,128)(2,1)S(1)}, bf16[512,256]{1,0:T(8,128)(2,1)S(1)}, u32[]{:S(2)}, u32[]{:S(2)}) collective-permute-start(bf16[512,256]{1,0:T(8,128)(2,1)S(1)} %get-tuple-element.25.refs_0_), channel_id=1, source_target_pairs={{0,8},{8,16},{16,24},{24,28},{28,20},{20,12},{12,4},{4,0},{1,9},{9... | collective-permute-start | bytes 786440 | tf_op jit(solution)/shard_map/ppermute | solution.py:337
  8.2 12.8 %collective-permute-start.4 = (bf16[512,256]{1,0:T(8,128)(2,1)S(1)}, bf16[512,256]{1,0:T(8,128)(2,1)S(1)}, u32[]{:S(2)}, u32[]{:S(2)}) collective-permute-start(bf16[512,256]{1,0:T(8,128)(2,1)S(1)} %get-tuple-element.26.refs_1_), channel_id=1, source_target_pairs={{8,0},{16,8},{24,16},{28,24},{20,28},{12,20},{4,12},{0,4},{9,1},{1... | collective-permute-start | bytes 786440 | tf_op jit(solution)/shard_map/ppermute | solution.py:337
  13.8 11.2 %collective-permute-start.18 = (bf16[512,256]{1,0:T(8,128)(2,1)S(1)}, bf16[512,256]{1,0:T(8,128)(2,1)S(1)}, u32[]{:S(2)}, u32[]{:S(2)}) collective-permute-start(bf16[512,256]{1,0:T(8,128)(2,1)S(1)} %collective-permute-done.17.refs_2_), channel_id=1, source_target_pairs={{0,8},{8,16},{16,24},{24,28},{28,20},{20,12},{12,4},{4,0},{1,9},{9... | collective-permute-start | bytes 786440 | tf_op jit(solution)/shard_map/ppermute | solution.py:337
  15.4 11.2 %collective-permute-start.24 = (bf16[512,256]{1,0:T(8,128)(2,1)S(1)}, bf16[512,256]{1,0:T(8,128)(2,1)S(1)}, u32[]{:S(2)}, u32[]{:S(2)}) collective-permute-start(bf16[512,256]{1,0:T(8,128)(2,1)S(1)} %collective-permute-done.23.refs_3_), channel_id=1, source_target_pairs={{8,0},{16,8},{24,16},{28,24},{20,28},{12,20},{4,12},{0,4},{9,1},{1... | collective-permute-start | bytes 786440 | tf_op jit(solution)/shard_map/ppermute | solution.py:337
  16.7 21.6 %collective-permute-start.1 = (bf16[1040,256]{1,0:T(8,128)(2,1)S(1)}, bf16[1040,256]{1,0:T(8,128)(2,1)S(1)}, u32[]{:S(2)}, u32[]{:S(2)}) collective-permute-start(bf16[1040,256]{1,0:T(8,128)(2,1)S(1)} %collective-permute-done.refs_2_), channel_id=1, source_target_pairs={{0,1},{1,0},{2,3},{3,2},{4,5},{5,4},{6,7},{7,6},{8,9},{9,8},{10,11... | collective-permute-start | bytes 1597448 | tf_op jit(solution)/shard_map/ppermute | solution.py:324
  19.4 11.2 %collective-permute-start.5 = (bf16[512,256]{1,0:T(8,128)(2,1)S(1)}, bf16[512,256]{1,0:T(8,128)(2,1)S(1)}, u32[]{:S(2)}, u32[]{:S(2)}) collective-permute-start(bf16[512,256]{1,0:T(8,128)(2,1)S(1)} %collective-permute-done.3.refs_2_), channel_id=1, source_target_pairs={{0,8},{8,16},{16,24},{24,28},{28,20},{20,12},{12,4},{4,0},{1,9},{9... | collective-permute-start | bytes 786440 | tf_op jit(solution)/shard_map/ppermute | solution.py:337
  21.0 11.2 %collective-permute-start.6 = (bf16[512,256]{1,0:T(8,128)(2,1)S(1)}, bf16[512,256]{1,0:T(8,128)(2,1)S(1)}, u32[]{:S(2)}, u32[]{:S(2)}) collective-permute-start(bf16[512,256]{1,0:T(8,128)(2,1)S(1)} %collective-permute-done.4.refs_3_), channel_id=1, source_target_pairs={{8,0},{16,8},{24,16},{28,24},{20,28},{12,20},{4,12},{0,4},{9,1},{1... | collective-permute-start | bytes 786440 | tf_op jit(solution)/shard_map/ppermute | solution.py:337
  25.0 11.2 %collective-permute-start.19 = (bf16[512,256]{1,0:T(8,128)(2,1)S(1)}, bf16[512,256]{1,0:T(8,128)(2,1)S(1)}, u32[]{:S(2)}, u32[]{:S(2)}) collective-permute-start(bf16[512,256]{1,0:T(8,128)(2,1)S(1)} %collective-permute-done.18.refs_4_), channel_id=1, source_target_pairs={{0,8},{8,16},{16,24},{24,28},{28,20},{20,12},{12,4},{4,0},{1,9},{9... | collective-permute-start | bytes 786440 | tf_op jit(solution)/shard_map/ppermute | solution.py:337
  26.6 11.2 %collective-permute-start.25 = (bf16[512,256]{1,0:T(8,128)(2,1)S(1)}, bf16[512,256]{1,0:T(8,128)(2,1)S(1)}, u32[]{:S(2)}, u32[]{:S(2)}) collective-permute-start(bf16[512,256]{1,0:T(8,128)(2,1)S(1)} %collective-permute-done.24.refs_5_), channel_id=1, source_target_pairs={{8,0},{16,8},{24,16},{28,24},{20,28},{12,20},{4,12},{0,4},{9,1},{1... | collective-permute-start | bytes 786440 | tf_op jit(solution)/shard_map/ppermute | solution.py:337
  30.6 11.2 %collective-permute-start.7 = (bf16[512,256]{1,0:T(8,128)(2,1)S(1)}, bf16[512,256]{1,0:T(8,128)(2,1)S(1)}, u32[]{:S(2)}, u32[]{:S(2)}) collective-permute-start(bf16[512,256]{1,0:T(8,128)(2,1)S(1)} %collective-permute-done.5.refs_4_), channel_id=1, source_target_pairs={{0,8},{8,16},{16,24},{24,28},{28,20},{20,12},{12,4},{4,0},{1,9},{9... | collective-permute-start | bytes 786440 | tf_op jit(solution)/shard_map/ppermute | solution.py:337
  32.2 11.2 %collective-permute-start.8 = (bf16[512,256]{1,0:T(8,128)(2,1)S(1)}, bf16[512,256]{1,0:T(8,128)(2,1)S(1)}, u32[]{:S(2)}, u32[]{:S(2)}) collective-permute-start(bf16[512,256]{1,0:T(8,128)(2,1)S(1)} %collective-permute-done.6.refs_5_), channel_id=1, source_target_pairs={{8,0},{16,8},{24,16},{28,24},{20,28},{12,20},{4,12},{0,4},{9,1},{1... | collective-permute-start | bytes 786440 | tf_op jit(solution)/shard_map/ppermute | solution.py:337
  36.3 11.2 %collective-permute-start.20 = (bf16[512,256]{1,0:T(8,128)(2,1)S(1)}, bf16[512,256]{1,0:T(8,128)(2,1)S(1)}, u32[]{:S(2)}, u32[]{:S(2)}) collective-permute-start(bf16[512,256]{1,0:T(8,128)(2,1)S(1)} %collective-permute-done.19.refs_6_), channel_id=1, source_target_pairs={{0,8},{8,16},{16,24},{24,28},{28,20},{20,12},{12,4},{4,0},{1,9},{9... | collective-permute-start | bytes 786440 | tf_op jit(solution)/shard_map/ppermute | solution.py:337
  37.9 11.2 %collective-permute-start.26 = (bf16[512,256]{1,0:T(8,128)(2,1)S(1)}, bf16[512,256]{1,0:T(8,128)(2,1)S(1)}, u32[]{:S(2)}, u32[]{:S(2)}) collective-permute-start(bf16[512,256]{1,0:T(8,128)(2,1)S(1)} %collective-permute-done.25.refs_7_), channel_id=1, source_target_pairs={{8,0},{16,8},{24,16},{28,24},{20,28},{12,20},{4,12},{0,4},{9,1},{1... | collective-permute-start | bytes 786440 | tf_op jit(solution)/shard_map/ppermute | solution.py:337
  38.3 28.1 %collective-permute-start.2 = (bf16[1040,256]{1,0:T(8,128)(2,1)S(1)}, bf16[1040,256]{1,0:T(8,128)(2,1)S(1)}, u32[]{:S(2)}, u32[]{:S(2)}) collective-permute-start(bf16[1040,256]{1,0:T(8,128)(2,1)S(1)} %get-tuple-element.22.refs_0_), channel_id=1, source_target_pairs={{0,1},{1,0},{2,3},{3,2},{4,5},{5,4},{6,7},{7,6},{8,9},{9,8},{10,11... | collective-permute-start | bytes 1597448 | tf_op jit(solution)/shard_map/ppermute | solution.py:327
  41.9 11.2 %collective-permute-start.9 = (bf16[512,256]{1,0:T(8,128)(2,1)S(1)}, bf16[512,256]{1,0:T(8,128)(2,1)S(1)}, u32[]{:S(2)}, u32[]{:S(2)}) collective-permute-start(bf16[512,256]{1,0:T(8,128)(2,1)S(1)} %collective-permute-done.7.refs_6_), channel_id=1, source_target_pairs={{0,8},{8,16},{16,24},{24,28},{28,20},{20,12},{12,4},{4,0},{1,9},{9... | collective-permute-start | bytes 786440 | tf_op jit(solution)/shard_map/ppermute | solution.py:337
  43.5 11.2 %collective-permute-start.10 = (bf16[512,256]{1,0:T(8,128)(2,1)S(1)}, bf16[512,256]{1,0:T(8,128)(2,1)S(1)}, u32[]{:S(2)}, u32[]{:S(2)}) collective-permute-start(bf16[512,256]{1,0:T(8,128)(2,1)S(1)} %collective-permute-done.8.refs_7_), channel_id=1, source_target_pairs={{8,0},{16,8},{24,16},{28,24},{20,28},{12,20},{4,12},{0,4},{9,1},{1... | collective-permute-start | bytes 786440 | tf_op jit(solution)/shard_map/ppermute | solution.py:337
  47.5 11.2 %collective-permute-start.21 = (bf16[512,256]{1,0:T(8,128)(2,1)S(1)}, bf16[512,256]{1,0:T(8,128)(2,1)S(1)}, u32[]{:S(2)}, u32[]{:S(2)}) collective-permute-start(bf16[512,256]{1,0:T(8,128)(2,1)S(1)} %collective-permute-done.20.refs_8_), channel_id=1, source_target_pairs={{0,8},{8,16},{16,24},{24,28},{28,20},{20,12},{12,4},{4,0},{1,9},{9... | collective-permute-start | bytes 786440 | tf_op jit(solution)/shard_map/ppermute | solution.py:337
  49.1 11.2 %collective-permute-start.27 = (bf16[512,256]{1,0:T(8,128)(2,1)S(1)}, bf16[512,256]{1,0:T(8,128)(2,1)S(1)}, u32[]{:S(2)}, u32[]{:S(2)}) collective-permute-start(bf16[512,256]{1,0:T(8,128)(2,1)S(1)} %collective-permute-done.26.refs_9_), channel_id=1, source_target_pairs={{8,0},{16,8},{24,16},{28,24},{20,28},{12,20},{4,12},{0,4},{9,1},{1... | collective-permute-start | bytes 786440 | tf_op jit(solution)/shard_map/ppermute | solution.py:337
  53.1 11.2 %collective-permute-start.11 = (bf16[512,256]{1,0:T(8,128)(2,1)S(1)}, bf16[512,256]{1,0:T(8,128)(2,1)S(1)}, u32[]{:S(2)}, u32[]{:S(2)}) collective-permute-start(bf16[512,256]{1,0:T(8,128)(2,1)S(1)} %collective-permute-done.9.refs_8_), channel_id=1, source_target_pairs={{0,8},{8,16},{16,24},{24,28},{28,20},{20,12},{12,4},{4,0},{1,9},{9... | collective-permute-start | bytes 786440 | tf_op jit(solution)/shard_map/ppermute | solution.py:337
  54.7 11.2 %collective-permute-start.12 = (bf16[512,256]{1,0:T(8,128)(2,1)S(1)}, bf16[512,256]{1,0:T(8,128)(2,1)S(1)}, u32[]{:S(2)}, u32[]{:S(2)}) collective-permute-start(bf16[512,256]{1,0:T(8,128)(2,1)S(1)} %collective-permute-done.10.refs_9_), channel_id=1, source_target_pairs={{8,0},{16,8},{24,16},{28,24},{20,28},{12,20},{4,12},{0,4},{9,1},{1... | collective-permute-start | bytes 786440 | tf_op jit(solution)/shard_map/ppermute | solution.py:337
  58.7 11.2 %collective-permute-start.22 = (bf16[512,256]{1,0:T(8,128)(2,1)S(1)}, bf16[512,256]{1,0:T(8,128)(2,1)S(1)}, u32[]{:S(2)}, u32[]{:S(2)}) collective-permute-start(bf16[512,256]{1,0:T(8,128)(2,1)S(1)} %collective-permute-done.21.refs_10_), channel_id=1, source_target_pairs={{0,8},{8,16},{16,24},{24,28},{28,20},{20,12},{12,4},{4,0},{1,9},{9... | collective-permute-start | bytes 786440 | tf_op jit(solution)/shard_map/ppermute | solution.py:337
  60.3 11.2 %collective-permute-start.28 = (bf16[512,256]{1,0:T(8,128)(2,1)S(1)}, bf16[512,256]{1,0:T(8,128)(2,1)S(1)}, u32[]{:S(2)}, u32[]{:S(2)}) collective-permute-start(bf16[512,256]{1,0:T(8,128)(2,1)S(1)} %collective-permute-done.27.refs_11_), channel_id=1, source_target_pairs={{8,0},{16,8},{24,16},{28,24},{20,28},{12,20},{4,12},{0,4},{9,1},{1... | collective-permute-start | bytes 786440 | tf_op jit(solution)/shard_map/ppermute | solution.py:337
  64.4 11.8 %collective-permute-start.13 = (bf16[512,256]{1,0:T(8,128)(2,1)S(1)}, bf16[512,256]{1,0:T(8,128)(2,1)S(1)}, u32[]{:S(2)}, u32[]{:S(2)}) collective-permute-start(bf16[512,256]{1,0:T(8,128)(2,1)S(1)} %collective-permute-done.11.refs_10_), channel_id=1, source_target_pairs={{0,8},{8,16},{16,24},{24,28},{28,20},{20,12},{12,4},{4,0},{1,9},{9... | collective-permute-start | bytes 786440 | tf_op jit(solution)/shard_map/ppermute | solution.py:337
  65.9 11.2 %collective-permute-start.14 = (bf16[512,256]{1,0:T(8,128)(2,1)S(1)}, bf16[512,256]{1,0:T(8,128)(2,1)S(1)}, u32[]{:S(2)}, u32[]{:S(2)}) collective-permute-start(bf16[512,256]{1,0:T(8,128)(2,1)S(1)} %collective-permute-done.12.refs_11_), channel_id=1, source_target_pairs={{8,0},{16,8},{24,16},{28,24},{20,28},{12,20},{4,12},{0,4},{9,1},{1... | collective-permute-start | bytes 786440 | tf_op jit(solution)/shard_map/ppermute | solution.py:337
  71.6 13.1 %collective-permute-start.29 = (bf16[512,256]{1,0:T(8,128)(2,1)S(1)}, bf16[512,256]{1,0:T(8,128)(2,1)S(1)}, u32[]{:S(2)}, u32[]{:S(2)}) collective-permute-start(bf16[512,256]{1,0:T(8,128)(2,1)S(1)} %collective-permute-done.22.refs_0_), channel_id=1, source_target_pairs={{0,8},{8,16},{16,24},{24,28},{28,20},{20,12},{12,4},{4,0},{1,9},{9... | collective-permute-start | bytes 786440 | tf_op jit(solution)/shard_map/ppermute | solution.py:337
  73.1 11.5 %collective-permute-start.30 = (bf16[512,256]{1,0:T(8,128)(2,1)S(1)}, bf16[512,256]{1,0:T(8,128)(2,1)S(1)}, u32[]{:S(2)}, u32[]{:S(2)}) collective-permute-start(bf16[512,256]{1,0:T(8,128)(2,1)S(1)} %collective-permute-done.28.refs_1_), channel_id=1, source_target_pairs={{8,0},{16,8},{24,16},{28,24},{20,28},{12,20},{4,12},{0,4},{9,1},{1... | collective-permute-start | bytes 786440 | tf_op jit(solution)/shard_map/ppermute | solution.py:337
  77.2 9.4 %collective-permute-start.15 = (bf16[512,256]{1,0:T(8,128)(2,1)S(1)}, bf16[512,256]{1,0:T(8,128)(2,1)S(1)}, u32[]{:S(2)}, u32[]{:S(2)}) collective-permute-start(bf16[512,256]{1,0:T(8,128)(2,1)S(1)} %collective-permute-done.13.refs_0_), channel_id=1, source_target_pairs={{0,8},{8,16},{16,24},{24,28},{28,20},{20,12},{12,4},{4,0},{1,9},{9... | collective-permute-start | bytes 786440 | tf_op jit(solution)/shard_map/ppermute | solution.py:337
  78.8 7.9 %collective-permute-start.16 = (bf16[512,256]{1,0:T(8,128)(2,1)S(1)}, bf16[512,256]{1,0:T(8,128)(2,1)S(1)}, u32[]{:S(2)}, u32[]{:S(2)}) collective-permute-start(bf16[512,256]{1,0:T(8,128)(2,1)S(1)} %collective-permute-done.14.refs_1_), channel_id=1, source_target_pairs={{8,0},{16,8},{24,16},{28,24},{20,28},{12,20},{4,12},{0,4},{9,1},{1... | collective-permute-start | bytes 786440 | tf_op jit(solution)/shard_map/ppermute | solution.py:337

commit v3 on v2

--- a/solution.py
+++ b/solution.py
@@ -119,12 +119,34 @@
     )(in_hbm(amp_rows), in_hbm(codes), in_hbm(amp_tiles), in_hbm(int_tiles))
 
 
+def join_kernel(*refs):
+    size = refs[0].shape[0]
+    for at, ref in enumerate(refs[:-1]):
+        refs[-1][pl.ds(at * size, size)] = ref[...]
+
+
+def join(parts):
+    size, width = parts[0].shape
+    vmem = pl.BlockSpec(memory_space=pltpu.VMEM)
+    return pl.pallas_call(
+        join_kernel,
+        out_shape=pltpu.VMEM((size * len(parts), width), parts[0].dtype),
+        in_specs=[vmem] * len(parts),
+        out_specs=vmem,
+        compiler_params=pltpu.CompilerParams(vmem_limit_bytes=VMEM_LIMIT),
+        name="join",
+    )(*map(in_vmem, parts))
+
+
 def collect_kernel(panels, slots, base, *refs):
-    parts, codes_ref, out_ref = refs[:-2], refs[-2], refs[-1]
-    width = parts[0].shape[1]
+    refs, totals = refs[: -len(GROUPS)], refs[-len(GROUPS) :]
+    joined, codes_ref, out_ref = refs[:-2], refs[-2], refs[-1]
+    width = joined[0].shape[1]
+    size = panels * slots * width + LINES
+    depth = len(joined)
+    parts = [joined[shift].at[pl.ds(flip * size, size)] for shift in range(depth) for flip in range(CORES)]
     col = lax.axis_index("col")
     y, core = col // CORES, lax.rem(col, CORES)
-    depth = len(parts) // CORES
     owners = []
     for at, part in enumerate(parts):
         shift, flip = at // CORES, at % CORES
@@ -145,21 +167,24 @@
             for slot in range(slots):
                 codes_ref[panel, owner * slots + slot] = lax.rem(digits, base) - 1
                 digits = digits // base
+    for total_ref in totals:
+        total_ref[...] = jnp.zeros(total_ref.shape, jnp.float32)
 
 
 def collect(parts, panels, slots, base):
     width = parts[0].shape[1]
-    total = slots * len(parts)
+    total = slots * CORES * len(parts)
     assert base ** (panels * slots) < 2**24
     vmem = pl.BlockSpec(memory_space=pltpu.VMEM)
     return pl.pallas_call(
         functools.partial(collect_kernel, panels, slots, base),
         out_shape=[
-            jax.ShapeDtypeStruct((panels, total), jnp.int32),
+            pltpu.SMEM((panels, total), jnp.int32),
             pltpu.VMEM((panels, total, width, width), parts[0].dtype),
+            *(pltpu.VMEM(((last - first) * width, NJ * width), jnp.float32) for first, last in GROUPS),
         ],
         in_specs=[vmem] * len(parts),
-        out_specs=[pl.BlockSpec(memory_space=pltpu.SMEM), vmem],
+        out_specs=[pl.BlockSpec(memory_space=pltpu.SMEM)] + [vmem] * (1 + len(GROUPS)),
         compiler_params=pltpu.CompilerParams(vmem_limit_bytes=VMEM_LIMIT),
         name="collect",
     )(*map(in_vmem, parts))
@@ -266,7 +291,7 @@
     rows, width = chunks[0].shape
     vmem = pl.BlockSpec(memory_space=pltpu.VMEM)
     anywhere = pl.BlockSpec(memory_space=pl.ANY)
-    operands = [codes, in_vmem(ints), *map(in_vmem, chunks)]
+    operands = [pltpu.with_memory_space_constraint(codes, pltpu.SMEM), in_vmem(ints), *map(in_vmem, chunks)]
     in_specs = [pl.BlockSpec(memory_space=pltpu.SMEM)] + [vmem] * (1 + len(chunks))
     aliases, scratch, out_shapes, out_specs = {}, [], [], []
     if not first:
@@ -313,27 +338,24 @@
 
     swap = [(c, c // CORES * CORES + (c + 1) % CORES) for c in range(n_col)]
     whole = (MI * width, NJ * width)
-    cuts = [n_row - 2, n_row - 1, n_row]
+    cuts = [n_row - 3, n_row - 1, n_row]
 
     placed = place(amp_tiles, amp_rows, int_tiles, int_codes)
     streams, parcel = placed[:-1], placed[-1]
-    parts, last = [], parcel
+    parts = [join([parcel, lax.ppermute(parcel, "col", swap)])]
     for shift in range(1, n_col // CORES):
-        moved = lax.optimization_barrier((parcel, last))[0] if shift > 1 else parcel
-        moved = lax.ppermute(moved, "col", [(c, (c + shift * CORES) % n_col) for c in range(n_col)])
-        last = lax.ppermute(moved, "col", swap)
-        parts += [moved, last]
-    last = lax.optimization_barrier((parcel, last))[0]
-    parts = [parcel, lax.ppermute(last, "col", swap)] + parts
-
-    codes, ints = collect(parts, panels, slots, rows_held * NJ + 1)
+        moved = lax.optimization_barrier((parts[0], parts[-1]))[0] if shift > 1 else parts[0]
+        parts.append(lax.ppermute(moved, "col", [(c, (c + shift * CORES) % n_col) for c in range(n_col)]))
+    codes, ints, *totals = collect(parts, panels, slots, rows_held * NJ + 1)
     rings = [[list(streams[group * panels : (group + 1) * panels])] for group in range(len(GROUPS))]
-    totals, early, out = [None] * len(GROUPS), [None] * len(GROUPS), None
+    early, out = [None] * len(GROUPS), None
     for at in range(1, n_row):
         for group, (top, bottom) in enumerate(GROUPS):
             held = rings[group][-1]
+            if at == n_row - 2 and group == len(GROUPS) - 1:
+                held = [lax.optimization_barrier((ints, one))[1] for one in held]
             if at == n_row - 1:
-                held = lax.optimization_barrier((early[group], held))[1]
+                held = [lax.optimization_barrier((early[group], one))[1] for one in held]
             rings[group].append([lax.ppermute(held[panel], "row", ways[panel]) for panel in range(panels)])
         if at + 1 not in cuts:
             continue

time: 88.7 us -> 87.4 us (0.985)
  Pallas kernels: 16.9 us -> 13.5 us
  waiting for transfers between devices: 40.3 us -> 42 us
    pallas_call x6, Pallas kernels: 14.4 us -> 11.2 us  [fold(): pl.pallas_call(functools.partial(fold_kernel, first, hops, later, order,...]
    ppermute x28, waiting for transfers between devices: 39.4 us -> 42 us  [body(): lax.ppermute(held[panel], 'row', ways[panel])]
    ppermute x1, starting transfers between devices: 3.03 us -> 2.03 us  [body(): lax.ppermute(moved, 'col', [(c, (c + shift * CORES) % n_col) for c in ran...]
  transfers between devices with their start and end apart: 31 -> 30, of which waited for: 14 -> 13; matrix products, arithmetic and copies ran while one was open for 0% -> 0% of each run, Pallas kernels for 15% -> 12%
where the time goes in v3:
time: 87.4 us; the launch traced here: 87.2 us
  waiting for transfers between devices  42 us (48%)
  starting transfers between devices  31.6 us (36%)
  Pallas kernels  13.5 us (15%)
    ppermute x28, waiting for transfers between devices, body(): lax.ppermute(held[panel], 'row', ways[panel])  42 us
    ppermute x28, starting transfers between devices, body(): lax.ppermute(held[panel], 'row', ways[panel])  29 us
    pallas_call x6, Pallas kernels, fold(): pl.pallas_call(functools.partial(fold_kernel, first, hops, later, order,...  11.2 us
    ppermute x1, starting transfers between devices, body(): lax.ppermute(moved, 'col', [(c, (c + shift * CORES) % n_col) for c in ran...  2.03 us
  transfers between devices with their start and end apart: 30, of which 13 were waited for; matrix products, arithmetic and copies ran while one was open for 0% of the time, Pallas kernels for 12%

profile of v3, /device:TPU:0, one launch (start us, length us, event | category | flops | bytes accessed | tf_op | source)
XLA Modules:
  0.0 87.2 jit_solution(6705576522078321841)
XLA Ops:
  0.0 1.5 %place.1 = (bf16[512,256]{1,0:T(8,128)(2,1)S(1)}, bf16[512,256]{1,0:T(8,128)(2,1)S(1)}, bf16[512,256]{1,0:T(8,128)(2,1)S(1)}, bf16[512,256]{1,0:T(8,128)(2,1)S(1)}, bf16[1040,256]{1,0:T(8,128)(2,1)S(1)}) custom-call(s32[2,1,4]{2,1,0:T(1,128)} %rows_hbm.1, s32[2,1,2]{2,1,0:T(1,128)} %bitcast.3, bf16[2,1,4,256,256]{4,3,2,1,0:T(8,128)(2,1)} %tiles_hbm.1, ...), custom_call_target="tpu_custom_call" | custom-call | tf_op jit(solution)/shard_map/place/pallas_call | solution.py:104
  2.0 2.6 %collective-permute-start.16 = (bf16[512,256]{1,0:T(8,128)(2,1)S(1)}, bf16[512,256]{1,0:T(8,128)(2,1)S(1)}, u32[]{:S(2)}, u32[]{:S(2)}) collective-permute-start(bf16[512,256]{1,0:T(8,128)(2,1)S(1)} %get-tuple-element.34.refs_0_), channel_id=1, source_target_pairs={{0,8},{8,16},{16,24},{24,28},{28,20},{20,12},{12,4},{4,0},{1,9},{9... | collective-permute-start | bytes 786440 | tf_op jit(solution)/shard_map/ppermute | solution.py:359
  4.7 1.9 %collective-permute-start.3 = (bf16[512,256]{1,0:T(8,128)(2,1)S(1)}, bf16[512,256]{1,0:T(8,128)(2,1)S(1)}, u32[]{:S(2)}, u32[]{:S(2)}) collective-permute-start(bf16[512,256]{1,0:T(8,128)(2,1)S(1)} %get-tuple-element.28.refs_1_), channel_id=1, source_target_pairs={{8,0},{16,8},{24,16},{28,24},{20,28},{12,20},{4,12},{0,4},{9,1},{1... | collective-permute-start | bytes 786440 | tf_op jit(solution)/shard_map/ppermute | solution.py:359
  6.7 5.0 %collective-permute-done.16.refs_2_ = bf16[512,256]{1,0:T(8,128)(2,1)S(1)} collective-permute-done((bf16[512,256]{1,0:T(8,128)(2,1)S(1)}, bf16[512,256]{1,0:T(8,128)(2,1)S(1)}, u32[]{:S(2)}, u32[]{:S(2)}) %collective-permute-start.16) | collective-permute-done | bytes 262176 | tf_op jit(solution)/shard_map/ppermute | solution.py:359
  11.8 2.0 %collective-permute-start.17 = (bf16[512,256]{1,0:T(8,128)(2,1)S(1)}, bf16[512,256]{1,0:T(8,128)(2,1)S(1)}, u32[]{:S(2)}, u32[]{:S(2)}) collective-permute-start(bf16[512,256]{1,0:T(8,128)(2,1)S(1)} %collective-permute-done.16.refs_2_), channel_id=1, source_target_pairs={{0,8},{8,16},{16,24},{24,28},{28,20},{20,12},{12,4},{4,0},{1,9},{9... | collective-permute-start | bytes 786440 | tf_op jit(solution)/shard_map/ppermute | solution.py:359
  13.9 2.0 %collective-permute-start.1 = (bf16[2080,256]{1,0:T(8,128)(2,1)S(1)}, bf16[2080,256]{1,0:T(8,128)(2,1)S(1)}, u32[]{:S(2)}, u32[]{:S(2)}) collective-permute-start(bf16[2080,256]{1,0:T(8,128)(2,1)S(1)} %join.1.refs_0_), channel_id=1, source_target_pairs={{0,2},{1,3},{2,0},{3,1},{4,6},{5,7},{6,4},{7,5},{8,10},{9,11},{10,... | collective-permute-start | bytes 3194888 | tf_op jit(solution)/shard_map/ppermute | solution.py:348
  15.9 3.5 %collective-permute-done.3.refs_3_ = bf16[512,256]{1,0:T(8,128)(2,1)S(1)} collective-permute-done((bf16[512,256]{1,0:T(8,128)(2,1)S(1)}, bf16[512,256]{1,0:T(8,128)(2,1)S(1)}, u32[]{:S(2)}, u32[]{:S(2)}) %collective-permute-start.3) | collective-permute-done | bytes 262176 | tf_op jit(solution)/shard_map/ppermute | solution.py:359
  19.4 2.0 %collective-permute-start.4 = (bf16[512,256]{1,0:T(8,128)(2,1)S(1)}, bf16[512,256]{1,0:T(8,128)(2,1)S(1)}, u32[]{:S(2)}, u32[]{:S(2)}) collective-permute-start(bf16[512,256]{1,0:T(8,128)(2,1)S(1)} %collective-permute-done.2.refs_2_), channel_id=1, source_target_pairs={{0,8},{8,16},{16,24},{24,28},{28,20},{20,12},{12,4},{4,0},{1,9},{9... | collective-permute-start | bytes 786440 | tf_op jit(solution)/shard_map/ppermute | solution.py:359
  21.5 1.5 %collective-permute-done.17.refs_4_ = bf16[512,256]{1,0:T(8,128)(2,1)S(1)} collective-permute-done((bf16[512,256]{1,0:T(8,128)(2,1)S(1)}, bf16[512,256]{1,0:T(8,128)(2,1)S(1)}, u32[]{:S(2)}, u32[]{:S(2)}) %collective-permute-start.17) | collective-permute-done | bytes 262176 | tf_op jit(solution)/shard_map/ppermute | solution.py:359
  23.0 2.0 %collective-permute-start.18 = (bf16[512,256]{1,0:T(8,128)(2,1)S(1)}, bf16[512,256]{1,0:T(8,128)(2,1)S(1)}, u32[]{:S(2)}, u32[]{:S(2)}) collective-permute-start(bf16[512,256]{1,0:T(8,128)(2,1)S(1)} %collective-permute-done.17.refs_4_), channel_id=1, source_target_pairs={{0,8},{8,16},{16,24},{24,28},{28,20},{20,12},{12,4},{4,0},{1,9},{9... | collective-permute-start | bytes 786440 | tf_op jit(solution)/shard_map/ppermute | solution.py:359
  25.1 5.6 %collective-permute-done.5.refs_5_ = bf16[512,256]{1,0:T(8,128)(2,1)S(1)} collective-permute-done((bf16[512,256]{1,0:T(8,128)(2,1)S(1)}, bf16[512,256]{1,0:T(8,128)(2,1)S(1)}, u32[]{:S(2)}, u32[]{:S(2)}) %collective-permute-start.5) | collective-permute-done | bytes 262176 | tf_op jit(solution)/shard_map/ppermute | solution.py:359
  30.7 2.0 %collective-permute-start.6 = (bf16[512,256]{1,0:T(8,128)(2,1)S(1)}, bf16[512,256]{1,0:T(8,128)(2,1)S(1)}, u32[]{:S(2)}, u32[]{:S(2)}) collective-permute-start(bf16[512,256]{1,0:T(8,128)(2,1)S(1)} %collective-permute-done.4.refs_4_), channel_id=1, source_target_pairs={{0,8},{8,16},{16,24},{24,28},{28,20},{20,12},{12,4},{4,0},{1,9},{9... | collective-permute-start | bytes 786440 | tf_op jit(solution)/shard_map/ppermute | solution.py:359
  32.7 1.6 %collective-permute-done.18.refs_6_ = bf16[512,256]{1,0:T(8,128)(2,1)S(1)} collective-permute-done((bf16[512,256]{1,0:T(8,128)(2,1)S(1)}, bf16[512,256]{1,0:T(8,128)(2,1)S(1)}, u32[]{:S(2)}, u32[]{:S(2)}) %collective-permute-start.18) | collective-permute-done | bytes 262176 | tf_op jit(solution)/shard_map/ppermute | solution.py:359
  34.3 2.0 %collective-permute-start.19 = (bf16[512,256]{1,0:T(8,128)(2,1)S(1)}, bf16[512,256]{1,0:T(8,128)(2,1)S(1)}, u32[]{:S(2)}, u32[]{:S(2)}) collective-permute-start(bf16[512,256]{1,0:T(8,128)(2,1)S(1)} %collective-permute-done.18.refs_6_), channel_id=1, source_target_pairs={{0,8},{8,16},{16,24},{24,28},{28,20},{20,12},{12,4},{4,0},{1,9},{9... | collective-permute-start | bytes 786440 | tf_op jit(solution)/shard_map/ppermute | solution.py:359
  36.3 5.6 %collective-permute-done.7.refs_7_ = bf16[512,256]{1,0:T(8,128)(2,1)S(1)} collective-permute-done((bf16[512,256]{1,0:T(8,128)(2,1)S(1)}, bf16[512,256]{1,0:T(8,128)(2,1)S(1)}, u32[]{:S(2)}, u32[]{:S(2)}) %collective-permute-start.7) | collective-permute-done | bytes 262176 | tf_op jit(solution)/shard_map/ppermute | solution.py:359
  41.9 2.0 %collective-permute-start.8 = (bf16[512,256]{1,0:T(8,128)(2,1)S(1)}, bf16[512,256]{1,0:T(8,128)(2,1)S(1)}, u32[]{:S(2)}, u32[]{:S(2)}) collective-permute-start(bf16[512,256]{1,0:T(8,128)(2,1)S(1)} %collective-permute-done.6.refs_6_), channel_id=1, source_target_pairs={{0,8},{8,16},{16,24},{24,28},{28,20},{20,12},{12,4},{4,0},{1,9},{9... | collective-permute-start | bytes 786440 | tf_op jit(solution)/shard_map/ppermute | solution.py:359
  43.9 1.6 %collective-permute-done.19.refs_8_ = bf16[512,256]{1,0:T(8,128)(2,1)S(1)} collective-permute-done((bf16[512,256]{1,0:T(8,128)(2,1)S(1)}, bf16[512,256]{1,0:T(8,128)(2,1)S(1)}, u32[]{:S(2)}, u32[]{:S(2)}) %collective-permute-start.19) | collective-permute-done | bytes 262176 | tf_op jit(solution)/shard_map/ppermute | solution.py:359
  45.5 2.0 %collective-permute-start.20 = (bf16[512,256]{1,0:T(8,128)(2,1)S(1)}, bf16[512,256]{1,0:T(8,128)(2,1)S(1)}, u32[]{:S(2)}, u32[]{:S(2)}) collective-permute-start(bf16[512,256]{1,0:T(8,128)(2,1)S(1)} %collective-permute-done.19.refs_8_), channel_id=1, source_target_pairs={{0,8},{8,16},{16,24},{24,28},{28,20},{20,12},{12,4},{4,0},{1,9},{9... | collective-permute-start | bytes 786440 | tf_op jit(solution)/shard_map/ppermute | solution.py:359
  47.6 5.6 %collective-permute-done.9.refs_9_ = bf16[512,256]{1,0:T(8,128)(2,1)S(1)} collective-permute-done((bf16[512,256]{1,0:T(8,128)(2,1)S(1)}, bf16[512,256]{1,0:T(8,128)(2,1)S(1)}, u32[]{:S(2)}, u32[]{:S(2)}) %collective-permute-start.9) | collective-permute-done | bytes 262176 | tf_op jit(solution)/shard_map/ppermute | solution.py:359
  53.2 2.0 %collective-permute-start.10 = (bf16[512,256]{1,0:T(8,128)(2,1)S(1)}, bf16[512,256]{1,0:T(8,128)(2,1)S(1)}, u32[]{:S(2)}, u32[]{:S(2)}) collective-permute-start(bf16[512,256]{1,0:T(8,128)(2,1)S(1)} %collective-permute-done.8.refs_8_), channel_id=1, source_target_pairs={{0,8},{8,16},{16,24},{24,28},{28,20},{20,12},{12,4},{4,0},{1,9},{9... | collective-permute-start | bytes 786440 | tf_op jit(solution)/shard_map/ppermute | solution.py:359
  55.2 1.6 %collective-permute-done.20.refs_0_ = bf16[512,256]{1,0:T(8,128)(2,1)S(1)} collective-permute-done((bf16[512,256]{1,0:T(8,128)(2,1)S(1)}, bf16[512,256]{1,0:T(8,128)(2,1)S(1)}, u32[]{:S(2)}, u32[]{:S(2)}) %collective-permute-start.20) | collective-permute-done | bytes 262176 | tf_op jit(solution)/shard_map/ppermute | solution.py:359
  56.8 2.0 %collective-permute-start.26 = (bf16[512,256]{1,0:T(8,128)(2,1)S(1)}, bf16[512,256]{1,0:T(8,128)(2,1)S(1)}, u32[]{:S(2)}, u32[]{:S(2)}) collective-permute-start(bf16[512,256]{1,0:T(8,128)(2,1)S(1)} %collective-permute-done.20.refs_0_), channel_id=1, source_target_pairs={{0,8},{8,16},{16,24},{24,28},{28,20},{20,12},{12,4},{4,0},{1,9},{9... | collective-permute-start | bytes 786440 | tf_op jit(solution)/shard_map/ppermute | solution.py:359
  59.5 4.9 %collective-permute-done.13.refs_1_ = bf16[512,256]{1,0:T(8,128)(2,1)S(1)} collective-permute-done((bf16[512,256]{1,0:T(8,128)(2,1)S(1)}, bf16[512,256]{1,0:T(8,128)(2,1)S(1)}, u32[]{:S(2)}, u32[]{:S(2)}) %collective-permute-start.13) | collective-permute-done | bytes 262176 | tf_op jit(solution)/shard_map/ppermute | solution.py:359
  64.4 2.0 %collective-permute-start.11 = (bf16[512,256]{1,0:T(8,128)(2,1)S(1)}, bf16[512,256]{1,0:T(8,128)(2,1)S(1)}, u32[]{:S(2)}, u32[]{:S(2)}) collective-permute-start(bf16[512,256]{1,0:T(8,128)(2,1)S(1)} %collective-permute-done.10.refs_0_), channel_id=1, source_target_pairs={{0,8},{8,16},{16,24},{24,28},{28,20},{20,12},{12,4},{4,0},{1,9},{9... | collective-permute-start | bytes 786440 | tf_op jit(solution)/shard_map/ppermute | solution.py:359
  66.4 2.6 %fold.7.refs_4_ = f32[512,1536]{1,0:T(8,128)S(1)} custom-call(s32[2,8]{1,0:T(2,128)S(4)} %get-tuple-element.25.codes_ref, bf16[2,8,256,256]{3,2,1,0:T(8,128)(2,1)S(1)} %get-tuple-element.26.ints_ref, bf16[512,256]{1,0:T(8,128)(2,1)S(1)} %get-tuple-element.34.refs_0_, ...), custom_call_target="tpu_custom_call", output_to_operand_aliasing={{}: (12, {})} | custom-call | flops 1342177280 | bytes 3145728 | tf_op jit(solution)/shard_map/fold/pallas_call | solution.py:313
  70.0 1.6 %collective-permute-start.28 = (bf16[512,256]{1,0:T(8,128)(2,1)S(1)}, bf16[512,256]{1,0:T(8,128)(2,1)S(1)}, u32[]{:S(2)}, u32[]{:S(2)}) collective-permute-start(bf16[512,256]{1,0:T(8,128)(2,1)S(1)} %collective-permute-done.26.refs_2_), channel_id=1, source_target_pairs={{0,8},{8,16},{16,24},{24,28},{28,20},{20,12},{12,4},{4,0},{1,9},{9... | collective-permute-start | bytes 786440 | tf_op jit(solution)/shard_map/ppermute | solution.py:359
  72.0 2.6 %fold.6.refs_4_ = f32[512,1536]{1,0:T(8,128)S(1)} custom-call(s32[2,8]{1,0:T(2,128)S(4)} %get-tuple-element.25.codes_ref, bf16[2,8,256,256]{3,2,1,0:T(8,128)(2,1)S(1)} %get-tuple-element.26.ints_ref, bf16[512,256]{1,0:T(8,128)(2,1)S(1)} %get-tuple-element.27.refs_0_, ...), custom_call_target="tpu_custom_call", output_to_operand_aliasing={{}: (12, {})} | custom-call | flops 1342177280 | bytes 3145728 | tf_op jit(solution)/shard_map/fold/pallas_call | solution.py:313
  75.6 2.0 %collective-permute-start.12 = (bf16[512,256]{1,0:T(8,128)(2,1)S(1)}, bf16[512,256]{1,0:T(8,128)(2,1)S(1)}, u32[]{:S(2)}, u32[]{:S(2)}) collective-permute-start(bf16[512,256]{1,0:T(8,128)(2,1)S(1)} %collective-permute-done.11.refs_2_), channel_id=1, source_target_pairs={{0,8},{8,16},{16,24},{24,28},{28,20},{20,12},{12,4},{4,0},{1,9},{9... | collective-permute-start | bytes 786440 | tf_op jit(solution)/shard_map/ppermute | solution.py:359
  77.6 1.7 %fold.8 = (f32[512,1536]{1,0:T(8,128)S(1)}, f32[1024,1536]{1,0:T(8,128)}) custom-call(s32[2,8]{1,0:T(2,128)S(4)} %get-tuple-element.25.codes_ref, bf16[2,8,256,256]{3,2,1,0:T(8,128)(2,1)S(1)} %get-tuple-element.26.ints_ref, bf16[512,256]{1,0:T(8,128)(2,1)S(1)} %collective-permute-done.20.refs_0_, ...), custom_call_target="tpu_custom_call", output_to_operand_aliasing={{0}: (6, {})} | custom-call | flops 536870912 | bytes 3145728 | tf_op jit(solution)/shard_map/fold/pallas_call | solution.py:313
  79.4 2.1 %fold.9 = (f32[512,1536]{1,0:T(8,128)S(1)}, f32[1024,1536]{1,0:T(8,128)}) custom-call(s32[2,8]{1,0:T(2,128)S(4)} %get-tuple-element.25.codes_ref, bf16[2,8,256,256]{3,2,1,0:T(8,128)(2,1)S(1)} %get-tuple-element.26.ints_ref, bf16[512,256]{1,0:T(8,128)(2,1)S(1)} %collective-permute-done.10.refs_0_, ...), custom_call_target="tpu_custom_call", output_to_operand_aliasing={{0}: (6, {}), {1}: (7, {})} | custom-call | flops 536870912 | bytes 3145728 | tf_op jit(solution)/shard_map/fold/pallas_call | solution.py:313
  81.5 1.1 %fold.10.refs_3_ = f32[1024,1536]{1,0:T(8,128)} custom-call(s32[2,8]{1,0:T(2,128)S(4)} %get-tuple-element.25.codes_ref, bf16[2,8,256,256]{3,2,1,0:T(8,128)(2,1)S(1)} %get-tuple-element.26.ints_ref, bf16[512,256]{1,0:T(8,128)(2,1)S(1)} %collective-permute-done.28.refs_0_, ...), custom_call_target="tpu_custom_call", output_to_operand_aliasing={{}: (5, {})} | custom-call | flops 268435456 | bytes 3145728 | tf_op jit(solution)/shard_map/fold/pallas_call | solution.py:313
  82.6 3.4 %collective-permute-done.15.refs_1_ = bf16[512,256]{1,0:T(8,128)(2,1)S(1)} collective-permute-done((bf16[512,256]{1,0:T(8,128)(2,1)S(1)}, bf16[512,256]{1,0:T(8,128)(2,1)S(1)}, u32[]{:S(2)}, u32[]{:S(2)}) %collective-permute-start.15) | collective-permute-done | bytes 262176 | tf_op jit(solution)/shard_map/ppermute | solution.py:359
  (37 shorter events, 5.0 us)
Async XLA Ops:
  1.5 12.3 %collective-permute-start = (bf16[1040,256]{1,0:T(8,128)(2,1)S(1)}, bf16[1040,256]{1,0:T(8,128)(2,1)S(1)}, u32[]{:S(2)}, u32[]{:S(2)}) collective-permute-start(bf16[1040,256]{1,0:T(8,128)(2,1)S(1)} %get-tuple-element.24.refs_0_), channel_id=1, source_target_pairs={{0,1},{1,0},{2,3},{3,2},{4,5},{5,4},{6,7},{7,6},{8,9},{9,8},{10,11... | collective-permute-start | bytes 1597448 | tf_op jit(solution)/shard_map/ppermute | solution.py:345
  2.0 9.7 %collective-permute-start.16 = (bf16[512,256]{1,0:T(8,128)(2,1)S(1)}, bf16[512,256]{1,0:T(8,128)(2,1)S(1)}, u32[]{:S(2)}, u32[]{:S(2)}) collective-permute-start(bf16[512,256]{1,0:T(8,128)(2,1)S(1)} %get-tuple-element.34.refs_0_), channel_id=1, source_target_pairs={{0,8},{8,16},{16,24},{24,28},{28,20},{20,12},{12,4},{4,0},{1,9},{9... | collective-permute-start | bytes 786440 | tf_op jit(solution)/shard_map/ppermute | solution.py:359
  4.7 9.1 %collective-permute-start.21 = (bf16[512,256]{1,0:T(8,128)(2,1)S(1)}, bf16[512,256]{1,0:T(8,128)(2,1)S(1)}, u32[]{:S(2)}, u32[]{:S(2)}) collective-permute-start(bf16[512,256]{1,0:T(8,128)(2,1)S(1)} %get-tuple-element.35.refs_1_), channel_id=1, source_target_pairs={{8,0},{16,8},{24,16},{28,24},{20,28},{12,20},{4,12},{0,4},{9,1},{1... | collective-permute-start | bytes 786440 | tf_op jit(solution)/shard_map/ppermute | solution.py:359
  4.7 14.8 %collective-permute-start.3 = (bf16[512,256]{1,0:T(8,128)(2,1)S(1)}, bf16[512,256]{1,0:T(8,128)(2,1)S(1)}, u32[]{:S(2)}, u32[]{:S(2)}) collective-permute-start(bf16[512,256]{1,0:T(8,128)(2,1)S(1)} %get-tuple-element.28.refs_1_), channel_id=1, source_target_pairs={{8,0},{16,8},{24,16},{28,24},{20,28},{12,20},{4,12},{0,4},{9,1},{1... | collective-permute-start | bytes 786440 | tf_op jit(solution)/shard_map/ppermute | solution.py:359
  6.6 12.8 %collective-permute-start.2 = (bf16[512,256]{1,0:T(8,128)(2,1)S(1)}, bf16[512,256]{1,0:T(8,128)(2,1)S(1)}, u32[]{:S(2)}, u32[]{:S(2)}) collective-permute-start(bf16[512,256]{1,0:T(8,128)(2,1)S(1)} %get-tuple-element.27.refs_0_), channel_id=1, source_target_pairs={{0,8},{8,16},{16,24},{24,28},{28,20},{20,12},{12,4},{4,0},{1,9},{9... | collective-permute-start | bytes 786440 | tf_op jit(solution)/shard_map/ppermute | solution.py:359
  11.8 11.2 %collective-permute-start.17 = (bf16[512,256]{1,0:T(8,128)(2,1)S(1)}, bf16[512,256]{1,0:T(8,128)(2,1)S(1)}, u32[]{:S(2)}, u32[]{:S(2)}) collective-permute-start(bf16[512,256]{1,0:T(8,128)(2,1)S(1)} %collective-permute-done.16.refs_2_), channel_id=1, source_target_pairs={{0,8},{8,16},{16,24},{24,28},{28,20},{20,12},{12,4},{4,0},{1,9},{9... | collective-permute-start | bytes 786440 | tf_op jit(solution)/shard_map/ppermute | solution.py:359
  13.8 11.2 %collective-permute-start.22 = (bf16[512,256]{1,0:T(8,128)(2,1)S(1)}, bf16[512,256]{1,0:T(8,128)(2,1)S(1)}, u32[]{:S(2)}, u32[]{:S(2)}) collective-permute-start(bf16[512,256]{1,0:T(8,128)(2,1)S(1)} %collective-permute-done.21.refs_3_), channel_id=1, source_target_pairs={{8,0},{16,8},{24,16},{28,24},{20,28},{12,20},{4,12},{0,4},{9,1},{1... | collective-permute-start | bytes 786440 | tf_op jit(solution)/shard_map/ppermute | solution.py:359
  13.9 44.9 %collective-permute-start.1 = (bf16[2080,256]{1,0:T(8,128)(2,1)S(1)}, bf16[2080,256]{1,0:T(8,128)(2,1)S(1)}, u32[]{:S(2)}, u32[]{:S(2)}) collective-permute-start(bf16[2080,256]{1,0:T(8,128)(2,1)S(1)} %join.1.refs_0_), channel_id=1, source_target_pairs={{0,2},{1,3},{2,0},{3,1},{4,6},{5,7},{6,4},{7,5},{8,10},{9,11},{10,... | collective-permute-start | bytes 3194888 | tf_op jit(solution)/shard_map/ppermute | solution.py:348
  19.4 11.2 %collective-permute-start.5 = (bf16[512,256]{1,0:T(8,128)(2,1)S(1)}, bf16[512,256]{1,0:T(8,128)(2,1)S(1)}, u32[]{:S(2)}, u32[]{:S(2)}) collective-permute-start(bf16[512,256]{1,0:T(8,128)(2,1)S(1)} %collective-permute-done.3.refs_3_), channel_id=1, source_target_pairs={{8,0},{16,8},{24,16},{28,24},{20,28},{12,20},{4,12},{0,4},{9,1},{1... | collective-permute-start | bytes 786440 | tf_op jit(solution)/shard_map/ppermute | solution.py:359
  19.4 11.2 %collective-permute-start.4 = (bf16[512,256]{1,0:T(8,128)(2,1)S(1)}, bf16[512,256]{1,0:T(8,128)(2,1)S(1)}, u32[]{:S(2)}, u32[]{:S(2)}) collective-permute-start(bf16[512,256]{1,0:T(8,128)(2,1)S(1)} %collective-permute-done.2.refs_2_), channel_id=1, source_target_pairs={{0,8},{8,16},{16,24},{24,28},{28,20},{20,12},{12,4},{4,0},{1,9},{9... | collective-permute-start | bytes 786440 | tf_op jit(solution)/shard_map/ppermute | solution.py:359
  23.0 11.3 %collective-permute-start.18 = (bf16[512,256]{1,0:T(8,128)(2,1)S(1)}, bf16[512,256]{1,0:T(8,128)(2,1)S(1)}, u32[]{:S(2)}, u32[]{:S(2)}) collective-permute-start(bf16[512,256]{1,0:T(8,128)(2,1)S(1)} %collective-permute-done.17.refs_4_), channel_id=1, source_target_pairs={{0,8},{8,16},{16,24},{24,28},{28,20},{20,12},{12,4},{4,0},{1,9},{9... | collective-permute-start | bytes 786440 | tf_op jit(solution)/shard_map/ppermute | solution.py:359
  25.1 11.3 %collective-permute-start.23 = (bf16[512,256]{1,0:T(8,128)(2,1)S(1)}, bf16[512,256]{1,0:T(8,128)(2,1)S(1)}, u32[]{:S(2)}, u32[]{:S(2)}) collective-permute-start(bf16[512,256]{1,0:T(8,128)(2,1)S(1)} %collective-permute-done.22.refs_5_), channel_id=1, source_target_pairs={{8,0},{16,8},{24,16},{28,24},{20,28},{12,20},{4,12},{0,4},{9,1},{1... | collective-permute-start | bytes 786440 | tf_op jit(solution)/shard_map/ppermute | solution.py:359
  30.7 11.2 %collective-permute-start.7 = (bf16[512,256]{1,0:T(8,128)(2,1)S(1)}, bf16[512,256]{1,0:T(8,128)(2,1)S(1)}, u32[]{:S(2)}, u32[]{:S(2)}) collective-permute-start(bf16[512,256]{1,0:T(8,128)(2,1)S(1)} %collective-permute-done.5.refs_5_), channel_id=1, source_target_pairs={{8,0},{16,8},{24,16},{28,24},{20,28},{12,20},{4,12},{0,4},{9,1},{1... | collective-permute-start | bytes 786440 | tf_op jit(solution)/shard_map/ppermute | solution.py:359
  30.7 11.2 %collective-permute-start.6 = (bf16[512,256]{1,0:T(8,128)(2,1)S(1)}, bf16[512,256]{1,0:T(8,128)(2,1)S(1)}, u32[]{:S(2)}, u32[]{:S(2)}) collective-permute-start(bf16[512,256]{1,0:T(8,128)(2,1)S(1)} %collective-permute-done.4.refs_4_), channel_id=1, source_target_pairs={{0,8},{8,16},{16,24},{24,28},{28,20},{20,12},{12,4},{4,0},{1,9},{9... | collective-permute-start | bytes 786440 | tf_op jit(solution)/shard_map/ppermute | solution.py:359
  34.3 11.2 %collective-permute-start.19 = (bf16[512,256]{1,0:T(8,128)(2,1)S(1)}, bf16[512,256]{1,0:T(8,128)(2,1)S(1)}, u32[]{:S(2)}, u32[]{:S(2)}) collective-permute-start(bf16[512,256]{1,0:T(8,128)(2,1)S(1)} %collective-permute-done.18.refs_6_), channel_id=1, source_target_pairs={{0,8},{8,16},{16,24},{24,28},{28,20},{20,12},{12,4},{4,0},{1,9},{9... | collective-permute-start | bytes 786440 | tf_op jit(solution)/shard_map/ppermute | solution.py:359
  36.3 11.2 %collective-permute-start.24 = (bf16[512,256]{1,0:T(8,128)(2,1)S(1)}, bf16[512,256]{1,0:T(8,128)(2,1)S(1)}, u32[]{:S(2)}, u32[]{:S(2)}) collective-permute-start(bf16[512,256]{1,0:T(8,128)(2,1)S(1)} %collective-permute-done.23.refs_7_), channel_id=1, source_target_pairs={{8,0},{16,8},{24,16},{28,24},{20,28},{12,20},{4,12},{0,4},{9,1},{1... | collective-permute-start | bytes 786440 | tf_op jit(solution)/shard_map/ppermute | solution.py:359
  41.9 11.2 %collective-permute-start.9 = (bf16[512,256]{1,0:T(8,128)(2,1)S(1)}, bf16[512,256]{1,0:T(8,128)(2,1)S(1)}, u32[]{:S(2)}, u32[]{:S(2)}) collective-permute-start(bf16[512,256]{1,0:T(8,128)(2,1)S(1)} %collective-permute-done.7.refs_7_), channel_id=1, source_target_pairs={{8,0},{16,8},{24,16},{28,24},{20,28},{12,20},{4,12},{0,4},{9,1},{1... | collective-permute-start | bytes 786440 | tf_op jit(solution)/shard_map/ppermute | solution.py:359
  41.9 11.2 %collective-permute-start.8 = (bf16[512,256]{1,0:T(8,128)(2,1)S(1)}, bf16[512,256]{1,0:T(8,128)(2,1)S(1)}, u32[]{:S(2)}, u32[]{:S(2)}) collective-permute-start(bf16[512,256]{1,0:T(8,128)(2,1)S(1)} %collective-permute-done.6.refs_6_), channel_id=1, source_target_pairs={{0,8},{8,16},{16,24},{24,28},{28,20},{20,12},{12,4},{4,0},{1,9},{9... | collective-permute-start | bytes 786440 | tf_op jit(solution)/shard_map/ppermute | solution.py:359
  45.5 11.2 %collective-permute-start.20 = (bf16[512,256]{1,0:T(8,128)(2,1)S(1)}, bf16[512,256]{1,0:T(8,128)(2,1)S(1)}, u32[]{:S(2)}, u32[]{:S(2)}) collective-permute-start(bf16[512,256]{1,0:T(8,128)(2,1)S(1)} %collective-permute-done.19.refs_8_), channel_id=1, source_target_pairs={{0,8},{8,16},{16,24},{24,28},{28,20},{20,12},{12,4},{4,0},{1,9},{9... | collective-permute-start | bytes 786440 | tf_op jit(solution)/shard_map/ppermute | solution.py:359
  47.6 11.2 %collective-permute-start.25 = (bf16[512,256]{1,0:T(8,128)(2,1)S(1)}, bf16[512,256]{1,0:T(8,128)(2,1)S(1)}, u32[]{:S(2)}, u32[]{:S(2)}) collective-permute-start(bf16[512,256]{1,0:T(8,128)(2,1)S(1)} %collective-permute-done.24.refs_9_), channel_id=1, source_target_pairs={{8,0},{16,8},{24,16},{28,24},{20,28},{12,20},{4,12},{0,4},{9,1},{1... | collective-permute-start | bytes 786440 | tf_op jit(solution)/shard_map/ppermute | solution.py:359
  53.1 11.2 %collective-permute-start.13 = (bf16[512,256]{1,0:T(8,128)(2,1)S(1)}, bf16[512,256]{1,0:T(8,128)(2,1)S(1)}, u32[]{:S(2)}, u32[]{:S(2)}) collective-permute-start(bf16[512,256]{1,0:T(8,128)(2,1)S(1)} %collective-permute-done.9.refs_9_), channel_id=1, source_target_pairs={{8,0},{16,8},{24,16},{28,24},{20,28},{12,20},{4,12},{0,4},{9,1},{1... | collective-permute-start | bytes 786440 | tf_op jit(solution)/shard_map/ppermute | solution.py:359
  53.2 11.2 %collective-permute-start.10 = (bf16[512,256]{1,0:T(8,128)(2,1)S(1)}, bf16[512,256]{1,0:T(8,128)(2,1)S(1)}, u32[]{:S(2)}, u32[]{:S(2)}) collective-permute-start(bf16[512,256]{1,0:T(8,128)(2,1)S(1)} %collective-permute-done.8.refs_8_), channel_id=1, source_target_pairs={{0,8},{8,16},{16,24},{24,28},{28,20},{20,12},{12,4},{4,0},{1,9},{9... | collective-permute-start | bytes 786440 | tf_op jit(solution)/shard_map/ppermute | solution.py:359
  56.8 12.2 %collective-permute-start.26 = (bf16[512,256]{1,0:T(8,128)(2,1)S(1)}, bf16[512,256]{1,0:T(8,128)(2,1)S(1)}, u32[]{:S(2)}, u32[]{:S(2)}) collective-permute-start(bf16[512,256]{1,0:T(8,128)(2,1)S(1)} %collective-permute-done.20.refs_0_), channel_id=1, source_target_pairs={{0,8},{8,16},{16,24},{24,28},{28,20},{20,12},{12,4},{4,0},{1,9},{9... | collective-permute-start | bytes 786440 | tf_op jit(solution)/shard_map/ppermute | solution.py:359
  58.8 11.2 %collective-permute-start.27 = (bf16[512,256]{1,0:T(8,128)(2,1)S(1)}, bf16[512,256]{1,0:T(8,128)(2,1)S(1)}, u32[]{:S(2)}, u32[]{:S(2)}) collective-permute-start(bf16[512,256]{1,0:T(8,128)(2,1)S(1)} %collective-permute-done.25.refs_1_), channel_id=1, source_target_pairs={{8,0},{16,8},{24,16},{28,24},{20,28},{12,20},{4,12},{0,4},{9,1},{1... | collective-permute-start | bytes 786440 | tf_op jit(solution)/shard_map/ppermute | solution.py:359
  64.4 11.2 %collective-permute-start.14 = (bf16[512,256]{1,0:T(8,128)(2,1)S(1)}, bf16[512,256]{1,0:T(8,128)(2,1)S(1)}, u32[]{:S(2)}, u32[]{:S(2)}) collective-permute-start(bf16[512,256]{1,0:T(8,128)(2,1)S(1)} %collective-permute-done.13.refs_1_), channel_id=1, source_target_pairs={{8,0},{16,8},{24,16},{28,24},{20,28},{12,20},{4,12},{0,4},{9,1},{1... | collective-permute-start | bytes 786440 | tf_op jit(solution)/shard_map/ppermute | solution.py:359
  64.4 11.2 %collective-permute-start.11 = (bf16[512,256]{1,0:T(8,128)(2,1)S(1)}, bf16[512,256]{1,0:T(8,128)(2,1)S(1)}, u32[]{:S(2)}, u32[]{:S(2)}) collective-permute-start(bf16[512,256]{1,0:T(8,128)(2,1)S(1)} %collective-permute-done.10.refs_0_), channel_id=1, source_target_pairs={{0,8},{8,16},{16,24},{24,28},{28,20},{20,12},{12,4},{4,0},{1,9},{9... | collective-permute-start | bytes 786440 | tf_op jit(solution)/shard_map/ppermute | solution.py:359
  70.0 11.5 %collective-permute-start.28 = (bf16[512,256]{1,0:T(8,128)(2,1)S(1)}, bf16[512,256]{1,0:T(8,128)(2,1)S(1)}, u32[]{:S(2)}, u32[]{:S(2)}) collective-permute-start(bf16[512,256]{1,0:T(8,128)(2,1)S(1)} %collective-permute-done.26.refs_2_), channel_id=1, source_target_pairs={{0,8},{8,16},{16,24},{24,28},{28,20},{20,12},{12,4},{4,0},{1,9},{9... | collective-permute-start | bytes 786440 | tf_op jit(solution)/shard_map/ppermute | solution.py:359
  71.6 9.9 %collective-permute-start.29 = (bf16[512,256]{1,0:T(8,128)(2,1)S(1)}, bf16[512,256]{1,0:T(8,128)(2,1)S(1)}, u32[]{:S(2)}, u32[]{:S(2)}) collective-permute-start(bf16[512,256]{1,0:T(8,128)(2,1)S(1)} %collective-permute-done.27.refs_3_), channel_id=1, source_target_pairs={{8,0},{16,8},{24,16},{28,24},{20,28},{12,20},{4,12},{0,4},{9,1},{1... | collective-permute-start | bytes 786440 | tf_op jit(solution)/shard_map/ppermute | solution.py:359
  75.6 10.5 %collective-permute-start.15 = (bf16[512,256]{1,0:T(8,128)(2,1)S(1)}, bf16[512,256]{1,0:T(8,128)(2,1)S(1)}, u32[]{:S(2)}, u32[]{:S(2)}) collective-permute-start(bf16[512,256]{1,0:T(8,128)(2,1)S(1)} %collective-permute-done.14.refs_3_), channel_id=1, source_target_pairs={{8,0},{16,8},{24,16},{28,24},{20,28},{12,20},{4,12},{0,4},{9,1},{1... | collective-permute-start | bytes 786440 | tf_op jit(solution)/shard_map/ppermute | solution.py:359
  75.6 10.5 %collective-permute-start.12 = (bf16[512,256]{1,0:T(8,128)(2,1)S(1)}, bf16[512,256]{1,0:T(8,128)(2,1)S(1)}, u32[]{:S(2)}, u32[]{:S(2)}) collective-permute-start(bf16[512,256]{1,0:T(8,128)(2,1)S(1)} %collective-permute-done.11.refs_2_), channel_id=1, source_target_pairs={{0,8},{8,16},{16,24},{24,28},{28,20},{20,12},{12,4},{4,0},{1,9},{9... | collective-permute-start | bytes 786440 | tf_op jit(solution)/shard_map/ppermute | solution.py:359

commit v4 on v3

--- a/solution.py
+++ b/solution.py
@@ -332,7 +332,7 @@
     rows_held = n_row // n_col
     panels, slots, width = int_tiles.shape[0], int_tiles.shape[1], int_tiles.shape[3]
     across = n_col // CORES
-    order = grid_cycle(n_row // across, across)
+    order = grid_cycle(n_row // across, across)[::-1]
     forth = [(order[at], order[(at + 1) % n_row]) for at in range(n_row)]
     ways = [forth if panel % 2 == 0 else [(b, a) for a, b in forth] for panel in range(panels)]
 

time: 87.4 us -> 87.5 us (level)
  transfers between devices with their start and end apart: 30 -> 30, of which waited for: 13 -> 14; matrix products, arithmetic and copies ran while one was open for 0% -> 0% of each run, Pallas kernels for 12% -> 13%
where the time goes in v4:
time: 87.5 us; the launch traced here: 87.6 us
  waiting for transfers between devices  41.8 us (48%)
  starting transfers between devices  31.6 us (36%)
  Pallas kernels  14.1 us (16%)
    ppermute x28, waiting for transfers between devices, body(): lax.ppermute(held[panel], 'row', ways[panel])  41.8 us
    ppermute x28, starting transfers between devices, body(): lax.ppermute(held[panel], 'row', ways[panel])  29.1 us
    pallas_call x6, Pallas kernels, fold(): pl.pallas_call(functools.partial(fold_kernel, first, hops, later, order,...  11.8 us
    ppermute x1, starting transfers between devices, body(): lax.ppermute(moved, 'col', [(c, (c + shift * CORES) % n_col) for c in ran...  1.97 us
  transfers between devices with their start and end apart: 30, of which 14 were waited for; matrix products, arithmetic and copies ran while one was open for 0% of the time, Pallas kernels for 13%

profile of v4, /device:TPU:0, one launch (start us, length us, event | category | flops | bytes accessed | tf_op | source)
XLA Modules:
  0.0 87.6 jit_solution(7976793416638508990)
XLA Ops:
  0.0 1.5 %place.1 = (bf16[512,256]{1,0:T(8,128)(2,1)S(1)}, bf16[512,256]{1,0:T(8,128)(2,1)S(1)}, bf16[512,256]{1,0:T(8,128)(2,1)S(1)}, bf16[512,256]{1,0:T(8,128)(2,1)S(1)}, bf16[1040,256]{1,0:T(8,128)(2,1)S(1)}) custom-call(s32[2,1,4]{2,1,0:T(1,128)} %rows_hbm.1, s32[2,1,2]{2,1,0:T(1,128)} %bitcast.3, bf16[2,1,4,256,256]{4,3,2,1,0:T(8,128)(2,1)} %tiles_hbm.1, ...), custom_call_target="tpu_custom_call" | custom-call | tf_op jit(solution)/shard_map/place/pallas_call | solution.py:104
  2.0 2.6 %collective-permute-start.16 = (bf16[512,256]{1,0:T(8,128)(2,1)S(1)}, bf16[512,256]{1,0:T(8,128)(2,1)S(1)}, u32[]{:S(2)}, u32[]{:S(2)}) collective-permute-start(bf16[512,256]{1,0:T(8,128)(2,1)S(1)} %get-tuple-element.34.refs_0_), channel_id=1, source_target_pairs={{4,12},{12,20},{20,28},{28,24},{24,16},{16,8},{8,0},{0,4},{5,13},{... | collective-permute-start | bytes 786440 | tf_op jit(solution)/shard_map/ppermute | solution.py:359
  4.8 1.9 %collective-permute-start.3 = (bf16[512,256]{1,0:T(8,128)(2,1)S(1)}, bf16[512,256]{1,0:T(8,128)(2,1)S(1)}, u32[]{:S(2)}, u32[]{:S(2)}) collective-permute-start(bf16[512,256]{1,0:T(8,128)(2,1)S(1)} %get-tuple-element.28.refs_1_), channel_id=1, source_target_pairs={{12,4},{20,12},{28,20},{24,28},{16,24},{8,16},{0,8},{4,0},{13,5},{... | collective-permute-start | bytes 786440 | tf_op jit(solution)/shard_map/ppermute | solution.py:359
  6.8 5.0 %collective-permute-done.16.refs_2_ = bf16[512,256]{1,0:T(8,128)(2,1)S(1)} collective-permute-done((bf16[512,256]{1,0:T(8,128)(2,1)S(1)}, bf16[512,256]{1,0:T(8,128)(2,1)S(1)}, u32[]{:S(2)}, u32[]{:S(2)}) %collective-permute-start.16) | collective-permute-done | bytes 262176 | tf_op jit(solution)/shard_map/ppermute | solution.py:359
  11.8 1.9 %collective-permute-start.17 = (bf16[512,256]{1,0:T(8,128)(2,1)S(1)}, bf16[512,256]{1,0:T(8,128)(2,1)S(1)}, u32[]{:S(2)}, u32[]{:S(2)}) collective-permute-start(bf16[512,256]{1,0:T(8,128)(2,1)S(1)} %collective-permute-done.16.refs_2_), channel_id=1, source_target_pairs={{4,12},{12,20},{20,28},{28,24},{24,16},{16,8},{8,0},{0,4},{5,13},{... | collective-permute-start | bytes 786440 | tf_op jit(solution)/shard_map/ppermute | solution.py:359
  14.0 2.0 %collective-permute-start.1 = (bf16[2080,256]{1,0:T(8,128)(2,1)S(1)}, bf16[2080,256]{1,0:T(8,128)(2,1)S(1)}, u32[]{:S(2)}, u32[]{:S(2)}) collective-permute-start(bf16[2080,256]{1,0:T(8,128)(2,1)S(1)} %join.1.refs_0_), channel_id=1, source_target_pairs={{0,2},{1,3},{2,0},{3,1},{4,6},{5,7},{6,4},{7,5},{8,10},{9,11},{10,... | collective-permute-start | bytes 3194888 | tf_op jit(solution)/shard_map/ppermute | solution.py:348
  15.9 3.4 %collective-permute-done.3.refs_3_ = bf16[512,256]{1,0:T(8,128)(2,1)S(1)} collective-permute-done((bf16[512,256]{1,0:T(8,128)(2,1)S(1)}, bf16[512,256]{1,0:T(8,128)(2,1)S(1)}, u32[]{:S(2)}, u32[]{:S(2)}) %collective-permute-start.3) | collective-permute-done | bytes 262176 | tf_op jit(solution)/shard_map/ppermute | solution.py:359
  19.5 1.9 %collective-permute-start.4 = (bf16[512,256]{1,0:T(8,128)(2,1)S(1)}, bf16[512,256]{1,0:T(8,128)(2,1)S(1)}, u32[]{:S(2)}, u32[]{:S(2)}) collective-permute-start(bf16[512,256]{1,0:T(8,128)(2,1)S(1)} %collective-permute-done.2.refs_2_), channel_id=1, source_target_pairs={{4,12},{12,20},{20,28},{28,24},{24,16},{16,8},{8,0},{0,4},{5,13},{... | collective-permute-start | bytes 786440 | tf_op jit(solution)/shard_map/ppermute | solution.py:359
  21.4 1.7 %collective-permute-done.17.refs_4_ = bf16[512,256]{1,0:T(8,128)(2,1)S(1)} collective-permute-done((bf16[512,256]{1,0:T(8,128)(2,1)S(1)}, bf16[512,256]{1,0:T(8,128)(2,1)S(1)}, u32[]{:S(2)}, u32[]{:S(2)}) %collective-permute-start.17) | collective-permute-done | bytes 262176 | tf_op jit(solution)/shard_map/ppermute | solution.py:359
  23.1 1.9 %collective-permute-start.18 = (bf16[512,256]{1,0:T(8,128)(2,1)S(1)}, bf16[512,256]{1,0:T(8,128)(2,1)S(1)}, u32[]{:S(2)}, u32[]{:S(2)}) collective-permute-start(bf16[512,256]{1,0:T(8,128)(2,1)S(1)} %collective-permute-done.17.refs_4_), channel_id=1, source_target_pairs={{4,12},{12,20},{20,28},{28,24},{24,16},{16,8},{8,0},{0,4},{5,13},{... | collective-permute-start | bytes 786440 | tf_op jit(solution)/shard_map/ppermute | solution.py:359
  25.1 5.5 %collective-permute-done.5.refs_5_ = bf16[512,256]{1,0:T(8,128)(2,1)S(1)} collective-permute-done((bf16[512,256]{1,0:T(8,128)(2,1)S(1)}, bf16[512,256]{1,0:T(8,128)(2,1)S(1)}, u32[]{:S(2)}, u32[]{:S(2)}) %collective-permute-start.5) | collective-permute-done | bytes 262176 | tf_op jit(solution)/shard_map/ppermute | solution.py:359
  30.7 1.9 %collective-permute-start.6 = (bf16[512,256]{1,0:T(8,128)(2,1)S(1)}, bf16[512,256]{1,0:T(8,128)(2,1)S(1)}, u32[]{:S(2)}, u32[]{:S(2)}) collective-permute-start(bf16[512,256]{1,0:T(8,128)(2,1)S(1)} %collective-permute-done.4.refs_4_), channel_id=1, source_target_pairs={{4,12},{12,20},{20,28},{28,24},{24,16},{16,8},{8,0},{0,4},{5,13},{... | collective-permute-start | bytes 786440 | tf_op jit(solution)/shard_map/ppermute | solution.py:359
  32.6 1.7 %collective-permute-done.18.refs_6_ = bf16[512,256]{1,0:T(8,128)(2,1)S(1)} collective-permute-done((bf16[512,256]{1,0:T(8,128)(2,1)S(1)}, bf16[512,256]{1,0:T(8,128)(2,1)S(1)}, u32[]{:S(2)}, u32[]{:S(2)}) %collective-permute-start.18) | collective-permute-done | bytes 262176 | tf_op jit(solution)/shard_map/ppermute | solution.py:359
  34.3 1.9 %collective-permute-start.19 = (bf16[512,256]{1,0:T(8,128)(2,1)S(1)}, bf16[512,256]{1,0:T(8,128)(2,1)S(1)}, u32[]{:S(2)}, u32[]{:S(2)}) collective-permute-start(bf16[512,256]{1,0:T(8,128)(2,1)S(1)} %collective-permute-done.18.refs_6_), channel_id=1, source_target_pairs={{4,12},{12,20},{20,28},{28,24},{24,16},{16,8},{8,0},{0,4},{5,13},{... | collective-permute-start | bytes 786440 | tf_op jit(solution)/shard_map/ppermute | solution.py:359
  36.4 5.5 %collective-permute-done.7.refs_7_ = bf16[512,256]{1,0:T(8,128)(2,1)S(1)} collective-permute-done((bf16[512,256]{1,0:T(8,128)(2,1)S(1)}, bf16[512,256]{1,0:T(8,128)(2,1)S(1)}, u32[]{:S(2)}, u32[]{:S(2)}) %collective-permute-start.7) | collective-permute-done | bytes 262176 | tf_op jit(solution)/shard_map/ppermute | solution.py:359
  42.0 1.9 %collective-permute-start.8 = (bf16[512,256]{1,0:T(8,128)(2,1)S(1)}, bf16[512,256]{1,0:T(8,128)(2,1)S(1)}, u32[]{:S(2)}, u32[]{:S(2)}) collective-permute-start(bf16[512,256]{1,0:T(8,128)(2,1)S(1)} %collective-permute-done.6.refs_6_), channel_id=1, source_target_pairs={{4,12},{12,20},{20,28},{28,24},{24,16},{16,8},{8,0},{0,4},{5,13},{... | collective-permute-start | bytes 786440 | tf_op jit(solution)/shard_map/ppermute | solution.py:359
  43.9 1.7 %collective-permute-done.19.refs_8_ = bf16[512,256]{1,0:T(8,128)(2,1)S(1)} collective-permute-done((bf16[512,256]{1,0:T(8,128)(2,1)S(1)}, bf16[512,256]{1,0:T(8,128)(2,1)S(1)}, u32[]{:S(2)}, u32[]{:S(2)}) %collective-permute-start.19) | collective-permute-done | bytes 262176 | tf_op jit(solution)/shard_map/ppermute | solution.py:359
  45.5 1.9 %collective-permute-start.20 = (bf16[512,256]{1,0:T(8,128)(2,1)S(1)}, bf16[512,256]{1,0:T(8,128)(2,1)S(1)}, u32[]{:S(2)}, u32[]{:S(2)}) collective-permute-start(bf16[512,256]{1,0:T(8,128)(2,1)S(1)} %collective-permute-done.19.refs_8_), channel_id=1, source_target_pairs={{4,12},{12,20},{20,28},{28,24},{24,16},{16,8},{8,0},{0,4},{5,13},{... | collective-permute-start | bytes 786440 | tf_op jit(solution)/shard_map/ppermute | solution.py:359
  47.6 5.5 %collective-permute-done.9.refs_9_ = bf16[512,256]{1,0:T(8,128)(2,1)S(1)} collective-permute-done((bf16[512,256]{1,0:T(8,128)(2,1)S(1)}, bf16[512,256]{1,0:T(8,128)(2,1)S(1)}, u32[]{:S(2)}, u32[]{:S(2)}) %collective-permute-start.9) | collective-permute-done | bytes 262176 | tf_op jit(solution)/shard_map/ppermute | solution.py:359
  53.2 1.9 %collective-permute-start.10 = (bf16[512,256]{1,0:T(8,128)(2,1)S(1)}, bf16[512,256]{1,0:T(8,128)(2,1)S(1)}, u32[]{:S(2)}, u32[]{:S(2)}) collective-permute-start(bf16[512,256]{1,0:T(8,128)(2,1)S(1)} %collective-permute-done.8.refs_8_), channel_id=1, source_target_pairs={{4,12},{12,20},{20,28},{28,24},{24,16},{16,8},{8,0},{0,4},{5,13},{... | collective-permute-start | bytes 786440 | tf_op jit(solution)/shard_map/ppermute | solution.py:359
  55.1 1.7 %collective-permute-done.20.refs_0_ = bf16[512,256]{1,0:T(8,128)(2,1)S(1)} collective-permute-done((bf16[512,256]{1,0:T(8,128)(2,1)S(1)}, bf16[512,256]{1,0:T(8,128)(2,1)S(1)}, u32[]{:S(2)}, u32[]{:S(2)}) %collective-permute-start.20) | collective-permute-done | bytes 262176 | tf_op jit(solution)/shard_map/ppermute | solution.py:359
  56.8 1.9 %collective-permute-start.26 = (bf16[512,256]{1,0:T(8,128)(2,1)S(1)}, bf16[512,256]{1,0:T(8,128)(2,1)S(1)}, u32[]{:S(2)}, u32[]{:S(2)}) collective-permute-start(bf16[512,256]{1,0:T(8,128)(2,1)S(1)} %collective-permute-done.20.refs_0_), channel_id=1, source_target_pairs={{4,12},{12,20},{20,28},{28,24},{24,16},{16,8},{8,0},{0,4},{5,13},{... | collective-permute-start | bytes 786440 | tf_op jit(solution)/shard_map/ppermute | solution.py:359
  59.5 4.8 %collective-permute-done.13.refs_1_ = bf16[512,256]{1,0:T(8,128)(2,1)S(1)} collective-permute-done((bf16[512,256]{1,0:T(8,128)(2,1)S(1)}, bf16[512,256]{1,0:T(8,128)(2,1)S(1)}, u32[]{:S(2)}, u32[]{:S(2)}) %collective-permute-start.13) | collective-permute-done | bytes 262176 | tf_op jit(solution)/shard_map/ppermute | solution.py:359
  64.4 1.9 %collective-permute-start.11 = (bf16[512,256]{1,0:T(8,128)(2,1)S(1)}, bf16[512,256]{1,0:T(8,128)(2,1)S(1)}, u32[]{:S(2)}, u32[]{:S(2)}) collective-permute-start(bf16[512,256]{1,0:T(8,128)(2,1)S(1)} %collective-permute-done.10.refs_0_), channel_id=1, source_target_pairs={{4,12},{12,20},{20,28},{28,24},{24,16},{16,8},{8,0},{0,4},{5,13},{... | collective-permute-start | bytes 786440 | tf_op jit(solution)/shard_map/ppermute | solution.py:359
  66.3 3.0 %fold.7.refs_4_ = f32[512,1536]{1,0:T(8,128)S(1)} custom-call(s32[2,8]{1,0:T(2,128)S(4)} %get-tuple-element.25.codes_ref, bf16[2,8,256,256]{3,2,1,0:T(8,128)(2,1)S(1)} %get-tuple-element.26.ints_ref, bf16[512,256]{1,0:T(8,128)(2,1)S(1)} %get-tuple-element.34.refs_0_, ...), custom_call_target="tpu_custom_call", output_to_operand_aliasing={{}: (12, {})} | custom-call | flops 1342177280 | bytes 3145728 | tf_op jit(solution)/shard_map/fold/pallas_call | solution.py:313
  69.9 1.6 %collective-permute-start.28 = (bf16[512,256]{1,0:T(8,128)(2,1)S(1)}, bf16[512,256]{1,0:T(8,128)(2,1)S(1)}, u32[]{:S(2)}, u32[]{:S(2)}) collective-permute-start(bf16[512,256]{1,0:T(8,128)(2,1)S(1)} %collective-permute-done.26.refs_2_), channel_id=1, source_target_pairs={{4,12},{12,20},{20,28},{28,24},{24,16},{16,8},{8,0},{0,4},{5,13},{... | collective-permute-start | bytes 786440 | tf_op jit(solution)/shard_map/ppermute | solution.py:359
  71.9 3.0 %fold.6.refs_4_ = f32[512,1536]{1,0:T(8,128)S(1)} custom-call(s32[2,8]{1,0:T(2,128)S(4)} %get-tuple-element.25.codes_ref, bf16[2,8,256,256]{3,2,1,0:T(8,128)(2,1)S(1)} %get-tuple-element.26.ints_ref, bf16[512,256]{1,0:T(8,128)(2,1)S(1)} %get-tuple-element.27.refs_0_, ...), custom_call_target="tpu_custom_call", output_to_operand_aliasing={{}: (12, {})} | custom-call | flops 1342177280 | bytes 3145728 | tf_op jit(solution)/shard_map/fold/pallas_call | solution.py:313
  75.7 1.9 %collective-permute-start.12 = (bf16[512,256]{1,0:T(8,128)(2,1)S(1)}, bf16[512,256]{1,0:T(8,128)(2,1)S(1)}, u32[]{:S(2)}, u32[]{:S(2)}) collective-permute-start(bf16[512,256]{1,0:T(8,128)(2,1)S(1)} %collective-permute-done.11.refs_2_), channel_id=1, source_target_pairs={{4,12},{12,20},{20,28},{28,24},{24,16},{16,8},{8,0},{0,4},{5,13},{... | collective-permute-start | bytes 786440 | tf_op jit(solution)/shard_map/ppermute | solution.py:359
  78.8 1.5 %fold.9 = (f32[512,1536]{1,0:T(8,128)S(1)}, f32[1024,1536]{1,0:T(8,128)}) custom-call(s32[2,8]{1,0:T(2,128)S(4)} %get-tuple-element.25.codes_ref, bf16[2,8,256,256]{3,2,1,0:T(8,128)(2,1)S(1)} %get-tuple-element.26.ints_ref, bf16[512,256]{1,0:T(8,128)(2,1)S(1)} %collective-permute-done.10.refs_0_, ...), custom_call_target="tpu_custom_call", output_to_operand_aliasing={{0}: (6, {}), {1}: (7, {})} | custom-call | flops 536870912 | bytes 3145728 | tf_op jit(solution)/shard_map/fold/pallas_call | solution.py:313
  81.2 1.5 %fold.10.refs_3_ = f32[1024,1536]{1,0:T(8,128)} custom-call(s32[2,8]{1,0:T(2,128)S(4)} %get-tuple-element.25.codes_ref, bf16[2,8,256,256]{3,2,1,0:T(8,128)(2,1)S(1)} %get-tuple-element.26.ints_ref, bf16[512,256]{1,0:T(8,128)(2,1)S(1)} %collective-permute-done.28.refs_0_, ...), custom_call_target="tpu_custom_call", output_to_operand_aliasing={{}: (5, {})} | custom-call | flops 268435456 | bytes 3145728 | tf_op jit(solution)/shard_map/fold/pallas_call | solution.py:313
  82.7 3.3 %collective-permute-done.15.refs_1_ = bf16[512,256]{1,0:T(8,128)(2,1)S(1)} collective-permute-done((bf16[512,256]{1,0:T(8,128)(2,1)S(1)}, bf16[512,256]{1,0:T(8,128)(2,1)S(1)}, u32[]{:S(2)}, u32[]{:S(2)}) %collective-permute-start.15) | collective-permute-done | bytes 262176 | tf_op jit(solution)/shard_map/ppermute | solution.py:359
  86.0 1.6 %fold.11 = f32[1024,1536]{1,0:T(8,128)} custom-call(s32[2,8]{1,0:T(2,128)S(4)} %get-tuple-element.25.codes_ref, bf16[2,8,256,256]{3,2,1,0:T(8,128)(2,1)S(1)} %get-tuple-element.26.ints_ref, bf16[512,256]{1,0:T(8,128)(2,1)S(1)} %collective-permute-done.12.refs_0_, ...), custom_call_target="tpu_custom_call", output_to_operand_aliasing={{}: (5, {})} | custom-call | flops 268435456 | bytes 3145728 | tf_op jit(solution)/shard_map/fold/pallas_call | solution.py:313
  (37 shorter events, 6.7 us)
Async XLA Ops:
  1.5 12.4 %collective-permute-start = (bf16[1040,256]{1,0:T(8,128)(2,1)S(1)}, bf16[1040,256]{1,0:T(8,128)(2,1)S(1)}, u32[]{:S(2)}, u32[]{:S(2)}) collective-permute-start(bf16[1040,256]{1,0:T(8,128)(2,1)S(1)} %get-tuple-element.24.refs_0_), channel_id=1, source_target_pairs={{0,1},{1,0},{2,3},{3,2},{4,5},{5,4},{6,7},{7,6},{8,9},{9,8},{10,11... | collective-permute-start | bytes 1597448 | tf_op jit(solution)/shard_map/ppermute | solution.py:345
  2.0 9.8 %collective-permute-start.16 = (bf16[512,256]{1,0:T(8,128)(2,1)S(1)}, bf16[512,256]{1,0:T(8,128)(2,1)S(1)}, u32[]{:S(2)}, u32[]{:S(2)}) collective-permute-start(bf16[512,256]{1,0:T(8,128)(2,1)S(1)} %get-tuple-element.34.refs_0_), channel_id=1, source_target_pairs={{4,12},{12,20},{20,28},{28,24},{24,16},{16,8},{8,0},{0,4},{5,13},{... | collective-permute-start | bytes 786440 | tf_op jit(solution)/shard_map/ppermute | solution.py:359
  4.6 9.1 %collective-permute-start.21 = (bf16[512,256]{1,0:T(8,128)(2,1)S(1)}, bf16[512,256]{1,0:T(8,128)(2,1)S(1)}, u32[]{:S(2)}, u32[]{:S(2)}) collective-permute-start(bf16[512,256]{1,0:T(8,128)(2,1)S(1)} %get-tuple-element.35.refs_1_), channel_id=1, source_target_pairs={{12,4},{20,12},{28,20},{24,28},{16,24},{8,16},{0,8},{4,0},{13,5},{... | collective-permute-start | bytes 786440 | tf_op jit(solution)/shard_map/ppermute | solution.py:359
  4.8 14.6 %collective-permute-start.3 = (bf16[512,256]{1,0:T(8,128)(2,1)S(1)}, bf16[512,256]{1,0:T(8,128)(2,1)S(1)}, u32[]{:S(2)}, u32[]{:S(2)}) collective-permute-start(bf16[512,256]{1,0:T(8,128)(2,1)S(1)} %get-tuple-element.28.refs_1_), channel_id=1, source_target_pairs={{12,4},{20,12},{28,20},{24,28},{16,24},{8,16},{0,8},{4,0},{13,5},{... | collective-permute-start | bytes 786440 | tf_op jit(solution)/shard_map/ppermute | solution.py:359
  6.7 12.8 %collective-permute-start.2 = (bf16[512,256]{1,0:T(8,128)(2,1)S(1)}, bf16[512,256]{1,0:T(8,128)(2,1)S(1)}, u32[]{:S(2)}, u32[]{:S(2)}) collective-permute-start(bf16[512,256]{1,0:T(8,128)(2,1)S(1)} %get-tuple-element.27.refs_0_), channel_id=1, source_target_pairs={{4,12},{12,20},{20,28},{28,24},{24,16},{16,8},{8,0},{0,4},{5,13},{... | collective-permute-start | bytes 786440 | tf_op jit(solution)/shard_map/ppermute | solution.py:359
  11.8 11.2 %collective-permute-start.17 = (bf16[512,256]{1,0:T(8,128)(2,1)S(1)}, bf16[512,256]{1,0:T(8,128)(2,1)S(1)}, u32[]{:S(2)}, u32[]{:S(2)}) collective-permute-start(bf16[512,256]{1,0:T(8,128)(2,1)S(1)} %collective-permute-done.16.refs_2_), channel_id=1, source_target_pairs={{4,12},{12,20},{20,28},{28,24},{24,16},{16,8},{8,0},{0,4},{5,13},{... | collective-permute-start | bytes 786440 | tf_op jit(solution)/shard_map/ppermute | solution.py:359
  13.7 11.2 %collective-permute-start.22 = (bf16[512,256]{1,0:T(8,128)(2,1)S(1)}, bf16[512,256]{1,0:T(8,128)(2,1)S(1)}, u32[]{:S(2)}, u32[]{:S(2)}) collective-permute-start(bf16[512,256]{1,0:T(8,128)(2,1)S(1)} %collective-permute-done.21.refs_3_), channel_id=1, source_target_pairs={{12,4},{20,12},{28,20},{24,28},{16,24},{8,16},{0,8},{4,0},{13,5},{... | collective-permute-start | bytes 786440 | tf_op jit(solution)/shard_map/ppermute | solution.py:359
  14.0 44.9 %collective-permute-start.1 = (bf16[2080,256]{1,0:T(8,128)(2,1)S(1)}, bf16[2080,256]{1,0:T(8,128)(2,1)S(1)}, u32[]{:S(2)}, u32[]{:S(2)}) collective-permute-start(bf16[2080,256]{1,0:T(8,128)(2,1)S(1)} %join.1.refs_0_), channel_id=1, source_target_pairs={{0,2},{1,3},{2,0},{3,1},{4,6},{5,7},{6,4},{7,5},{8,10},{9,11},{10,... | collective-permute-start | bytes 3194888 | tf_op jit(solution)/shard_map/ppermute | solution.py:348
  19.4 11.2 %collective-permute-start.5 = (bf16[512,256]{1,0:T(8,128)(2,1)S(1)}, bf16[512,256]{1,0:T(8,128)(2,1)S(1)}, u32[]{:S(2)}, u32[]{:S(2)}) collective-permute-start(bf16[512,256]{1,0:T(8,128)(2,1)S(1)} %collective-permute-done.3.refs_3_), channel_id=1, source_target_pairs={{12,4},{20,12},{28,20},{24,28},{16,24},{8,16},{0,8},{4,0},{13,5},{... | collective-permute-start | bytes 786440 | tf_op jit(solution)/shard_map/ppermute | solution.py:359
  19.5 11.2 %collective-permute-start.4 = (bf16[512,256]{1,0:T(8,128)(2,1)S(1)}, bf16[512,256]{1,0:T(8,128)(2,1)S(1)}, u32[]{:S(2)}, u32[]{:S(2)}) collective-permute-start(bf16[512,256]{1,0:T(8,128)(2,1)S(1)} %collective-permute-done.2.refs_2_), channel_id=1, source_target_pairs={{4,12},{12,20},{20,28},{28,24},{24,16},{16,8},{8,0},{0,4},{5,13},{... | collective-permute-start | bytes 786440 | tf_op jit(solution)/shard_map/ppermute | solution.py:359
  23.1 11.2 %collective-permute-start.18 = (bf16[512,256]{1,0:T(8,128)(2,1)S(1)}, bf16[512,256]{1,0:T(8,128)(2,1)S(1)}, u32[]{:S(2)}, u32[]{:S(2)}) collective-permute-start(bf16[512,256]{1,0:T(8,128)(2,1)S(1)} %collective-permute-done.17.refs_4_), channel_id=1, source_target_pairs={{4,12},{12,20},{20,28},{28,24},{24,16},{16,8},{8,0},{0,4},{5,13},{... | collective-permute-start | bytes 786440 | tf_op jit(solution)/shard_map/ppermute | solution.py:359
  25.0 11.3 %collective-permute-start.23 = (bf16[512,256]{1,0:T(8,128)(2,1)S(1)}, bf16[512,256]{1,0:T(8,128)(2,1)S(1)}, u32[]{:S(2)}, u32[]{:S(2)}) collective-permute-start(bf16[512,256]{1,0:T(8,128)(2,1)S(1)} %collective-permute-done.22.refs_5_), channel_id=1, source_target_pairs={{12,4},{20,12},{28,20},{24,28},{16,24},{8,16},{0,8},{4,0},{13,5},{... | collective-permute-start | bytes 786440 | tf_op jit(solution)/shard_map/ppermute | solution.py:359
  30.6 11.2 %collective-permute-start.7 = (bf16[512,256]{1,0:T(8,128)(2,1)S(1)}, bf16[512,256]{1,0:T(8,128)(2,1)S(1)}, u32[]{:S(2)}, u32[]{:S(2)}) collective-permute-start(bf16[512,256]{1,0:T(8,128)(2,1)S(1)} %collective-permute-done.5.refs_5_), channel_id=1, source_target_pairs={{12,4},{20,12},{28,20},{24,28},{16,24},{8,16},{0,8},{4,0},{13,5},{... | collective-permute-start | bytes 786440 | tf_op jit(solution)/shard_map/ppermute | solution.py:359
  30.7 11.2 %collective-permute-start.6 = (bf16[512,256]{1,0:T(8,128)(2,1)S(1)}, bf16[512,256]{1,0:T(8,128)(2,1)S(1)}, u32[]{:S(2)}, u32[]{:S(2)}) collective-permute-start(bf16[512,256]{1,0:T(8,128)(2,1)S(1)} %collective-permute-done.4.refs_4_), channel_id=1, source_target_pairs={{4,12},{12,20},{20,28},{28,24},{24,16},{16,8},{8,0},{0,4},{5,13},{... | collective-permute-start | bytes 786440 | tf_op jit(solution)/shard_map/ppermute | solution.py:359
  34.3 11.2 %collective-permute-start.19 = (bf16[512,256]{1,0:T(8,128)(2,1)S(1)}, bf16[512,256]{1,0:T(8,128)(2,1)S(1)}, u32[]{:S(2)}, u32[]{:S(2)}) collective-permute-start(bf16[512,256]{1,0:T(8,128)(2,1)S(1)} %collective-permute-done.18.refs_6_), channel_id=1, source_target_pairs={{4,12},{12,20},{20,28},{28,24},{24,16},{16,8},{8,0},{0,4},{5,13},{... | collective-permute-start | bytes 786440 | tf_op jit(solution)/shard_map/ppermute | solution.py:359
  36.3 11.2 %collective-permute-start.24 = (bf16[512,256]{1,0:T(8,128)(2,1)S(1)}, bf16[512,256]{1,0:T(8,128)(2,1)S(1)}, u32[]{:S(2)}, u32[]{:S(2)}) collective-permute-start(bf16[512,256]{1,0:T(8,128)(2,1)S(1)} %collective-permute-done.23.refs_7_), channel_id=1, source_target_pairs={{12,4},{20,12},{28,20},{24,28},{16,24},{8,16},{0,8},{4,0},{13,5},{... | collective-permute-start | bytes 786440 | tf_op jit(solution)/shard_map/ppermute | solution.py:359
  41.8 11.2 %collective-permute-start.9 = (bf16[512,256]{1,0:T(8,128)(2,1)S(1)}, bf16[512,256]{1,0:T(8,128)(2,1)S(1)}, u32[]{:S(2)}, u32[]{:S(2)}) collective-permute-start(bf16[512,256]{1,0:T(8,128)(2,1)S(1)} %collective-permute-done.7.refs_7_), channel_id=1, source_target_pairs={{12,4},{20,12},{28,20},{24,28},{16,24},{8,16},{0,8},{4,0},{13,5},{... | collective-permute-start | bytes 786440 | tf_op jit(solution)/shard_map/ppermute | solution.py:359
  42.0 11.2 %collective-permute-start.8 = (bf16[512,256]{1,0:T(8,128)(2,1)S(1)}, bf16[512,256]{1,0:T(8,128)(2,1)S(1)}, u32[]{:S(2)}, u32[]{:S(2)}) collective-permute-start(bf16[512,256]{1,0:T(8,128)(2,1)S(1)} %collective-permute-done.6.refs_6_), channel_id=1, source_target_pairs={{4,12},{12,20},{20,28},{28,24},{24,16},{16,8},{8,0},{0,4},{5,13},{... | collective-permute-start | bytes 786440 | tf_op jit(solution)/shard_map/ppermute | solution.py:359
  45.5 11.2 %collective-permute-start.20 = (bf16[512,256]{1,0:T(8,128)(2,1)S(1)}, bf16[512,256]{1,0:T(8,128)(2,1)S(1)}, u32[]{:S(2)}, u32[]{:S(2)}) collective-permute-start(bf16[512,256]{1,0:T(8,128)(2,1)S(1)} %collective-permute-done.19.refs_8_), channel_id=1, source_target_pairs={{4,12},{12,20},{20,28},{28,24},{24,16},{16,8},{8,0},{0,4},{5,13},{... | collective-permute-start | bytes 786440 | tf_op jit(solution)/shard_map/ppermute | solution.py:359
  47.5 11.2 %collective-permute-start.25 = (bf16[512,256]{1,0:T(8,128)(2,1)S(1)}, bf16[512,256]{1,0:T(8,128)(2,1)S(1)}, u32[]{:S(2)}, u32[]{:S(2)}) collective-permute-start(bf16[512,256]{1,0:T(8,128)(2,1)S(1)} %collective-permute-done.24.refs_9_), channel_id=1, source_target_pairs={{12,4},{20,12},{28,20},{24,28},{16,24},{8,16},{0,8},{4,0},{13,5},{... | collective-permute-start | bytes 786440 | tf_op jit(solution)/shard_map/ppermute | solution.py:359
  53.1 11.2 %collective-permute-start.13 = (bf16[512,256]{1,0:T(8,128)(2,1)S(1)}, bf16[512,256]{1,0:T(8,128)(2,1)S(1)}, u32[]{:S(2)}, u32[]{:S(2)}) collective-permute-start(bf16[512,256]{1,0:T(8,128)(2,1)S(1)} %collective-permute-done.9.refs_9_), channel_id=1, source_target_pairs={{12,4},{20,12},{28,20},{24,28},{16,24},{8,16},{0,8},{4,0},{13,5},{... | collective-permute-start | bytes 786440 | tf_op jit(solution)/shard_map/ppermute | solution.py:359
  53.2 11.2 %collective-permute-start.10 = (bf16[512,256]{1,0:T(8,128)(2,1)S(1)}, bf16[512,256]{1,0:T(8,128)(2,1)S(1)}, u32[]{:S(2)}, u32[]{:S(2)}) collective-permute-start(bf16[512,256]{1,0:T(8,128)(2,1)S(1)} %collective-permute-done.8.refs_8_), channel_id=1, source_target_pairs={{4,12},{12,20},{20,28},{28,24},{24,16},{16,8},{8,0},{0,4},{5,13},{... | collective-permute-start | bytes 786440 | tf_op jit(solution)/shard_map/ppermute | solution.py:359
  56.8 12.6 %collective-permute-start.26 = (bf16[512,256]{1,0:T(8,128)(2,1)S(1)}, bf16[512,256]{1,0:T(8,128)(2,1)S(1)}, u32[]{:S(2)}, u32[]{:S(2)}) collective-permute-start(bf16[512,256]{1,0:T(8,128)(2,1)S(1)} %collective-permute-done.20.refs_0_), channel_id=1, source_target_pairs={{4,12},{12,20},{20,28},{28,24},{24,16},{16,8},{8,0},{0,4},{5,13},{... | collective-permute-start | bytes 786440 | tf_op jit(solution)/shard_map/ppermute | solution.py:359
  58.7 11.2 %collective-permute-start.27 = (bf16[512,256]{1,0:T(8,128)(2,1)S(1)}, bf16[512,256]{1,0:T(8,128)(2,1)S(1)}, u32[]{:S(2)}, u32[]{:S(2)}) collective-permute-start(bf16[512,256]{1,0:T(8,128)(2,1)S(1)} %collective-permute-done.25.refs_1_), channel_id=1, source_target_pairs={{12,4},{20,12},{28,20},{24,28},{16,24},{8,16},{0,8},{4,0},{13,5},{... | collective-permute-start | bytes 786440 | tf_op jit(solution)/shard_map/ppermute | solution.py:359
  64.3 11.2 %collective-permute-start.14 = (bf16[512,256]{1,0:T(8,128)(2,1)S(1)}, bf16[512,256]{1,0:T(8,128)(2,1)S(1)}, u32[]{:S(2)}, u32[]{:S(2)}) collective-permute-start(bf16[512,256]{1,0:T(8,128)(2,1)S(1)} %collective-permute-done.13.refs_1_), channel_id=1, source_target_pairs={{12,4},{20,12},{28,20},{24,28},{16,24},{8,16},{0,8},{4,0},{13,5},{... | collective-permute-start | bytes 786440 | tf_op jit(solution)/shard_map/ppermute | solution.py:359
  64.4 11.1 %collective-permute-start.11 = (bf16[512,256]{1,0:T(8,128)(2,1)S(1)}, bf16[512,256]{1,0:T(8,128)(2,1)S(1)}, u32[]{:S(2)}, u32[]{:S(2)}) collective-permute-start(bf16[512,256]{1,0:T(8,128)(2,1)S(1)} %collective-permute-done.10.refs_0_), channel_id=1, source_target_pairs={{4,12},{12,20},{20,28},{28,24},{24,16},{16,8},{8,0},{0,4},{5,13},{... | collective-permute-start | bytes 786440 | tf_op jit(solution)/shard_map/ppermute | solution.py:359
  69.9 10.3 %collective-permute-start.28 = (bf16[512,256]{1,0:T(8,128)(2,1)S(1)}, bf16[512,256]{1,0:T(8,128)(2,1)S(1)}, u32[]{:S(2)}, u32[]{:S(2)}) collective-permute-start(bf16[512,256]{1,0:T(8,128)(2,1)S(1)} %collective-permute-done.26.refs_2_), channel_id=1, source_target_pairs={{4,12},{12,20},{20,28},{28,24},{24,16},{16,8},{8,0},{0,4},{5,13},{... | collective-permute-start | bytes 786440 | tf_op jit(solution)/shard_map/ppermute | solution.py:359
  71.5 9.7 %collective-permute-start.29 = (bf16[512,256]{1,0:T(8,128)(2,1)S(1)}, bf16[512,256]{1,0:T(8,128)(2,1)S(1)}, u32[]{:S(2)}, u32[]{:S(2)}) collective-permute-start(bf16[512,256]{1,0:T(8,128)(2,1)S(1)} %collective-permute-done.27.refs_3_), channel_id=1, source_target_pairs={{12,4},{20,12},{28,20},{24,28},{16,24},{8,16},{0,8},{4,0},{13,5},{... | collective-permute-start | bytes 786440 | tf_op jit(solution)/shard_map/ppermute | solution.py:359
  75.5 10.5 %collective-permute-start.15 = (bf16[512,256]{1,0:T(8,128)(2,1)S(1)}, bf16[512,256]{1,0:T(8,128)(2,1)S(1)}, u32[]{:S(2)}, u32[]{:S(2)}) collective-permute-start(bf16[512,256]{1,0:T(8,128)(2,1)S(1)} %collective-permute-done.14.refs_3_), channel_id=1, source_target_pairs={{12,4},{20,12},{28,20},{24,28},{16,24},{8,16},{0,8},{4,0},{13,5},{... | collective-permute-start | bytes 786440 | tf_op jit(solution)/shard_map/ppermute | solution.py:359
  75.7 10.3 %collective-permute-start.12 = (bf16[512,256]{1,0:T(8,128)(2,1)S(1)}, bf16[512,256]{1,0:T(8,128)(2,1)S(1)}, u32[]{:S(2)}, u32[]{:S(2)}) collective-permute-start(bf16[512,256]{1,0:T(8,128)(2,1)S(1)} %collective-permute-done.11.refs_2_), channel_id=1, source_target_pairs={{4,12},{12,20},{20,28},{28,24},{24,16},{16,8},{8,0},{0,4},{5,13},{... | collective-permute-start | bytes 786440 | tf_op jit(solution)/shard_map/ppermute | solution.py:359

commit v5 on v4

--- a/solution.py
+++ b/solution.py
@@ -10,7 +10,7 @@
 MI = 4
 NJ = 6
 CORES = 2
-GROUPS = ((0, 2), (2, 4))
+GROUPS = ((0, MI),)
 LINES = 16
 VMEM_LIMIT = 8 * 1024 * 1024
 
@@ -119,6 +119,28 @@
     )(in_hbm(amp_rows), in_hbm(codes), in_hbm(amp_tiles), in_hbm(int_tiles))
 
 
+def split_kernel(*refs):
+    count = len(refs) // 3
+    for at, ref in enumerate(refs[:count]):
+        size = ref.shape[0] // 2
+        for half in range(2):
+            refs[count + half * count + at][...] = ref[pl.ds(half * size, size)]
+
+
+def split(chunks):
+    rows, width = chunks[0].shape
+    vmem = pl.BlockSpec(memory_space=pltpu.VMEM)
+    made = pl.pallas_call(
+        split_kernel,
+        out_shape=[pltpu.VMEM((rows // 2, width), chunks[0].dtype)] * (2 * len(chunks)),
+        in_specs=[vmem] * len(chunks),
+        out_specs=[vmem] * (2 * len(chunks)),
+        compiler_params=pltpu.CompilerParams(vmem_limit_bytes=VMEM_LIMIT),
+        name="split",
+    )(*map(in_vmem, chunks))
+    return made[: len(chunks)], made[len(chunks) :]
+
+
 def join_kernel(*refs):
     size = refs[0].shape[0]
     for at, ref in enumerate(refs[:-1]):
@@ -195,8 +217,7 @@
     inverse = [order.index(at) for at in range(len(order))]
     here = pick(inverse, me)
     found = []
-    for panel, hop in hops:
-        way = hop if panel % 2 == 0 else len(order) - hop
+    for panel, way in hops:
         source = pick(order, lax.rem(here + len(order) - way, len(order)))
         owner, held = source // rows_held, lax.rem(source, rows_held)
         for at in range(slots):
@@ -228,10 +249,12 @@
         ready = [jnp.logical_not(hit) for hit in columns_of(chunk_updates(codes_ref, later, order, rows_held, slots))]
     else:
         total_ref, out_ref, sem = rest[0], rest[-2], rest[-1]
+    rows = pl.ds(band[0], band[1])
+
     def send(column):
         cols = pl.ds(pl.multiple_of(column * width, width), width)
         return pltpu.make_async_copy(
-            total_ref.at[:, cols], out_ref.at[pl.ds(band[0], band[1]), cols], sem.at[column]
+            total_ref.at[rows, cols], out_ref.at[rows, cols], sem.at[column]
         )
 
     if first:
@@ -255,7 +278,7 @@
         @pl.when(live)
         def _():
             cols = pl.ds(pl.multiple_of(column * width, width), width)
-            total_ref[:, cols] += jnp.dot(
+            total_ref[rows, cols] += jnp.dot(
                 chunk[...], ints_ref[panel, slot], preferred_element_type=jnp.float32
             )
 
@@ -300,7 +323,7 @@
     if later is None or later:
         if not first:
             aliases[len(operands) - 1] = 0
-        out_shapes.append(pltpu.VMEM((rows, NJ * width), jnp.float32))
+        out_shapes.append(pltpu.VMEM(total.shape, jnp.float32))
         out_specs.append(vmem)
     if later is not None:
         if out is not None:
@@ -334,49 +357,50 @@
     across = n_col // CORES
     order = grid_cycle(n_row // across, across)[::-1]
     forth = [(order[at], order[(at + 1) % n_row]) for at in range(n_row)]
-    ways = [forth if panel % 2 == 0 else [(b, a) for a, b in forth] for panel in range(panels)]
+    ways = [forth, [(b, a) for a, b in forth]]
 
     swap = [(c, c // CORES * CORES + (c + 1) % CORES) for c in range(n_col)]
     whole = (MI * width, NJ * width)
-    cuts = [n_row - 3, n_row - 1, n_row]
-
     placed = place(amp_tiles, amp_rows, int_tiles, int_codes)
     streams, parcel = placed[:-1], placed[-1]
     parts = [join([parcel, lax.ppermute(parcel, "col", swap)])]
     for shift in range(1, n_col // CORES):
         moved = lax.optimization_barrier((parts[0], parts[-1]))[0] if shift > 1 else parts[0]
         parts.append(lax.ppermute(moved, "col", [(c, (c + shift * CORES) % n_col) for c in range(n_col)]))
-    codes, ints, *totals = collect(parts, panels, slots, rows_held * NJ + 1)
-    rings = [[list(streams[group * panels : (group + 1) * panels])] for group in range(len(GROUPS))]
-    early, out = [None] * len(GROUPS), None
-    for at in range(1, n_row):
-        for group, (top, bottom) in enumerate(GROUPS):
-            held = rings[group][-1]
-            if at == n_row - 2 and group == len(GROUPS) - 1:
-                held = [lax.optimization_barrier((ints, one))[1] for one in held]
-            if at == n_row - 1:
-                held = [lax.optimization_barrier((early[group], one))[1] for one in held]
-            rings[group].append([lax.ppermute(held[panel], "row", ways[panel]) for panel in range(panels)])
-        if at + 1 not in cuts:
-            continue
-        which = cuts.index(at + 1)
-        begin = cuts[which - 1] if which else 0
-        hops = [(panel, step) for step in range(begin, at + 1) for panel in range(panels)]
-        later = None
-        if which >= len(cuts) - 2:
-            later = [(panel, step) for step in range(at + 1, n_row) for panel in range(panels)]
-        for group, (top, bottom) in enumerate(GROUPS):
-            chunks = [rings[group][step][panel] for panel, step in hops]
-            band = (top * width, (bottom - top) * width)
-            made = fold(
-                codes, ints, chunks, hops, later, totals[group], out, order, rows_held, slots, band, whole
-            )
-            if later is None:
-                totals[group] = early[group] = made[0]
-            elif later:
-                totals[group], out = made
-            else:
-                out = made[0]
+    codes, ints, total = collect(parts, panels, slots, rows_held * NJ + 1)
+    rows = MI * width
+
+    def add(chunks, later, total, out, band):
+        tags = [tag for tag, _ in chunks]
+        made = fold(
+            codes, ints, [chunk for _, chunk in chunks], tags, later, total, out, order, rows_held, slots, band, whole
+        )
+        return made if later else made[0]
+
+    far = n_row // 2
+    lead = [(panel % 2, panel) for panel in range(panels)]
+    rest = [(1 - panel % 2, panel) for panel in range(panels)]
+
+    def tag(way, panel, hop):
+        return (panel, hop if way == 0 else n_row - hop)
+
+    held = {(way, panel): streams[panel] for way in range(2) for panel in range(panels)}
+    have = [((panel, 0), streams[panel]) for panel in range(panels)]
+    for hop in range(1, far):
+        if hop == far - 1:
+            total = early = add(have, None, total, None, (0, rows))
+            have = []
+        for one in lead + rest:
+            if hop < far - 1 or far - 1 <= n_row - 1 - far or one in lead:
+                held[one] = lax.ppermute(held[one], "row", ways[one[0]])
+                have.append((tag(*one, hop), held[one]))
+    last = [lax.optimization_barrier((early, held[one]))[1] for one in lead]
+    pieces = split(last)
+    later = [tag(*one, far) for one in lead]
+    ends = [[lax.ppermute(piece, "row", ways[one[0]]) for one, piece in zip(lead, half)] for half in pieces]
+    total, out = add(have, later, total, None, (0, rows))
+    for at, half in enumerate(ends):
+        out = add(list(zip(later, half)), [], total, out, (at * rows // 2, rows // 2))
     return out
 
 

time: 87.5 us -> 86.8 us (level)
  waiting for transfers between devices: 41.8 us -> 58.7 us
  starting transfers between devices: 31.6 us -> 19.5 us
  Pallas kernels: 14.1 us -> 7.87 us
    ppermute x28 -> x16, waiting for transfers between devices: 41.8 us -> 58.7 us  [the longest x12 51 us: body(): held[one] = lax.ppermute(held[one], 'row', ways[one[0]])]
    ppermute x28 -> x16, starting transfers between devices: 29.1 us -> 17 us  [the longest x12 12.8 us: body(): held[one] = lax.ppermute(held[one], 'row', ways[one[0]])]
    pallas_call x6 -> x4, Pallas kernels: 11.8 us -> 5.52 us  [fold(): pl.pallas_call(functools.partial(fold_kernel, first, hops, later, order,...]
  transfers between devices with their start and end apart: 30 -> 18, of which waited for: 14 -> 9; matrix products, arithmetic and copies ran while one was open for 0% -> 0% of each run, Pallas kernels for 13% -> 7%
where the time goes in v5:
time: 86.8 us; the launch traced here: 86.1 us
  waiting for transfers between devices  58.7 us (68%)
  starting transfers between devices  19.5 us (22%)
  Pallas kernels  7.87 us (9%)
    ppermute x12, waiting for transfers between devices, body(): held[one] = lax.ppermute(held[one], 'row', ways[one[0]])  51 us
    ppermute x12, starting transfers between devices, body(): held[one] = lax.ppermute(held[one], 'row', ways[one[0]])  12.8 us
    ppermute x4, waiting for transfers between devices, body(): lax.ppermute(piece, 'row', ways[one[0]])  7.67 us
    pallas_call x4, Pallas kernels, fold(): pl.pallas_call(functools.partial(fold_kernel, first, hops, later, order,...  5.52 us
    ppermute x4, starting transfers between devices, body(): lax.ppermute(piece, 'row', ways[one[0]])  4.17 us
    ppermute x1, starting transfers between devices, body(): lax.ppermute(moved, 'col', [(c, (c + shift * CORES) % n_col) for c in ran...  2.03 us
  transfers between devices with their start and end apart: 18, of which 9 were waited for; matrix products, arithmetic and copies ran while one was open for 0% of the time, Pallas kernels for 7%

profile of v5, /device:TPU:0, one launch (start us, length us, event | category | flops | bytes accessed | tf_op | source)
XLA Modules:
  0.0 86.1 jit_solution(1721176448622227517)
XLA Ops:
  0.0 1.5 %place.1 = (bf16[1024,256]{1,0:T(8,128)(2,1)S(1)}, bf16[1024,256]{1,0:T(8,128)(2,1)S(1)}, bf16[1040,256]{1,0:T(8,128)(2,1)S(1)}) custom-call(s32[2,1,4]{2,1,0:T(1,128)} %rows_hbm.1, s32[2,1,2]{2,1,0:T(1,128)} %bitcast.3, bf16[2,1,4,256,256]{4,3,2,1,0:T(8,128)(2,1)} %tiles_hbm.1, bf16[2,2,1,256,256]{4,3,2,1,0:T(8,128)(2,1)} %ints_hbm.1), custom_call_target="tpu_custom_call" | custom-call | tf_op jit(solution)/shard_map/place/pallas_call | solution.py:104
  1.5 0.5 collective-permute-start
  2.0 2.6 %collective-permute-start.3 = (bf16[1024,256]{1,0:T(8,128)(2,1)S(1)}, bf16[1024,256]{1,0:T(8,128)(2,1)S(1)}, u32[]{:S(2)}, u32[]{:S(2)}) collective-permute-start(bf16[1024,256]{1,0:T(8,128)(2,1)S(1)} %get-tuple-element.23.refs_1_), channel_id=1, source_target_pairs={{12,4},{20,12},{28,20},{24,28},{16,24},{8,16},{0,8},{4,0},{13,5},{... | collective-permute-start | bytes 1572872 | tf_op jit(solution)/shard_map/ppermute | solution.py:395
  4.7 2.0 %collective-permute-start.4 = (bf16[1024,256]{1,0:T(8,128)(2,1)S(1)}, bf16[1024,256]{1,0:T(8,128)(2,1)S(1)}, u32[]{:S(2)}, u32[]{:S(2)}) collective-permute-start(bf16[1024,256]{1,0:T(8,128)(2,1)S(1)} %get-tuple-element.22.refs_0_), channel_id=1, source_target_pairs={{12,4},{20,12},{28,20},{24,28},{16,24},{8,16},{0,8},{4,0},{13,5},{... | collective-permute-start | bytes 1572872 | tf_op jit(solution)/shard_map/ppermute | solution.py:395
  6.7 0.1 join.1.refs_0_
  6.8 2.0 %collective-permute-start.1 = (bf16[2080,256]{1,0:T(8,128)(2,1)S(1)}, bf16[2080,256]{1,0:T(8,128)(2,1)S(1)}, u32[]{:S(2)}, u32[]{:S(2)}) collective-permute-start(bf16[2080,256]{1,0:T(8,128)(2,1)S(1)} %join.1.refs_0_), channel_id=1, source_target_pairs={{0,2},{1,3},{2,0},{3,1},{4,6},{5,7},{6,4},{7,5},{8,10},{9,11},{10,... | collective-permute-start | bytes 3194888 | tf_op jit(solution)/shard_map/ppermute | solution.py:369
  8.8 8.6 %collective-permute-done.3.refs_3_ = bf16[1024,256]{1,0:T(8,128)(2,1)S(1)} collective-permute-done((bf16[1024,256]{1,0:T(8,128)(2,1)S(1)}, bf16[1024,256]{1,0:T(8,128)(2,1)S(1)}, u32[]{:S(2)}, u32[]{:S(2)}) %collective-permute-start.3) | collective-permute-done | bytes 524320 | tf_op jit(solution)/shard_map/ppermute | solution.py:395
  17.4 2.0 %collective-permute-start.7 = (bf16[1024,256]{1,0:T(8,128)(2,1)S(1)}, bf16[1024,256]{1,0:T(8,128)(2,1)S(1)}, u32[]{:S(2)}, u32[]{:S(2)}) collective-permute-start(bf16[1024,256]{1,0:T(8,128)(2,1)S(1)} %collective-permute-done.3.refs_3_), channel_id=1, source_target_pairs={{12,4},{20,12},{28,20},{24,28},{16,24},{8,16},{0,8},{4,0},{13,5},{... | collective-permute-start | bytes 1572872 | tf_op jit(solution)/shard_map/ppermute | solution.py:395
  19.4 0.0 collective-permute-done.2.refs_2_
  19.5 9.2 %collective-permute-done.4.refs_4_ = bf16[1024,256]{1,0:T(8,128)(2,1)S(1)} collective-permute-done((bf16[1024,256]{1,0:T(8,128)(2,1)S(1)}, bf16[1024,256]{1,0:T(8,128)(2,1)S(1)}, u32[]{:S(2)}, u32[]{:S(2)}) %collective-permute-start.4) | collective-permute-done | bytes 524320 | tf_op jit(solution)/shard_map/ppermute | solution.py:395
  28.6 2.0 %collective-permute-start.8 = (bf16[1024,256]{1,0:T(8,128)(2,1)S(1)}, bf16[1024,256]{1,0:T(8,128)(2,1)S(1)}, u32[]{:S(2)}, u32[]{:S(2)}) collective-permute-start(bf16[1024,256]{1,0:T(8,128)(2,1)S(1)} %collective-permute-done.4.refs_4_), channel_id=1, source_target_pairs={{12,4},{20,12},{28,20},{24,28},{16,24},{8,16},{0,8},{4,0},{13,5},{... | collective-permute-start | bytes 1572872 | tf_op jit(solution)/shard_map/ppermute | solution.py:395
  30.6 0.0 collective-permute-done.5.refs_5_
  30.7 9.2 %collective-permute-done.7.refs_7_ = bf16[1024,256]{1,0:T(8,128)(2,1)S(1)} collective-permute-done((bf16[1024,256]{1,0:T(8,128)(2,1)S(1)}, bf16[1024,256]{1,0:T(8,128)(2,1)S(1)}, u32[]{:S(2)}, u32[]{:S(2)}) %collective-permute-start.7) | collective-permute-done | bytes 524320 | tf_op jit(solution)/shard_map/ppermute | solution.py:395
  39.8 2.0 %collective-permute-start.11 = (bf16[1024,256]{1,0:T(8,128)(2,1)S(1)}, bf16[1024,256]{1,0:T(8,128)(2,1)S(1)}, u32[]{:S(2)}, u32[]{:S(2)}) collective-permute-start(bf16[1024,256]{1,0:T(8,128)(2,1)S(1)} %collective-permute-done.7.refs_7_), channel_id=1, source_target_pairs={{12,4},{20,12},{28,20},{24,28},{16,24},{8,16},{0,8},{4,0},{13,5},{... | collective-permute-start | bytes 1572872 | tf_op jit(solution)/shard_map/ppermute | solution.py:395
  41.9 0.0 collective-permute-done.6.refs_6_
  41.9 9.2 %collective-permute-done.8.refs_8_ = bf16[1024,256]{1,0:T(8,128)(2,1)S(1)} collective-permute-done((bf16[1024,256]{1,0:T(8,128)(2,1)S(1)}, bf16[1024,256]{1,0:T(8,128)(2,1)S(1)}, u32[]{:S(2)}, u32[]{:S(2)}) %collective-permute-start.8) | collective-permute-done | bytes 524320 | tf_op jit(solution)/shard_map/ppermute | solution.py:395
  51.1 2.0 %collective-permute-start.14 = (bf16[1024,256]{1,0:T(8,128)(2,1)S(1)}, bf16[1024,256]{1,0:T(8,128)(2,1)S(1)}, u32[]{:S(2)}, u32[]{:S(2)}) collective-permute-start(bf16[1024,256]{1,0:T(8,128)(2,1)S(1)} %collective-permute-done.8.refs_8_), channel_id=1, source_target_pairs={{12,4},{20,12},{28,20},{24,28},{16,24},{8,16},{0,8},{4,0},{13,5},{... | collective-permute-start | bytes 1572872 | tf_op jit(solution)/shard_map/ppermute | solution.py:395
  53.2 0.7 collect.1
  53.9 2.7 %fold.4.refs_4_ = f32[1024,1536]{1,0:T(8,128)S(1)} custom-call(s32[2,8]{1,0:T(2,128)S(4)} %get-tuple-element.20.codes_ref, bf16[2,8,256,256]{3,2,1,0:T(8,128)(2,1)S(1)} %get-tuple-element.21.ints_ref, bf16[1024,256]{1,0:T(8,128)(2,1)S(1)} %get-tuple-element.22.refs_0_, ...), custom_call_target="tpu_custom_call", output_to_operand_aliasing={{}: (12, {})} | custom-call | flops 2684354560 | bytes 6291456 | tf_op jit(solution)/shard_map/fold/pallas_call | solution.py:336
  56.6 5.8 %collective-permute-done.11.refs_1_ = bf16[1024,256]{1,0:T(8,128)(2,1)S(1)} collective-permute-done((bf16[1024,256]{1,0:T(8,128)(2,1)S(1)}, bf16[1024,256]{1,0:T(8,128)(2,1)S(1)}, u32[]{:S(2)}, u32[]{:S(2)}) %collective-permute-start.11) | collective-permute-done | bytes 524320 | tf_op jit(solution)/shard_map/ppermute | solution.py:395
  62.3 2.1 %collective-permute-done.10.refs_0_ = bf16[1024,256]{1,0:T(8,128)(2,1)S(1)} collective-permute-done((bf16[1024,256]{1,0:T(8,128)(2,1)S(1)}, bf16[1024,256]{1,0:T(8,128)(2,1)S(1)}, u32[]{:S(2)}, u32[]{:S(2)}) %collective-permute-start.10) | collective-permute-done | bytes 524320 | tf_op jit(solution)/shard_map/ppermute | solution.py:395
  64.4 0.1 split.1
  64.5 0.1 collective-permute-start.16
  64.5 2.0 %collective-permute-start.17 = (bf16[512,256]{1,0:T(8,128)(2,1)S(1)}, bf16[512,256]{1,0:T(8,128)(2,1)S(1)}, u32[]{:S(2)}, u32[]{:S(2)}) collective-permute-start(bf16[512,256]{1,0:T(8,128)(2,1)S(1)} %get-tuple-element.31), channel_id=1, source_target_pairs={{12,4},{20,12},{28,20},{24,28},{16,24},{8,16},{0,8},{4,0},{13,5},{... | collective-permute-start | bytes 786440 | tf_op jit(solution)/shard_map/ppermute | solution.py:400
  66.5 0.1 collective-permute-start.12
  66.6 6.9 %collective-permute-done.14.refs_2_ = bf16[1024,256]{1,0:T(8,128)(2,1)S(1)} collective-permute-done((bf16[1024,256]{1,0:T(8,128)(2,1)S(1)}, bf16[1024,256]{1,0:T(8,128)(2,1)S(1)}, u32[]{:S(2)}, u32[]{:S(2)}) %collective-permute-start.14) | collective-permute-done | bytes 524320 | tf_op jit(solution)/shard_map/ppermute | solution.py:395
  73.5 2.0 %collective-permute-start.13 = (bf16[512,256]{1,0:T(8,128)(2,1)S(1)}, bf16[512,256]{1,0:T(8,128)(2,1)S(1)}, u32[]{:S(2)}, u32[]{:S(2)}) collective-permute-start(bf16[512,256]{1,0:T(8,128)(2,1)S(1)} %get-tuple-element.28), channel_id=1, source_target_pairs={{12,4},{20,12},{28,20},{24,28},{16,24},{8,16},{0,8},{4,0},{13,5},{... | collective-permute-start | bytes 786440 | tf_op jit(solution)/shard_map/ppermute | solution.py:400
  75.6 2.7 %fold.5 = (f32[1024,1536]{1,0:T(8,128)S(1)}, f32[1024,1536]{1,0:T(8,128)}) custom-call(s32[2,8]{1,0:T(2,128)S(4)} %get-tuple-element.20.codes_ref, bf16[2,8,256,256]{3,2,1,0:T(8,128)(2,1)S(1)} %get-tuple-element.21.ints_ref, bf16[1024,256]{1,0:T(8,128)(2,1)S(1)} %collective-permute-done.10.refs_0_, ...), custom_call_target="tpu_custom_call", output_to_operand_aliasing={{0}: (6, {})} | custom-call | flops 1073741824 | bytes 6291456 | tf_op jit(solution)/shard_map/fold/pallas_call | solution.py:336
  78.4 2.9 %collective-permute-done.16.refs_0_ = bf16[512,256]{1,0:T(8,128)(2,1)S(1)} collective-permute-done((bf16[512,256]{1,0:T(8,128)(2,1)S(1)}, bf16[512,256]{1,0:T(8,128)(2,1)S(1)}, u32[]{:S(2)}, u32[]{:S(2)}) %collective-permute-start.16) | collective-permute-done | bytes 262176 | tf_op jit(solution)/shard_map/ppermute | solution.py:400
  81.2 0.1 fold.6.refs_3_
  81.3 4.8 %collective-permute-done.12.refs_0_ = bf16[512,256]{1,0:T(8,128)(2,1)S(1)} collective-permute-done((bf16[512,256]{1,0:T(8,128)(2,1)S(1)}, bf16[512,256]{1,0:T(8,128)(2,1)S(1)}, u32[]{:S(2)}, u32[]{:S(2)}) %collective-permute-start.12) | collective-permute-done | bytes 262176 | tf_op jit(solution)/shard_map/ppermute | solution.py:400
  86.1 0.1 fold.7
  (12 shorter events, 0.1 us)
Async XLA Ops:
  1.5 5.2 %collective-permute-start = (bf16[1040,256]{1,0:T(8,128)(2,1)S(1)}, bf16[1040,256]{1,0:T(8,128)(2,1)S(1)}, u32[]{:S(2)}, u32[]{:S(2)}) collective-permute-start(bf16[1040,256]{1,0:T(8,128)(2,1)S(1)} %get-tuple-element.19.refs_0_), channel_id=1, source_target_pairs={{0,1},{1,0},{2,3},{3,2},{4,5},{5,4},{6,7},{7,6},{8,9},{9,8},{10,11... | collective-permute-start | bytes 1597448 | tf_op jit(solution)/shard_map/ppermute | solution.py:366
  2.0 15.3 %collective-permute-start.3 = (bf16[1024,256]{1,0:T(8,128)(2,1)S(1)}, bf16[1024,256]{1,0:T(8,128)(2,1)S(1)}, u32[]{:S(2)}, u32[]{:S(2)}) collective-permute-start(bf16[1024,256]{1,0:T(8,128)(2,1)S(1)} %get-tuple-element.23.refs_1_), channel_id=1, source_target_pairs={{12,4},{20,12},{28,20},{24,28},{16,24},{8,16},{0,8},{4,0},{13,5},{... | collective-permute-start | bytes 1572872 | tf_op jit(solution)/shard_map/ppermute | solution.py:395
  4.7 14.8 %collective-permute-start.2 = (bf16[1024,256]{1,0:T(8,128)(2,1)S(1)}, bf16[1024,256]{1,0:T(8,128)(2,1)S(1)}, u32[]{:S(2)}, u32[]{:S(2)}) collective-permute-start(bf16[1024,256]{1,0:T(8,128)(2,1)S(1)} %get-tuple-element.22.refs_0_), channel_id=1, source_target_pairs={{4,12},{12,20},{20,28},{28,24},{24,16},{16,8},{8,0},{0,4},{5,13},{... | collective-permute-start | bytes 1572872 | tf_op jit(solution)/shard_map/ppermute | solution.py:395
  4.7 23.9 %collective-permute-start.4 = (bf16[1024,256]{1,0:T(8,128)(2,1)S(1)}, bf16[1024,256]{1,0:T(8,128)(2,1)S(1)}, u32[]{:S(2)}, u32[]{:S(2)}) collective-permute-start(bf16[1024,256]{1,0:T(8,128)(2,1)S(1)} %get-tuple-element.22.refs_0_), channel_id=1, source_target_pairs={{12,4},{20,12},{28,20},{24,28},{16,24},{8,16},{0,8},{4,0},{13,5},{... | collective-permute-start | bytes 1572872 | tf_op jit(solution)/shard_map/ppermute | solution.py:395
  6.7 24.0 %collective-permute-start.5 = (bf16[1024,256]{1,0:T(8,128)(2,1)S(1)}, bf16[1024,256]{1,0:T(8,128)(2,1)S(1)}, u32[]{:S(2)}, u32[]{:S(2)}) collective-permute-start(bf16[1024,256]{1,0:T(8,128)(2,1)S(1)} %get-tuple-element.23.refs_1_), channel_id=1, source_target_pairs={{4,12},{12,20},{20,28},{28,24},{24,16},{16,8},{8,0},{0,4},{5,13},{... | collective-permute-start | bytes 1572872 | tf_op jit(solution)/shard_map/ppermute | solution.py:395
  6.8 46.4 %collective-permute-start.1 = (bf16[2080,256]{1,0:T(8,128)(2,1)S(1)}, bf16[2080,256]{1,0:T(8,128)(2,1)S(1)}, u32[]{:S(2)}, u32[]{:S(2)}) collective-permute-start(bf16[2080,256]{1,0:T(8,128)(2,1)S(1)} %join.1.refs_0_), channel_id=1, source_target_pairs={{0,2},{1,3},{2,0},{3,1},{4,6},{5,7},{6,4},{7,5},{8,10},{9,11},{10,... | collective-permute-start | bytes 3194888 | tf_op jit(solution)/shard_map/ppermute | solution.py:369
  17.4 22.5 %collective-permute-start.7 = (bf16[1024,256]{1,0:T(8,128)(2,1)S(1)}, bf16[1024,256]{1,0:T(8,128)(2,1)S(1)}, u32[]{:S(2)}, u32[]{:S(2)}) collective-permute-start(bf16[1024,256]{1,0:T(8,128)(2,1)S(1)} %collective-permute-done.3.refs_3_), channel_id=1, source_target_pairs={{12,4},{20,12},{28,20},{24,28},{16,24},{8,16},{0,8},{4,0},{13,5},{... | collective-permute-start | bytes 1572872 | tf_op jit(solution)/shard_map/ppermute | solution.py:395
  19.4 22.5 %collective-permute-start.6 = (bf16[1024,256]{1,0:T(8,128)(2,1)S(1)}, bf16[1024,256]{1,0:T(8,128)(2,1)S(1)}, u32[]{:S(2)}, u32[]{:S(2)}) collective-permute-start(bf16[1024,256]{1,0:T(8,128)(2,1)S(1)} %collective-permute-done.2.refs_2_), channel_id=1, source_target_pairs={{4,12},{12,20},{20,28},{28,24},{24,16},{16,8},{8,0},{0,4},{5,13},{... | collective-permute-start | bytes 1572872 | tf_op jit(solution)/shard_map/ppermute | solution.py:395
  28.6 22.5 %collective-permute-start.8 = (bf16[1024,256]{1,0:T(8,128)(2,1)S(1)}, bf16[1024,256]{1,0:T(8,128)(2,1)S(1)}, u32[]{:S(2)}, u32[]{:S(2)}) collective-permute-start(bf16[1024,256]{1,0:T(8,128)(2,1)S(1)} %collective-permute-done.4.refs_4_), channel_id=1, source_target_pairs={{12,4},{20,12},{28,20},{24,28},{16,24},{8,16},{0,8},{4,0},{13,5},{... | collective-permute-start | bytes 1572872 | tf_op jit(solution)/shard_map/ppermute | solution.py:395
  30.7 22.5 %collective-permute-start.9 = (bf16[1024,256]{1,0:T(8,128)(2,1)S(1)}, bf16[1024,256]{1,0:T(8,128)(2,1)S(1)}, u32[]{:S(2)}, u32[]{:S(2)}) collective-permute-start(bf16[1024,256]{1,0:T(8,128)(2,1)S(1)} %collective-permute-done.5.refs_5_), channel_id=1, source_target_pairs={{4,12},{12,20},{20,28},{28,24},{24,16},{16,8},{8,0},{0,4},{5,13},{... | collective-permute-start | bytes 1572872 | tf_op jit(solution)/shard_map/ppermute | solution.py:395
  39.8 22.5 %collective-permute-start.11 = (bf16[1024,256]{1,0:T(8,128)(2,1)S(1)}, bf16[1024,256]{1,0:T(8,128)(2,1)S(1)}, u32[]{:S(2)}, u32[]{:S(2)}) collective-permute-start(bf16[1024,256]{1,0:T(8,128)(2,1)S(1)} %collective-permute-done.7.refs_7_), channel_id=1, source_target_pairs={{12,4},{20,12},{28,20},{24,28},{16,24},{8,16},{0,8},{4,0},{13,5},{... | collective-permute-start | bytes 1572872 | tf_op jit(solution)/shard_map/ppermute | solution.py:395
  41.9 22.5 %collective-permute-start.10 = (bf16[1024,256]{1,0:T(8,128)(2,1)S(1)}, bf16[1024,256]{1,0:T(8,128)(2,1)S(1)}, u32[]{:S(2)}, u32[]{:S(2)}) collective-permute-start(bf16[1024,256]{1,0:T(8,128)(2,1)S(1)} %collective-permute-done.6.refs_6_), channel_id=1, source_target_pairs={{4,12},{12,20},{20,28},{28,24},{24,16},{16,8},{8,0},{0,4},{5,13},{... | collective-permute-start | bytes 1572872 | tf_op jit(solution)/shard_map/ppermute | solution.py:395
  51.1 22.5 %collective-permute-start.14 = (bf16[1024,256]{1,0:T(8,128)(2,1)S(1)}, bf16[1024,256]{1,0:T(8,128)(2,1)S(1)}, u32[]{:S(2)}, u32[]{:S(2)}) collective-permute-start(bf16[1024,256]{1,0:T(8,128)(2,1)S(1)} %collective-permute-done.8.refs_8_), channel_id=1, source_target_pairs={{12,4},{20,12},{28,20},{24,28},{16,24},{8,16},{0,8},{4,0},{13,5},{... | collective-permute-start | bytes 1572872 | tf_op jit(solution)/shard_map/ppermute | solution.py:395
  53.2 22.5 %collective-permute-start.15 = (bf16[1024,256]{1,0:T(8,128)(2,1)S(1)}, bf16[1024,256]{1,0:T(8,128)(2,1)S(1)}, u32[]{:S(2)}, u32[]{:S(2)}) collective-permute-start(bf16[1024,256]{1,0:T(8,128)(2,1)S(1)} %collective-permute-done.9.refs_9_), channel_id=1, source_target_pairs={{4,12},{12,20},{20,28},{28,24},{24,16},{16,8},{8,0},{0,4},{5,13},{... | collective-permute-start | bytes 1572872 | tf_op jit(solution)/shard_map/ppermute | solution.py:395
  64.5 16.8 %collective-permute-start.16 = (bf16[512,256]{1,0:T(8,128)(2,1)S(1)}, bf16[512,256]{1,0:T(8,128)(2,1)S(1)}, u32[]{:S(2)}, u32[]{:S(2)}) collective-permute-start(bf16[512,256]{1,0:T(8,128)(2,1)S(1)} %get-tuple-element.30), channel_id=1, source_target_pairs={{4,12},{12,20},{20,28},{28,24},{24,16},{16,8},{8,0},{0,4},{5,13},{... | collective-permute-start | bytes 786440 | tf_op jit(solution)/shard_map/ppermute | solution.py:400
  64.5 16.7 %collective-permute-start.17 = (bf16[512,256]{1,0:T(8,128)(2,1)S(1)}, bf16[512,256]{1,0:T(8,128)(2,1)S(1)}, u32[]{:S(2)}, u32[]{:S(2)}) collective-permute-start(bf16[512,256]{1,0:T(8,128)(2,1)S(1)} %get-tuple-element.31), channel_id=1, source_target_pairs={{12,4},{20,12},{28,20},{24,28},{16,24},{8,16},{0,8},{4,0},{13,5},{... | collective-permute-start | bytes 786440 | tf_op jit(solution)/shard_map/ppermute | solution.py:400
  66.5 19.5 %collective-permute-start.12 = (bf16[512,256]{1,0:T(8,128)(2,1)S(1)}, bf16[512,256]{1,0:T(8,128)(2,1)S(1)}, u32[]{:S(2)}, u32[]{:S(2)}) collective-permute-start(bf16[512,256]{1,0:T(8,128)(2,1)S(1)} %get-tuple-element.27), channel_id=1, source_target_pairs={{4,12},{12,20},{20,28},{28,24},{24,16},{16,8},{8,0},{0,4},{5,13},{... | collective-permute-start | bytes 786440 | tf_op jit(solution)/shard_map/ppermute | solution.py:400
  73.5 12.5 %collective-permute-start.13 = (bf16[512,256]{1,0:T(8,128)(2,1)S(1)}, bf16[512,256]{1,0:T(8,128)(2,1)S(1)}, u32[]{:S(2)}, u32[]{:S(2)}) collective-permute-start(bf16[512,256]{1,0:T(8,128)(2,1)S(1)} %get-tuple-element.28), channel_id=1, source_target_pairs={{12,4},{20,12},{28,20},{24,28},{16,24},{8,16},{0,8},{4,0},{13,5},{... | collective-permute-start | bytes 786440 | tf_op jit(solution)/shard_map/ppermute | solution.py:400

commit v6 on v5

--- a/solution.py
+++ b/solution.py
@@ -12,6 +12,7 @@
 CORES = 2
 GROUPS = ((0, MI),)
 LINES = 16
+PIECES = (6, 2)
 VMEM_LIMIT = 8 * 1024 * 1024
 
 
@@ -120,25 +121,28 @@
 
 
 def split_kernel(*refs):
-    count = len(refs) // 3
+    count = len(refs) // (1 + len(PIECES))
     for at, ref in enumerate(refs[:count]):
-        size = ref.shape[0] // 2
-        for half in range(2):
-            refs[count + half * count + at][...] = ref[pl.ds(half * size, size)]
+        first = 0
+        for piece in range(len(PIECES)):
+            part = refs[count * (1 + piece) + at]
+            part[...] = ref[pl.ds(first, part.shape[0])]
+            first += part.shape[0]
 
 
 def split(chunks):
     rows, width = chunks[0].shape
     vmem = pl.BlockSpec(memory_space=pltpu.VMEM)
+    shapes = [pltpu.VMEM((rows * eighths // 8, width), chunks[0].dtype) for eighths in PIECES for _ in chunks]
     made = pl.pallas_call(
         split_kernel,
-        out_shape=[pltpu.VMEM((rows // 2, width), chunks[0].dtype)] * (2 * len(chunks)),
+        out_shape=shapes,
         in_specs=[vmem] * len(chunks),
-        out_specs=[vmem] * (2 * len(chunks)),
+        out_specs=[vmem] * len(shapes),
         compiler_params=pltpu.CompilerParams(vmem_limit_bytes=VMEM_LIMIT),
         name="split",
     )(*map(in_vmem, chunks))
-    return made[: len(chunks)], made[len(chunks) :]
+    return [made[at : at + len(chunks)] for at in range(0, len(made), len(chunks))]
 
 
 def join_kernel(*refs):
@@ -397,10 +401,12 @@
     last = [lax.optimization_barrier((early, held[one]))[1] for one in lead]
     pieces = split(last)
     later = [tag(*one, far) for one in lead]
-    ends = [[lax.ppermute(piece, "row", ways[one[0]]) for one, piece in zip(lead, half)] for half in pieces]
+    ends = [[lax.ppermute(part, "row", ways[one[0]]) for one, part in zip(lead, piece)] for piece in pieces]
     total, out = add(have, later, total, None, (0, rows))
-    for at, half in enumerate(ends):
-        out = add(list(zip(later, half)), [], total, out, (at * rows // 2, rows // 2))
+    first = 0
+    for piece, eighths in zip(ends, PIECES):
+        out = add(list(zip(later, piece)), [], total, out, (first, rows * eighths // 8))
+        first += rows * eighths // 8
     return out
 
 

time: 86.8 us -> 87.3 us (level)
  Pallas kernels: 7.87 us -> 9.81 us
  waiting for transfers between devices: 58.7 us -> 57.6 us
    pallas_call x4, Pallas kernels: 5.52 us -> 7.47 us  [fold(): pl.pallas_call(functools.partial(fold_kernel, first, hops, later, order,...]
    ppermute x4, waiting for transfers between devices: 7.67 us -> 6.34 us  [body(): lax.ppermute(part, 'row', ways[one[0]])]
  transfers between devices with their start and end apart: 18 -> 18, of which waited for: 9 -> 9; matrix products, arithmetic and copies ran while one was open for 0% -> 0% of each run, Pallas kernels for 7% -> 8%
where the time goes in v6:
time: 87.3 us; the launch traced here: 87 us
  waiting for transfers between devices  57.6 us (66%)
  starting transfers between devices  19.5 us (22%)
  Pallas kernels  9.81 us (11%)
    ppermute x12, waiting for transfers between devices, body(): held[one] = lax.ppermute(held[one], 'row', ways[one[0]])  51.3 us
    ppermute x12, starting transfers between devices, body(): held[one] = lax.ppermute(held[one], 'row', ways[one[0]])  12.8 us
    pallas_call x4, Pallas kernels, fold(): pl.pallas_call(functools.partial(fold_kernel, first, hops, later, order,...  7.47 us
    ppermute x4, waiting for transfers between devices, body(): lax.ppermute(part, 'row', ways[one[0]])  6.34 us
    ppermute x4, starting transfers between devices, body(): lax.ppermute(part, 'row', ways[one[0]])  4.17 us
    ppermute x1, starting transfers between devices, body(): lax.ppermute(moved, 'col', [(c, (c + shift * CORES) % n_col) for c in ran...  2.03 us
  transfers between devices with their start and end apart: 18, of which 9 were waited for; matrix products, arithmetic and copies ran while one was open for 0% of the time, Pallas kernels for 8%

profile of v6, /device:TPU:0, one launch (start us, length us, event | category | flops | bytes accessed | tf_op | source)
XLA Modules:
  0.0 87.0 jit_solution(5595195489105780986)
XLA Ops:
  0.0 1.5 %place.1 = (bf16[1024,256]{1,0:T(8,128)(2,1)S(1)}, bf16[1024,256]{1,0:T(8,128)(2,1)S(1)}, bf16[1040,256]{1,0:T(8,128)(2,1)S(1)}) custom-call(s32[2,1,4]{2,1,0:T(1,128)} %rows_hbm.1, s32[2,1,2]{2,1,0:T(1,128)} %bitcast.3, bf16[2,1,4,256,256]{4,3,2,1,0:T(8,128)(2,1)} %tiles_hbm.1, bf16[2,2,1,256,256]{4,3,2,1,0:T(8,128)(2,1)} %ints_hbm.1), custom_call_target="tpu_custom_call" | custom-call | tf_op jit(solution)/shard_map/place/pallas_call | solution.py:105
  1.5 0.5 collective-permute-start
  2.0 2.6 %collective-permute-start.3 = (bf16[1024,256]{1,0:T(8,128)(2,1)S(1)}, bf16[1024,256]{1,0:T(8,128)(2,1)S(1)}, u32[]{:S(2)}, u32[]{:S(2)}) collective-permute-start(bf16[1024,256]{1,0:T(8,128)(2,1)S(1)} %get-tuple-element.23.refs_1_), channel_id=1, source_target_pairs={{12,4},{20,12},{28,20},{24,28},{16,24},{8,16},{0,8},{4,0},{13,5},{... | collective-permute-start | bytes 1572872 | tf_op jit(solution)/shard_map/ppermute | solution.py:399
  4.7 0.1 join.1.refs_0_
  4.8 2.0 %collective-permute-start.1 = (bf16[2080,256]{1,0:T(8,128)(2,1)S(1)}, bf16[2080,256]{1,0:T(8,128)(2,1)S(1)}, u32[]{:S(2)}, u32[]{:S(2)}) collective-permute-start(bf16[2080,256]{1,0:T(8,128)(2,1)S(1)} %join.1.refs_0_), channel_id=1, source_target_pairs={{0,2},{1,3},{2,0},{3,1},{4,6},{5,7},{6,4},{7,5},{8,10},{9,11},{10,... | collective-permute-start | bytes 3194888 | tf_op jit(solution)/shard_map/ppermute | solution.py:373
  6.8 1.6 %collective-permute-start.4 = (bf16[1024,256]{1,0:T(8,128)(2,1)S(1)}, bf16[1024,256]{1,0:T(8,128)(2,1)S(1)}, u32[]{:S(2)}, u32[]{:S(2)}) collective-permute-start(bf16[1024,256]{1,0:T(8,128)(2,1)S(1)} %get-tuple-element.22.refs_0_), channel_id=1, source_target_pairs={{12,4},{20,12},{28,20},{24,28},{16,24},{8,16},{0,8},{4,0},{13,5},{... | collective-permute-start | bytes 1572872 | tf_op jit(solution)/shard_map/ppermute | solution.py:399
  8.4 0.4 collective-permute-start.5
  8.8 8.6 %collective-permute-done.3.refs_3_ = bf16[1024,256]{1,0:T(8,128)(2,1)S(1)} collective-permute-done((bf16[1024,256]{1,0:T(8,128)(2,1)S(1)}, bf16[1024,256]{1,0:T(8,128)(2,1)S(1)}, u32[]{:S(2)}, u32[]{:S(2)}) %collective-permute-start.3) | collective-permute-done | bytes 524320 | tf_op jit(solution)/shard_map/ppermute | solution.py:399
  17.4 2.0 %collective-permute-start.7 = (bf16[1024,256]{1,0:T(8,128)(2,1)S(1)}, bf16[1024,256]{1,0:T(8,128)(2,1)S(1)}, u32[]{:S(2)}, u32[]{:S(2)}) collective-permute-start(bf16[1024,256]{1,0:T(8,128)(2,1)S(1)} %collective-permute-done.3.refs_3_), channel_id=1, source_target_pairs={{12,4},{20,12},{28,20},{24,28},{16,24},{8,16},{0,8},{4,0},{13,5},{... | collective-permute-start | bytes 1572872 | tf_op jit(solution)/shard_map/ppermute | solution.py:399
  19.4 0.0 collective-permute-done.2.refs_2_
  19.5 9.2 %collective-permute-done.4.refs_4_ = bf16[1024,256]{1,0:T(8,128)(2,1)S(1)} collective-permute-done((bf16[1024,256]{1,0:T(8,128)(2,1)S(1)}, bf16[1024,256]{1,0:T(8,128)(2,1)S(1)}, u32[]{:S(2)}, u32[]{:S(2)}) %collective-permute-start.4) | collective-permute-done | bytes 524320 | tf_op jit(solution)/shard_map/ppermute | solution.py:399
  28.6 2.0 %collective-permute-start.8 = (bf16[1024,256]{1,0:T(8,128)(2,1)S(1)}, bf16[1024,256]{1,0:T(8,128)(2,1)S(1)}, u32[]{:S(2)}, u32[]{:S(2)}) collective-permute-start(bf16[1024,256]{1,0:T(8,128)(2,1)S(1)} %collective-permute-done.4.refs_4_), channel_id=1, source_target_pairs={{12,4},{20,12},{28,20},{24,28},{16,24},{8,16},{0,8},{4,0},{13,5},{... | collective-permute-start | bytes 1572872 | tf_op jit(solution)/shard_map/ppermute | solution.py:399
  30.6 0.0 collective-permute-done.5.refs_5_
  30.7 9.1 %collective-permute-done.7.refs_7_ = bf16[1024,256]{1,0:T(8,128)(2,1)S(1)} collective-permute-done((bf16[1024,256]{1,0:T(8,128)(2,1)S(1)}, bf16[1024,256]{1,0:T(8,128)(2,1)S(1)}, u32[]{:S(2)}, u32[]{:S(2)}) %collective-permute-start.7) | collective-permute-done | bytes 524320 | tf_op jit(solution)/shard_map/ppermute | solution.py:399
  39.8 2.0 %collective-permute-start.11 = (bf16[1024,256]{1,0:T(8,128)(2,1)S(1)}, bf16[1024,256]{1,0:T(8,128)(2,1)S(1)}, u32[]{:S(2)}, u32[]{:S(2)}) collective-permute-start(bf16[1024,256]{1,0:T(8,128)(2,1)S(1)} %collective-permute-done.7.refs_7_), channel_id=1, source_target_pairs={{12,4},{20,12},{28,20},{24,28},{16,24},{8,16},{0,8},{4,0},{13,5},{... | collective-permute-start | bytes 1572872 | tf_op jit(solution)/shard_map/ppermute | solution.py:399
  41.9 9.1 %collective-permute-done.8.refs_8_ = bf16[1024,256]{1,0:T(8,128)(2,1)S(1)} collective-permute-done((bf16[1024,256]{1,0:T(8,128)(2,1)S(1)}, bf16[1024,256]{1,0:T(8,128)(2,1)S(1)}, u32[]{:S(2)}, u32[]{:S(2)}) %collective-permute-start.8) | collective-permute-done | bytes 524320 | tf_op jit(solution)/shard_map/ppermute | solution.py:399
  51.1 2.0 %collective-permute-start.14 = (bf16[1024,256]{1,0:T(8,128)(2,1)S(1)}, bf16[1024,256]{1,0:T(8,128)(2,1)S(1)}, u32[]{:S(2)}, u32[]{:S(2)}) collective-permute-start(bf16[1024,256]{1,0:T(8,128)(2,1)S(1)} %collective-permute-done.8.refs_8_), channel_id=1, source_target_pairs={{12,4},{20,12},{28,20},{24,28},{16,24},{8,16},{0,8},{4,0},{13,5},{... | collective-permute-start | bytes 1572872 | tf_op jit(solution)/shard_map/ppermute | solution.py:399
  53.2 0.7 collect.1
  53.9 2.4 %fold.4.refs_4_ = f32[1024,1536]{1,0:T(8,128)S(1)} custom-call(s32[2,8]{1,0:T(2,128)S(4)} %get-tuple-element.20.codes_ref, bf16[2,8,256,256]{3,2,1,0:T(8,128)(2,1)S(1)} %get-tuple-element.21.ints_ref, bf16[1024,256]{1,0:T(8,128)(2,1)S(1)} %get-tuple-element.22.refs_0_, ...), custom_call_target="tpu_custom_call", output_to_operand_aliasing={{}: (12, {})} | custom-call | flops 2684354560 | bytes 6291456 | tf_op jit(solution)/shard_map/fold/pallas_call | solution.py:340
  56.3 6.0 %collective-permute-done.11.refs_1_ = bf16[1024,256]{1,0:T(8,128)(2,1)S(1)} collective-permute-done((bf16[1024,256]{1,0:T(8,128)(2,1)S(1)}, bf16[1024,256]{1,0:T(8,128)(2,1)S(1)}, u32[]{:S(2)}, u32[]{:S(2)}) %collective-permute-start.11) | collective-permute-done | bytes 524320 | tf_op jit(solution)/shard_map/ppermute | solution.py:399
  62.3 2.1 %collective-permute-done.10.refs_0_ = bf16[1024,256]{1,0:T(8,128)(2,1)S(1)} collective-permute-done((bf16[1024,256]{1,0:T(8,128)(2,1)S(1)}, bf16[1024,256]{1,0:T(8,128)(2,1)S(1)}, u32[]{:S(2)}, u32[]{:S(2)}) %collective-permute-start.10) | collective-permute-done | bytes 524320 | tf_op jit(solution)/shard_map/ppermute | solution.py:399
  64.4 0.1 split.1
  64.5 0.1 collective-permute-start.16
  64.5 2.0 %collective-permute-start.17 = (bf16[768,256]{1,0:T(8,128)(2,1)S(1)}, bf16[768,256]{1,0:T(8,128)(2,1)S(1)}, u32[]{:S(2)}, u32[]{:S(2)}) collective-permute-start(bf16[768,256]{1,0:T(8,128)(2,1)S(1)} %get-tuple-element.31), channel_id=1, source_target_pairs={{12,4},{20,12},{28,20},{24,28},{16,24},{8,16},{0,8},{4,0},{13,5},{... | collective-permute-start | bytes 1179656 | tf_op jit(solution)/shard_map/ppermute | solution.py:404
  66.5 0.1 collective-permute-start.12
  66.6 6.9 %collective-permute-done.14.refs_2_ = bf16[1024,256]{1,0:T(8,128)(2,1)S(1)} collective-permute-done((bf16[1024,256]{1,0:T(8,128)(2,1)S(1)}, bf16[1024,256]{1,0:T(8,128)(2,1)S(1)}, u32[]{:S(2)}, u32[]{:S(2)}) %collective-permute-start.14) | collective-permute-done | bytes 524320 | tf_op jit(solution)/shard_map/ppermute | solution.py:399
  73.5 2.0 %collective-permute-start.13 = (bf16[256,256]{1,0:T(8,128)(2,1)S(1)}, bf16[256,256]{1,0:T(8,128)(2,1)S(1)}, u32[]{:S(2)}, u32[]{:S(2)}) collective-permute-start(bf16[256,256]{1,0:T(8,128)(2,1)S(1)} %get-tuple-element.28), channel_id=1, source_target_pairs={{12,4},{20,12},{28,20},{24,28},{16,24},{8,16},{0,8},{4,0},{13,5},{... | collective-permute-start | bytes 393224 | tf_op jit(solution)/shard_map/ppermute | solution.py:404
  75.6 2.9 %fold.5 = (f32[1024,1536]{1,0:T(8,128)S(1)}, f32[1024,1536]{1,0:T(8,128)}) custom-call(s32[2,8]{1,0:T(2,128)S(4)} %get-tuple-element.20.codes_ref, bf16[2,8,256,256]{3,2,1,0:T(8,128)(2,1)S(1)} %get-tuple-element.21.ints_ref, bf16[1024,256]{1,0:T(8,128)(2,1)S(1)} %collective-permute-done.10.refs_0_, ...), custom_call_target="tpu_custom_call", output_to_operand_aliasing={{0}: (6, {})} | custom-call | flops 1073741824 | bytes 6291456 | tf_op jit(solution)/shard_map/fold/pallas_call | solution.py:340
  78.5 5.5 %collective-permute-done.16.refs_0_ = bf16[768,256]{1,0:T(8,128)(2,1)S(1)} collective-permute-done((bf16[768,256]{1,0:T(8,128)(2,1)S(1)}, bf16[768,256]{1,0:T(8,128)(2,1)S(1)}, u32[]{:S(2)}, u32[]{:S(2)}) %collective-permute-start.16) | collective-permute-done | bytes 393248 | tf_op jit(solution)/shard_map/ppermute | solution.py:404
  84.1 1.2 %fold.6.refs_3_ = f32[1024,1536]{1,0:T(8,128)} custom-call(s32[2,8]{1,0:T(2,128)S(4)} %get-tuple-element.20.codes_ref, bf16[2,8,256,256]{3,2,1,0:T(8,128)(2,1)S(1)} %get-tuple-element.21.ints_ref, bf16[768,256]{1,0:T(8,128)(2,1)S(1)} %collective-permute-done.16.refs_0_, ...), custom_call_target="tpu_custom_call", output_to_operand_aliasing={{}: (5, {})} | custom-call | flops 402653184 | bytes 4718592 | tf_op jit(solution)/shard_map/fold/pallas_call | solution.py:340
  85.3 0.8 collective-permute-done.12.refs_0_
  86.1 0.9 %fold.7 = f32[1024,1536]{1,0:T(8,128)} custom-call(s32[2,8]{1,0:T(2,128)S(4)} %get-tuple-element.20.codes_ref, bf16[2,8,256,256]{3,2,1,0:T(8,128)(2,1)S(1)} %get-tuple-element.21.ints_ref, bf16[256,256]{1,0:T(8,128)(2,1)S(1)} %collective-permute-done.12.refs_0_, ...), custom_call_target="tpu_custom_call", output_to_operand_aliasing={{}: (5, {})} | custom-call | flops 134217728 | bytes 1572864 | tf_op jit(solution)/shard_map/fold/pallas_call | solution.py:340
  (12 shorter events, 0.2 us)
Async XLA Ops:
  1.5 3.2 %collective-permute-start = (bf16[1040,256]{1,0:T(8,128)(2,1)S(1)}, bf16[1040,256]{1,0:T(8,128)(2,1)S(1)}, u32[]{:S(2)}, u32[]{:S(2)}) collective-permute-start(bf16[1040,256]{1,0:T(8,128)(2,1)S(1)} %get-tuple-element.19.refs_0_), channel_id=1, source_target_pairs={{0,1},{1,0},{2,3},{3,2},{4,5},{5,4},{6,7},{7,6},{8,9},{9,8},{10,11... | collective-permute-start | bytes 1597448 | tf_op jit(solution)/shard_map/ppermute | solution.py:370
  2.0 15.3 %collective-permute-start.3 = (bf16[1024,256]{1,0:T(8,128)(2,1)S(1)}, bf16[1024,256]{1,0:T(8,128)(2,1)S(1)}, u32[]{:S(2)}, u32[]{:S(2)}) collective-permute-start(bf16[1024,256]{1,0:T(8,128)(2,1)S(1)} %get-tuple-element.23.refs_1_), channel_id=1, source_target_pairs={{12,4},{20,12},{28,20},{24,28},{16,24},{8,16},{0,8},{4,0},{13,5},{... | collective-permute-start | bytes 1572872 | tf_op jit(solution)/shard_map/ppermute | solution.py:399
  4.7 14.8 %collective-permute-start.2 = (bf16[1024,256]{1,0:T(8,128)(2,1)S(1)}, bf16[1024,256]{1,0:T(8,128)(2,1)S(1)}, u32[]{:S(2)}, u32[]{:S(2)}) collective-permute-start(bf16[1024,256]{1,0:T(8,128)(2,1)S(1)} %get-tuple-element.22.refs_0_), channel_id=1, source_target_pairs={{4,12},{12,20},{20,28},{28,24},{24,16},{16,8},{8,0},{0,4},{5,13},{... | collective-permute-start | bytes 1572872 | tf_op jit(solution)/shard_map/ppermute | solution.py:399
  4.8 48.4 %collective-permute-start.1 = (bf16[2080,256]{1,0:T(8,128)(2,1)S(1)}, bf16[2080,256]{1,0:T(8,128)(2,1)S(1)}, u32[]{:S(2)}, u32[]{:S(2)}) collective-permute-start(bf16[2080,256]{1,0:T(8,128)(2,1)S(1)} %join.1.refs_0_), channel_id=1, source_target_pairs={{0,2},{1,3},{2,0},{3,1},{4,6},{5,7},{6,4},{7,5},{8,10},{9,11},{10,... | collective-permute-start | bytes 3194888 | tf_op jit(solution)/shard_map/ppermute | solution.py:373
  6.8 21.8 %collective-permute-start.4 = (bf16[1024,256]{1,0:T(8,128)(2,1)S(1)}, bf16[1024,256]{1,0:T(8,128)(2,1)S(1)}, u32[]{:S(2)}, u32[]{:S(2)}) collective-permute-start(bf16[1024,256]{1,0:T(8,128)(2,1)S(1)} %get-tuple-element.22.refs_0_), channel_id=1, source_target_pairs={{12,4},{20,12},{28,20},{24,28},{16,24},{8,16},{0,8},{4,0},{13,5},{... | collective-permute-start | bytes 1572872 | tf_op jit(solution)/shard_map/ppermute | solution.py:399
  8.4 22.3 %collective-permute-start.5 = (bf16[1024,256]{1,0:T(8,128)(2,1)S(1)}, bf16[1024,256]{1,0:T(8,128)(2,1)S(1)}, u32[]{:S(2)}, u32[]{:S(2)}) collective-permute-start(bf16[1024,256]{1,0:T(8,128)(2,1)S(1)} %get-tuple-element.23.refs_1_), channel_id=1, source_target_pairs={{4,12},{12,20},{20,28},{28,24},{24,16},{16,8},{8,0},{0,4},{5,13},{... | collective-permute-start | bytes 1572872 | tf_op jit(solution)/shard_map/ppermute | solution.py:399
  17.4 22.5 %collective-permute-start.7 = (bf16[1024,256]{1,0:T(8,128)(2,1)S(1)}, bf16[1024,256]{1,0:T(8,128)(2,1)S(1)}, u32[]{:S(2)}, u32[]{:S(2)}) collective-permute-start(bf16[1024,256]{1,0:T(8,128)(2,1)S(1)} %collective-permute-done.3.refs_3_), channel_id=1, source_target_pairs={{12,4},{20,12},{28,20},{24,28},{16,24},{8,16},{0,8},{4,0},{13,5},{... | collective-permute-start | bytes 1572872 | tf_op jit(solution)/shard_map/ppermute | solution.py:399
  19.4 22.5 %collective-permute-start.6 = (bf16[1024,256]{1,0:T(8,128)(2,1)S(1)}, bf16[1024,256]{1,0:T(8,128)(2,1)S(1)}, u32[]{:S(2)}, u32[]{:S(2)}) collective-permute-start(bf16[1024,256]{1,0:T(8,128)(2,1)S(1)} %collective-permute-done.2.refs_2_), channel_id=1, source_target_pairs={{4,12},{12,20},{20,28},{28,24},{24,16},{16,8},{8,0},{0,4},{5,13},{... | collective-permute-start | bytes 1572872 | tf_op jit(solution)/shard_map/ppermute | solution.py:399
  28.6 22.5 %collective-permute-start.8 = (bf16[1024,256]{1,0:T(8,128)(2,1)S(1)}, bf16[1024,256]{1,0:T(8,128)(2,1)S(1)}, u32[]{:S(2)}, u32[]{:S(2)}) collective-permute-start(bf16[1024,256]{1,0:T(8,128)(2,1)S(1)} %collective-permute-done.4.refs_4_), channel_id=1, source_target_pairs={{12,4},{20,12},{28,20},{24,28},{16,24},{8,16},{0,8},{4,0},{13,5},{... | collective-permute-start | bytes 1572872 | tf_op jit(solution)/shard_map/ppermute | solution.py:399
  30.7 22.5 %collective-permute-start.9 = (bf16[1024,256]{1,0:T(8,128)(2,1)S(1)}, bf16[1024,256]{1,0:T(8,128)(2,1)S(1)}, u32[]{:S(2)}, u32[]{:S(2)}) collective-permute-start(bf16[1024,256]{1,0:T(8,128)(2,1)S(1)} %collective-permute-done.5.refs_5_), channel_id=1, source_target_pairs={{4,12},{12,20},{20,28},{28,24},{24,16},{16,8},{8,0},{0,4},{5,13},{... | collective-permute-start | bytes 1572872 | tf_op jit(solution)/shard_map/ppermute | solution.py:399
  39.8 22.5 %collective-permute-start.11 = (bf16[1024,256]{1,0:T(8,128)(2,1)S(1)}, bf16[1024,256]{1,0:T(8,128)(2,1)S(1)}, u32[]{:S(2)}, u32[]{:S(2)}) collective-permute-start(bf16[1024,256]{1,0:T(8,128)(2,1)S(1)} %collective-permute-done.7.refs_7_), channel_id=1, source_target_pairs={{12,4},{20,12},{28,20},{24,28},{16,24},{8,16},{0,8},{4,0},{13,5},{... | collective-permute-start | bytes 1572872 | tf_op jit(solution)/shard_map/ppermute | solution.py:399
  41.9 22.5 %collective-permute-start.10 = (bf16[1024,256]{1,0:T(8,128)(2,1)S(1)}, bf16[1024,256]{1,0:T(8,128)(2,1)S(1)}, u32[]{:S(2)}, u32[]{:S(2)}) collective-permute-start(bf16[1024,256]{1,0:T(8,128)(2,1)S(1)} %collective-permute-done.6.refs_6_), channel_id=1, source_target_pairs={{4,12},{12,20},{20,28},{28,24},{24,16},{16,8},{8,0},{0,4},{5,13},{... | collective-permute-start | bytes 1572872 | tf_op jit(solution)/shard_map/ppermute | solution.py:399
  51.1 22.5 %collective-permute-start.14 = (bf16[1024,256]{1,0:T(8,128)(2,1)S(1)}, bf16[1024,256]{1,0:T(8,128)(2,1)S(1)}, u32[]{:S(2)}, u32[]{:S(2)}) collective-permute-start(bf16[1024,256]{1,0:T(8,128)(2,1)S(1)} %collective-permute-done.8.refs_8_), channel_id=1, source_target_pairs={{12,4},{20,12},{28,20},{24,28},{16,24},{8,16},{0,8},{4,0},{13,5},{... | collective-permute-start | bytes 1572872 | tf_op jit(solution)/shard_map/ppermute | solution.py:399
  53.2 22.5 %collective-permute-start.15 = (bf16[1024,256]{1,0:T(8,128)(2,1)S(1)}, bf16[1024,256]{1,0:T(8,128)(2,1)S(1)}, u32[]{:S(2)}, u32[]{:S(2)}) collective-permute-start(bf16[1024,256]{1,0:T(8,128)(2,1)S(1)} %collective-permute-done.9.refs_9_), channel_id=1, source_target_pairs={{4,12},{12,20},{20,28},{28,24},{24,16},{16,8},{8,0},{0,4},{5,13},{... | collective-permute-start | bytes 1572872 | tf_op jit(solution)/shard_map/ppermute | solution.py:399
  64.5 19.6 %collective-permute-start.16 = (bf16[768,256]{1,0:T(8,128)(2,1)S(1)}, bf16[768,256]{1,0:T(8,128)(2,1)S(1)}, u32[]{:S(2)}, u32[]{:S(2)}) collective-permute-start(bf16[768,256]{1,0:T(8,128)(2,1)S(1)} %get-tuple-element.30), channel_id=1, source_target_pairs={{4,12},{12,20},{20,28},{28,24},{24,16},{16,8},{8,0},{0,4},{5,13},{... | collective-permute-start | bytes 1179656 | tf_op jit(solution)/shard_map/ppermute | solution.py:404
  64.5 19.5 %collective-permute-start.17 = (bf16[768,256]{1,0:T(8,128)(2,1)S(1)}, bf16[768,256]{1,0:T(8,128)(2,1)S(1)}, u32[]{:S(2)}, u32[]{:S(2)}) collective-permute-start(bf16[768,256]{1,0:T(8,128)(2,1)S(1)} %get-tuple-element.31), channel_id=1, source_target_pairs={{12,4},{20,12},{28,20},{24,28},{16,24},{8,16},{0,8},{4,0},{13,5},{... | collective-permute-start | bytes 1179656 | tf_op jit(solution)/shard_map/ppermute | solution.py:404
  66.5 19.5 %collective-permute-start.12 = (bf16[256,256]{1,0:T(8,128)(2,1)S(1)}, bf16[256,256]{1,0:T(8,128)(2,1)S(1)}, u32[]{:S(2)}, u32[]{:S(2)}) collective-permute-start(bf16[256,256]{1,0:T(8,128)(2,1)S(1)} %get-tuple-element.27), channel_id=1, source_target_pairs={{4,12},{12,20},{20,28},{28,24},{24,16},{16,8},{8,0},{0,4},{5,13},{... | collective-permute-start | bytes 393224 | tf_op jit(solution)/shard_map/ppermute | solution.py:404
  73.5 12.5 %collective-permute-start.13 = (bf16[256,256]{1,0:T(8,128)(2,1)S(1)}, bf16[256,256]{1,0:T(8,128)(2,1)S(1)}, u32[]{:S(2)}, u32[]{:S(2)}) collective-permute-start(bf16[256,256]{1,0:T(8,128)(2,1)S(1)} %get-tuple-element.28), channel_id=1, source_target_pairs={{12,4},{20,12},{28,20},{24,28},{16,24},{8,16},{0,8},{4,0},{13,5},{... | collective-permute-start | bytes 393224 | tf_op jit(solution)/shard_map/ppermute | solution.py:404

commit v7 on v6

--- a/solution.py
+++ b/solution.py
@@ -398,7 +398,7 @@
             if hop < far - 1 or far - 1 <= n_row - 1 - far or one in lead:
                 held[one] = lax.ppermute(held[one], "row", ways[one[0]])
                 have.append((tag(*one, hop), held[one]))
-    last = [lax.optimization_barrier((early, held[one]))[1] for one in lead]
+    last = [held[one] for one in lead]
     pieces = split(last)
     later = [tag(*one, far) for one in lead]
     ends = [[lax.ppermute(part, "row", ways[one[0]]) for one, part in zip(lead, piece)] for piece in pieces]

time: 87.3 us -> 87 us (level)
  no operation moved by 1% of the time
where the time goes in v7:
time: 87 us; the launch traced here: 86.6 us
  waiting for transfers between devices  57.9 us (67%)
  starting transfers between devices  19.2 us (22%)
  Pallas kernels  9.46 us (11%)
    ppermute x12, waiting for transfers between devices, body(): held[one] = lax.ppermute(held[one], 'row', ways[one[0]])  51.7 us
    ppermute x12, starting transfers between devices, body(): held[one] = lax.ppermute(held[one], 'row', ways[one[0]])  13.4 us
    pallas_call x4, Pallas kernels, fold(): pl.pallas_call(functools.partial(fold_kernel, first, hops, later, order,...  7.11 us
    ppermute x4, waiting for transfers between devices, body(): lax.ppermute(part, 'row', ways[one[0]])  6.18 us
    ppermute x4, starting transfers between devices, body(): lax.ppermute(part, 'row', ways[one[0]])  3.79 us
    ppermute x1, starting transfers between devices, body(): lax.ppermute(moved, 'col', [(c, (c + shift * CORES) % n_col) for c in ran...  2.01 us
  transfers between devices with their start and end apart: 18, of which 9 were waited for; matrix products, arithmetic and copies ran while one was open for 0% of the time, Pallas kernels for 8%

profile of v7, /device:TPU:0, one launch (start us, length us, event | category | flops | bytes accessed | tf_op | source)
XLA Modules:
  0.0 86.6 jit_solution(16032966015206792762)
XLA Ops:
  0.0 1.5 %place.1 = (bf16[1024,256]{1,0:T(8,128)(2,1)S(1)}, bf16[1024,256]{1,0:T(8,128)(2,1)S(1)}, bf16[1040,256]{1,0:T(8,128)(2,1)S(1)}) custom-call(s32[2,1,4]{2,1,0:T(1,128)} %rows_hbm.1, s32[2,1,2]{2,1,0:T(1,128)} %bitcast.3, bf16[2,1,4,256,256]{4,3,2,1,0:T(8,128)(2,1)} %tiles_hbm.1, bf16[2,2,1,256,256]{4,3,2,1,0:T(8,128)(2,1)} %ints_hbm.1), custom_call_target="tpu_custom_call" | custom-call | tf_op jit(solution)/shard_map/place/pallas_call | solution.py:105
  1.5 3.0 %collective-permute-start.2 = (bf16[1024,256]{1,0:T(8,128)(2,1)S(1)}, bf16[1024,256]{1,0:T(8,128)(2,1)S(1)}, u32[]{:S(2)}, u32[]{:S(2)}) collective-permute-start(bf16[1024,256]{1,0:T(8,128)(2,1)S(1)} %get-tuple-element.20.refs_0_), channel_id=1, source_target_pairs={{4,12},{12,20},{20,28},{28,24},{24,16},{16,8},{8,0},{0,4},{5,13},{... | collective-permute-start | bytes 1572872 | tf_op jit(solution)/shard_map/ppermute | solution.py:399
  4.5 0.2 collective-permute-start.5
  4.7 2.0 %collective-permute-start.10 = (bf16[1024,256]{1,0:T(8,128)(2,1)S(1)}, bf16[1024,256]{1,0:T(8,128)(2,1)S(1)}, u32[]{:S(2)}, u32[]{:S(2)}) collective-permute-start(bf16[1024,256]{1,0:T(8,128)(2,1)S(1)} %get-tuple-element.20.refs_0_), channel_id=1, source_target_pairs={{12,4},{20,12},{28,20},{24,28},{16,24},{8,16},{0,8},{4,0},{13,5},{... | collective-permute-start | bytes 1572872 | tf_op jit(solution)/shard_map/ppermute | solution.py:399
  6.7 10.7 %collective-permute-done.2.refs_2_ = bf16[1024,256]{1,0:T(8,128)(2,1)S(1)} collective-permute-done((bf16[1024,256]{1,0:T(8,128)(2,1)S(1)}, bf16[1024,256]{1,0:T(8,128)(2,1)S(1)}, u32[]{:S(2)}, u32[]{:S(2)}) %collective-permute-start.2) | collective-permute-done | bytes 524320 | tf_op jit(solution)/shard_map/ppermute | solution.py:399
  17.4 2.0 %collective-permute-start.3 = (bf16[1024,256]{1,0:T(8,128)(2,1)S(1)}, bf16[1024,256]{1,0:T(8,128)(2,1)S(1)}, u32[]{:S(2)}, u32[]{:S(2)}) collective-permute-start(bf16[1024,256]{1,0:T(8,128)(2,1)S(1)} %collective-permute-done.2.refs_2_), channel_id=1, source_target_pairs={{4,12},{12,20},{20,28},{28,24},{24,16},{16,8},{8,0},{0,4},{5,13},{... | collective-permute-start | bytes 1572872 | tf_op jit(solution)/shard_map/ppermute | solution.py:399
  19.4 0.1 collective-permute-start.6
  19.5 0.1 join.1.refs_0_
  19.6 2.0 %collective-permute-start.1 = (bf16[2080,256]{1,0:T(8,128)(2,1)S(1)}, bf16[2080,256]{1,0:T(8,128)(2,1)S(1)}, u32[]{:S(2)}, u32[]{:S(2)}) collective-permute-start(bf16[2080,256]{1,0:T(8,128)(2,1)S(1)} %join.1.refs_0_), channel_id=1, source_target_pairs={{0,2},{1,3},{2,0},{3,1},{4,6},{5,7},{6,4},{7,5},{8,10},{9,11},{10,... | collective-permute-start | bytes 3194888 | tf_op jit(solution)/shard_map/ppermute | solution.py:373
  21.6 9.0 %collective-permute-done.10.refs_4_ = bf16[1024,256]{1,0:T(8,128)(2,1)S(1)} collective-permute-done((bf16[1024,256]{1,0:T(8,128)(2,1)S(1)}, bf16[1024,256]{1,0:T(8,128)(2,1)S(1)}, u32[]{:S(2)}, u32[]{:S(2)}) %collective-permute-start.10) | collective-permute-done | bytes 524320 | tf_op jit(solution)/shard_map/ppermute | solution.py:399
  30.6 0.1 collective-permute-start.11
  30.7 1.9 %collective-permute-start.14 = (bf16[1024,256]{1,0:T(8,128)(2,1)S(1)}, bf16[1024,256]{1,0:T(8,128)(2,1)S(1)}, u32[]{:S(2)}, u32[]{:S(2)}) collective-permute-start(bf16[1024,256]{1,0:T(8,128)(2,1)S(1)} %collective-permute-done.13.refs_5_), channel_id=1, source_target_pairs={{4,12},{12,20},{20,28},{28,24},{24,16},{16,8},{8,0},{0,4},{5,13},{... | collective-permute-start | bytes 1572872 | tf_op jit(solution)/shard_map/ppermute | solution.py:399
  32.6 7.2 %collective-permute-done.3.refs_6_ = bf16[1024,256]{1,0:T(8,128)(2,1)S(1)} collective-permute-done((bf16[1024,256]{1,0:T(8,128)(2,1)S(1)}, bf16[1024,256]{1,0:T(8,128)(2,1)S(1)}, u32[]{:S(2)}, u32[]{:S(2)}) %collective-permute-start.3) | collective-permute-done | bytes 524320 | tf_op jit(solution)/shard_map/ppermute | solution.py:399
  39.8 2.0 %collective-permute-start.4 = (bf16[1024,256]{1,0:T(8,128)(2,1)S(1)}, bf16[1024,256]{1,0:T(8,128)(2,1)S(1)}, u32[]{:S(2)}, u32[]{:S(2)}) collective-permute-start(bf16[1024,256]{1,0:T(8,128)(2,1)S(1)} %collective-permute-done.3.refs_6_), channel_id=1, source_target_pairs={{4,12},{12,20},{20,28},{28,24},{24,16},{16,8},{8,0},{0,4},{5,13},{... | collective-permute-start | bytes 1572872 | tf_op jit(solution)/shard_map/ppermute | solution.py:399
  41.8 0.1 collective-permute-start.7
  41.9 11.1 %collective-permute-done.11.refs_8_ = bf16[1024,256]{1,0:T(8,128)(2,1)S(1)} collective-permute-done((bf16[1024,256]{1,0:T(8,128)(2,1)S(1)}, bf16[1024,256]{1,0:T(8,128)(2,1)S(1)}, u32[]{:S(2)}, u32[]{:S(2)}) %collective-permute-start.11) | collective-permute-done | bytes 524320 | tf_op jit(solution)/shard_map/ppermute | solution.py:399
  53.1 0.1 collective-permute-start.12
  53.2 1.9 %collective-permute-start.15 = (bf16[1024,256]{1,0:T(8,128)(2,1)S(1)}, bf16[1024,256]{1,0:T(8,128)(2,1)S(1)}, u32[]{:S(2)}, u32[]{:S(2)}) collective-permute-start(bf16[1024,256]{1,0:T(8,128)(2,1)S(1)} %collective-permute-done.14.refs_9_), channel_id=1, source_target_pairs={{4,12},{12,20},{20,28},{28,24},{24,16},{16,8},{8,0},{0,4},{5,13},{... | collective-permute-start | bytes 1572872 | tf_op jit(solution)/shard_map/ppermute | solution.py:399
  55.1 7.2 %collective-permute-done.4.refs_0_ = bf16[1024,256]{1,0:T(8,128)(2,1)S(1)} collective-permute-done((bf16[1024,256]{1,0:T(8,128)(2,1)S(1)}, bf16[1024,256]{1,0:T(8,128)(2,1)S(1)}, u32[]{:S(2)}, u32[]{:S(2)}) %collective-permute-start.4) | collective-permute-done | bytes 524320 | tf_op jit(solution)/shard_map/ppermute | solution.py:399
  62.3 2.0 %collective-permute-done.7.refs_1_ = bf16[1024,256]{1,0:T(8,128)(2,1)S(1)} collective-permute-done((bf16[1024,256]{1,0:T(8,128)(2,1)S(1)}, bf16[1024,256]{1,0:T(8,128)(2,1)S(1)}, u32[]{:S(2)}, u32[]{:S(2)}) %collective-permute-start.7) | collective-permute-done | bytes 524320 | tf_op jit(solution)/shard_map/ppermute | solution.py:399
  64.4 1.6 %collective-permute-start.16 = (bf16[768,256]{1,0:T(8,128)(2,1)S(1)}, bf16[768,256]{1,0:T(8,128)(2,1)S(1)}, u32[]{:S(2)}, u32[]{:S(2)}) collective-permute-start(bf16[768,256]{1,0:T(8,128)(2,1)S(1)} %get-tuple-element.26), channel_id=1, source_target_pairs={{4,12},{12,20},{20,28},{28,24},{24,16},{16,8},{8,0},{0,4},{5,13},{... | collective-permute-start | bytes 1179656 | tf_op jit(solution)/shard_map/ppermute | solution.py:404
  66.0 0.4 collective-permute-start.17
  66.5 1.6 %collective-permute-start.8 = (bf16[256,256]{1,0:T(8,128)(2,1)S(1)}, bf16[256,256]{1,0:T(8,128)(2,1)S(1)}, u32[]{:S(2)}, u32[]{:S(2)}) collective-permute-start(bf16[256,256]{1,0:T(8,128)(2,1)S(1)} %get-tuple-element.22), channel_id=1, source_target_pairs={{4,12},{12,20},{20,28},{28,24},{24,16},{16,8},{8,0},{0,4},{5,13},{... | collective-permute-start | bytes 393224 | tf_op jit(solution)/shard_map/ppermute | solution.py:404
  68.0 0.7 collect.1
  68.7 2.4 %fold.4.refs_4_ = f32[1024,1536]{1,0:T(8,128)S(1)} custom-call(s32[2,8]{1,0:T(2,128)S(4)} %get-tuple-element.18.codes_ref, bf16[2,8,256,256]{3,2,1,0:T(8,128)(2,1)S(1)} %get-tuple-element.19.ints_ref, bf16[1024,256]{1,0:T(8,128)(2,1)S(1)} %get-tuple-element.20.refs_0_, ...), custom_call_target="tpu_custom_call", output_to_operand_aliasing={{}: (12, {})} | custom-call | flops 2684354560 | bytes 6291456 | tf_op jit(solution)/shard_map/fold/pallas_call | solution.py:340
  71.1 4.4 %collective-permute-done.12.refs_2_ = bf16[1024,256]{1,0:T(8,128)(2,1)S(1)} collective-permute-done((bf16[1024,256]{1,0:T(8,128)(2,1)S(1)}, bf16[1024,256]{1,0:T(8,128)(2,1)S(1)}, u32[]{:S(2)}, u32[]{:S(2)}) %collective-permute-start.12) | collective-permute-done | bytes 524320 | tf_op jit(solution)/shard_map/ppermute | solution.py:399
  75.5 0.1 collective-permute-start.9
  75.7 2.1 %fold.5 = (f32[1024,1536]{1,0:T(8,128)S(1)}, f32[1024,1536]{1,0:T(8,128)}) custom-call(s32[2,8]{1,0:T(2,128)S(4)} %get-tuple-element.18.codes_ref, bf16[2,8,256,256]{3,2,1,0:T(8,128)(2,1)S(1)} %get-tuple-element.19.ints_ref, bf16[1024,256]{1,0:T(8,128)(2,1)S(1)} %collective-permute-done.4.refs_0_, ...), custom_call_target="tpu_custom_call", output_to_operand_aliasing={{0}: (6, {})} | custom-call | flops 1073741824 | bytes 6291456 | tf_op jit(solution)/shard_map/fold/pallas_call | solution.py:340
  77.7 4.2 %collective-permute-done.16.refs_0_ = bf16[768,256]{1,0:T(8,128)(2,1)S(1)} collective-permute-done((bf16[768,256]{1,0:T(8,128)(2,1)S(1)}, bf16[768,256]{1,0:T(8,128)(2,1)S(1)}, u32[]{:S(2)}, u32[]{:S(2)}) %collective-permute-start.16) | collective-permute-done | bytes 393248 | tf_op jit(solution)/shard_map/ppermute | solution.py:404
  82.0 1.9 %collective-permute-done.17.refs_1_ = bf16[768,256]{1,0:T(8,128)(2,1)S(1)} collective-permute-done((bf16[768,256]{1,0:T(8,128)(2,1)S(1)}, bf16[768,256]{1,0:T(8,128)(2,1)S(1)}, u32[]{:S(2)}, u32[]{:S(2)}) %collective-permute-start.17) | collective-permute-done | bytes 393248 | tf_op jit(solution)/shard_map/ppermute | solution.py:404
  83.9 1.5 %fold.6.refs_3_ = f32[1024,1536]{1,0:T(8,128)} custom-call(s32[2,8]{1,0:T(2,128)S(4)} %get-tuple-element.18.codes_ref, bf16[2,8,256,256]{3,2,1,0:T(8,128)(2,1)S(1)} %get-tuple-element.19.ints_ref, bf16[768,256]{1,0:T(8,128)(2,1)S(1)} %collective-permute-done.16.refs_0_, ...), custom_call_target="tpu_custom_call", output_to_operand_aliasing={{}: (5, {})} | custom-call | flops 402653184 | bytes 4718592 | tf_op jit(solution)/shard_map/fold/pallas_call | solution.py:340
  85.4 1.2 %fold.7 = f32[1024,1536]{1,0:T(8,128)} custom-call(s32[2,8]{1,0:T(2,128)S(4)} %get-tuple-element.18.codes_ref, bf16[2,8,256,256]{3,2,1,0:T(8,128)(2,1)S(1)} %get-tuple-element.19.ints_ref, bf16[256,256]{1,0:T(8,128)(2,1)S(1)} %collective-permute-done.8.refs_0_, bf16[256,256]{1,0:T(8,128)(2,1)S(1)} %collective-permute-done.9.refs_1_, ...), custom_call_target="tpu_custom_call", output_to_operand_aliasing={{}: (5, {})} | custom-call | flops 134217728 | bytes 1572864 | tf_op jit(solution)/shard_map/fold/pallas_call | solution.py:340
  (12 shorter events, 0.2 us)
Async XLA Ops:
  1.5 15.8 %collective-permute-start.2 = (bf16[1024,256]{1,0:T(8,128)(2,1)S(1)}, bf16[1024,256]{1,0:T(8,128)(2,1)S(1)}, u32[]{:S(2)}, u32[]{:S(2)}) collective-permute-start(bf16[1024,256]{1,0:T(8,128)(2,1)S(1)} %get-tuple-element.20.refs_0_), channel_id=1, source_target_pairs={{4,12},{12,20},{20,28},{28,24},{24,16},{16,8},{8,0},{0,4},{5,13},{... | collective-permute-start | bytes 1572872 | tf_op jit(solution)/shard_map/ppermute | solution.py:399
  4.5 14.8 %collective-permute-start.5 = (bf16[1024,256]{1,0:T(8,128)(2,1)S(1)}, bf16[1024,256]{1,0:T(8,128)(2,1)S(1)}, u32[]{:S(2)}, u32[]{:S(2)}) collective-permute-start(bf16[1024,256]{1,0:T(8,128)(2,1)S(1)} %get-tuple-element.21.refs_1_), channel_id=1, source_target_pairs={{12,4},{20,12},{28,20},{24,28},{16,24},{8,16},{0,8},{4,0},{13,5},{... | collective-permute-start | bytes 1572872 | tf_op jit(solution)/shard_map/ppermute | solution.py:399
  4.7 14.8 %collective-permute-start = (bf16[1040,256]{1,0:T(8,128)(2,1)S(1)}, bf16[1040,256]{1,0:T(8,128)(2,1)S(1)}, u32[]{:S(2)}, u32[]{:S(2)}) collective-permute-start(bf16[1040,256]{1,0:T(8,128)(2,1)S(1)} %get-tuple-element.17.refs_0_), channel_id=1, source_target_pairs={{0,1},{1,0},{2,3},{3,2},{4,5},{5,4},{6,7},{7,6},{8,9},{9,8},{10,11... | collective-permute-start | bytes 1597448 | tf_op jit(solution)/shard_map/ppermute | solution.py:370
  4.7 25.9 %collective-permute-start.10 = (bf16[1024,256]{1,0:T(8,128)(2,1)S(1)}, bf16[1024,256]{1,0:T(8,128)(2,1)S(1)}, u32[]{:S(2)}, u32[]{:S(2)}) collective-permute-start(bf16[1024,256]{1,0:T(8,128)(2,1)S(1)} %get-tuple-element.20.refs_0_), channel_id=1, source_target_pairs={{12,4},{20,12},{28,20},{24,28},{16,24},{8,16},{0,8},{4,0},{13,5},{... | collective-permute-start | bytes 1572872 | tf_op jit(solution)/shard_map/ppermute | solution.py:399
  6.6 24.1 %collective-permute-start.13 = (bf16[1024,256]{1,0:T(8,128)(2,1)S(1)}, bf16[1024,256]{1,0:T(8,128)(2,1)S(1)}, u32[]{:S(2)}, u32[]{:S(2)}) collective-permute-start(bf16[1024,256]{1,0:T(8,128)(2,1)S(1)} %get-tuple-element.21.refs_1_), channel_id=1, source_target_pairs={{4,12},{12,20},{20,28},{28,24},{24,16},{16,8},{8,0},{0,4},{5,13},{... | collective-permute-start | bytes 1572872 | tf_op jit(solution)/shard_map/ppermute | solution.py:399
  17.4 22.5 %collective-permute-start.3 = (bf16[1024,256]{1,0:T(8,128)(2,1)S(1)}, bf16[1024,256]{1,0:T(8,128)(2,1)S(1)}, u32[]{:S(2)}, u32[]{:S(2)}) collective-permute-start(bf16[1024,256]{1,0:T(8,128)(2,1)S(1)} %collective-permute-done.2.refs_2_), channel_id=1, source_target_pairs={{4,12},{12,20},{20,28},{28,24},{24,16},{16,8},{8,0},{0,4},{5,13},{... | collective-permute-start | bytes 1572872 | tf_op jit(solution)/shard_map/ppermute | solution.py:399
  19.4 22.5 %collective-permute-start.6 = (bf16[1024,256]{1,0:T(8,128)(2,1)S(1)}, bf16[1024,256]{1,0:T(8,128)(2,1)S(1)}, u32[]{:S(2)}, u32[]{:S(2)}) collective-permute-start(bf16[1024,256]{1,0:T(8,128)(2,1)S(1)} %collective-permute-done.5.refs_3_), channel_id=1, source_target_pairs={{12,4},{20,12},{28,20},{24,28},{16,24},{8,16},{0,8},{4,0},{13,5},{... | collective-permute-start | bytes 1572872 | tf_op jit(solution)/shard_map/ppermute | solution.py:399
  19.6 46.9 %collective-permute-start.1 = (bf16[2080,256]{1,0:T(8,128)(2,1)S(1)}, bf16[2080,256]{1,0:T(8,128)(2,1)S(1)}, u32[]{:S(2)}, u32[]{:S(2)}) collective-permute-start(bf16[2080,256]{1,0:T(8,128)(2,1)S(1)} %join.1.refs_0_), channel_id=1, source_target_pairs={{0,2},{1,3},{2,0},{3,1},{4,6},{5,7},{6,4},{7,5},{8,10},{9,11},{10,... | collective-permute-start | bytes 3194888 | tf_op jit(solution)/shard_map/ppermute | solution.py:373
  30.6 22.5 %collective-permute-start.11 = (bf16[1024,256]{1,0:T(8,128)(2,1)S(1)}, bf16[1024,256]{1,0:T(8,128)(2,1)S(1)}, u32[]{:S(2)}, u32[]{:S(2)}) collective-permute-start(bf16[1024,256]{1,0:T(8,128)(2,1)S(1)} %collective-permute-done.10.refs_4_), channel_id=1, source_target_pairs={{12,4},{20,12},{28,20},{24,28},{16,24},{8,16},{0,8},{4,0},{13,5},{... | collective-permute-start | bytes 1572872 | tf_op jit(solution)/shard_map/ppermute | solution.py:399
  30.7 22.5 %collective-permute-start.14 = (bf16[1024,256]{1,0:T(8,128)(2,1)S(1)}, bf16[1024,256]{1,0:T(8,128)(2,1)S(1)}, u32[]{:S(2)}, u32[]{:S(2)}) collective-permute-start(bf16[1024,256]{1,0:T(8,128)(2,1)S(1)} %collective-permute-done.13.refs_5_), channel_id=1, source_target_pairs={{4,12},{12,20},{20,28},{28,24},{24,16},{16,8},{8,0},{0,4},{5,13},{... | collective-permute-start | bytes 1572872 | tf_op jit(solution)/shard_map/ppermute | solution.py:399
  39.8 22.5 %collective-permute-start.4 = (bf16[1024,256]{1,0:T(8,128)(2,1)S(1)}, bf16[1024,256]{1,0:T(8,128)(2,1)S(1)}, u32[]{:S(2)}, u32[]{:S(2)}) collective-permute-start(bf16[1024,256]{1,0:T(8,128)(2,1)S(1)} %collective-permute-done.3.refs_6_), channel_id=1, source_target_pairs={{4,12},{12,20},{20,28},{28,24},{24,16},{16,8},{8,0},{0,4},{5,13},{... | collective-permute-start | bytes 1572872 | tf_op jit(solution)/shard_map/ppermute | solution.py:399
  41.8 22.5 %collective-permute-start.7 = (bf16[1024,256]{1,0:T(8,128)(2,1)S(1)}, bf16[1024,256]{1,0:T(8,128)(2,1)S(1)}, u32[]{:S(2)}, u32[]{:S(2)}) collective-permute-start(bf16[1024,256]{1,0:T(8,128)(2,1)S(1)} %collective-permute-done.6.refs_7_), channel_id=1, source_target_pairs={{12,4},{20,12},{28,20},{24,28},{16,24},{8,16},{0,8},{4,0},{13,5},{... | collective-permute-start | bytes 1572872 | tf_op jit(solution)/shard_map/ppermute | solution.py:399
  53.1 22.5 %collective-permute-start.12 = (bf16[1024,256]{1,0:T(8,128)(2,1)S(1)}, bf16[1024,256]{1,0:T(8,128)(2,1)S(1)}, u32[]{:S(2)}, u32[]{:S(2)}) collective-permute-start(bf16[1024,256]{1,0:T(8,128)(2,1)S(1)} %collective-permute-done.11.refs_8_), channel_id=1, source_target_pairs={{12,4},{20,12},{28,20},{24,28},{16,24},{8,16},{0,8},{4,0},{13,5},{... | collective-permute-start | bytes 1572872 | tf_op jit(solution)/shard_map/ppermute | solution.py:399
  53.2 22.5 %collective-permute-start.15 = (bf16[1024,256]{1,0:T(8,128)(2,1)S(1)}, bf16[1024,256]{1,0:T(8,128)(2,1)S(1)}, u32[]{:S(2)}, u32[]{:S(2)}) collective-permute-start(bf16[1024,256]{1,0:T(8,128)(2,1)S(1)} %collective-permute-done.14.refs_9_), channel_id=1, source_target_pairs={{4,12},{12,20},{20,28},{28,24},{24,16},{16,8},{8,0},{0,4},{5,13},{... | collective-permute-start | bytes 1572872 | tf_op jit(solution)/shard_map/ppermute | solution.py:399
  64.4 17.6 %collective-permute-start.16 = (bf16[768,256]{1,0:T(8,128)(2,1)S(1)}, bf16[768,256]{1,0:T(8,128)(2,1)S(1)}, u32[]{:S(2)}, u32[]{:S(2)}) collective-permute-start(bf16[768,256]{1,0:T(8,128)(2,1)S(1)} %get-tuple-element.26), channel_id=1, source_target_pairs={{4,12},{12,20},{20,28},{28,24},{24,16},{16,8},{8,0},{0,4},{5,13},{... | collective-permute-start | bytes 1179656 | tf_op jit(solution)/shard_map/ppermute | solution.py:404
  66.0 17.9 %collective-permute-start.17 = (bf16[768,256]{1,0:T(8,128)(2,1)S(1)}, bf16[768,256]{1,0:T(8,128)(2,1)S(1)}, u32[]{:S(2)}, u32[]{:S(2)}) collective-permute-start(bf16[768,256]{1,0:T(8,128)(2,1)S(1)} %get-tuple-element.27), channel_id=1, source_target_pairs={{12,4},{20,12},{28,20},{24,28},{16,24},{8,16},{0,8},{4,0},{13,5},{... | collective-permute-start | bytes 1179656 | tf_op jit(solution)/shard_map/ppermute | solution.py:404
  66.5 18.9 %collective-permute-start.8 = (bf16[256,256]{1,0:T(8,128)(2,1)S(1)}, bf16[256,256]{1,0:T(8,128)(2,1)S(1)}, u32[]{:S(2)}, u32[]{:S(2)}) collective-permute-start(bf16[256,256]{1,0:T(8,128)(2,1)S(1)} %get-tuple-element.22), channel_id=1, source_target_pairs={{4,12},{12,20},{20,28},{28,24},{24,16},{16,8},{8,0},{0,4},{5,13},{... | collective-permute-start | bytes 393224 | tf_op jit(solution)/shard_map/ppermute | solution.py:404
  75.5 9.8 %collective-permute-start.9 = (bf16[256,256]{1,0:T(8,128)(2,1)S(1)}, bf16[256,256]{1,0:T(8,128)(2,1)S(1)}, u32[]{:S(2)}, u32[]{:S(2)}) collective-permute-start(bf16[256,256]{1,0:T(8,128)(2,1)S(1)} %get-tuple-element.23), channel_id=1, source_target_pairs={{12,4},{20,12},{28,20},{24,28},{16,24},{8,16},{0,8},{4,0},{13,5},{... | collective-permute-start | bytes 393224 | tf_op jit(solution)/shard_map/ppermute | solution.py:404

commit v8 on v7

--- a/solution.py
+++ b/solution.py
@@ -12,7 +12,7 @@
 CORES = 2
 GROUPS = ((0, MI),)
 LINES = 16
-PIECES = (6, 2)
+PIECES = (5, 3)
 VMEM_LIMIT = 8 * 1024 * 1024
 
 

time: 87 us -> 86.9 us (level); the launches traced: 86.6 us -> 87.4 us
    ppermute x12, waiting for transfers between devices: 51.7 us -> 54.2 us  [body(): held[one] = lax.ppermute(held[one], 'row', ways[one[0]])]
    ppermute x4, waiting for transfers between devices: 6.18 us -> 3.94 us  [body(): lax.ppermute(part, 'row', ways[one[0]])]
  transfers between devices with their start and end apart: 18 -> 18, of which waited for: 9 -> 11; matrix products, arithmetic and copies ran while one was open for 0% -> 0% of each run, Pallas kernels for 8% -> 8%
where the time goes in v8:
time: 86.9 us; the launch traced here: 87.4 us
  waiting for transfers between devices  58.2 us (67%)
  starting transfers between devices  19.1 us (22%)
  Pallas kernels  10.1 us (12%)
    ppermute x12, waiting for transfers between devices, body(): held[one] = lax.ppermute(held[one], 'row', ways[one[0]])  54.2 us
    ppermute x12, starting transfers between devices, body(): held[one] = lax.ppermute(held[one], 'row', ways[one[0]])  12.8 us
    pallas_call x4, Pallas kernels, fold(): pl.pallas_call(functools.partial(fold_kernel, first, hops, later, order,...  7.79 us
    ppermute x4, waiting for transfers between devices, body(): lax.ppermute(part, 'row', ways[one[0]])  3.94 us
    ppermute x4, starting transfers between devices, body(): lax.ppermute(part, 'row', ways[one[0]])  3.8 us
    ppermute x1, starting transfers between devices, body(): lax.ppermute(moved, 'col', [(c, (c + shift * CORES) % n_col) for c in ran...  1.95 us
  transfers between devices with their start and end apart: 18, of which 11 were waited for; matrix products, arithmetic and copies ran while one was open for 0% of the time, Pallas kernels for 8%

profile of v8, /device:TPU:0, one launch (start us, length us, event | category | flops | bytes accessed | tf_op | source)
XLA Modules:
  0.0 87.4 jit_solution(1222489057519664066)
XLA Ops:
  0.0 1.5 %place.1 = (bf16[1024,256]{1,0:T(8,128)(2,1)S(1)}, bf16[1024,256]{1,0:T(8,128)(2,1)S(1)}, bf16[1040,256]{1,0:T(8,128)(2,1)S(1)}) custom-call(s32[2,1,4]{2,1,0:T(1,128)} %rows_hbm.1, s32[2,1,2]{2,1,0:T(1,128)} %bitcast.3, bf16[2,1,4,256,256]{4,3,2,1,0:T(8,128)(2,1)} %tiles_hbm.1, bf16[2,2,1,256,256]{4,3,2,1,0:T(8,128)(2,1)} %ints_hbm.1), custom_call_target="tpu_custom_call" | custom-call | tf_op jit(solution)/shard_map/place/pallas_call | solution.py:105
  1.5 0.5 collective-permute-start
  2.0 2.6 %collective-permute-start.2 = (bf16[1024,256]{1,0:T(8,128)(2,1)S(1)}, bf16[1024,256]{1,0:T(8,128)(2,1)S(1)}, u32[]{:S(2)}, u32[]{:S(2)}) collective-permute-start(bf16[1024,256]{1,0:T(8,128)(2,1)S(1)} %get-tuple-element.20.refs_0_), channel_id=1, source_target_pairs={{4,12},{12,20},{20,28},{28,24},{24,16},{16,8},{8,0},{0,4},{5,13},{... | collective-permute-start | bytes 1572872 | tf_op jit(solution)/shard_map/ppermute | solution.py:399
  4.6 0.2 collective-permute-start.5
  4.8 1.9 %collective-permute-start.10 = (bf16[1024,256]{1,0:T(8,128)(2,1)S(1)}, bf16[1024,256]{1,0:T(8,128)(2,1)S(1)}, u32[]{:S(2)}, u32[]{:S(2)}) collective-permute-start(bf16[1024,256]{1,0:T(8,128)(2,1)S(1)} %get-tuple-element.20.refs_0_), channel_id=1, source_target_pairs={{12,4},{20,12},{28,20},{24,28},{16,24},{8,16},{0,8},{4,0},{13,5},{... | collective-permute-start | bytes 1572872 | tf_op jit(solution)/shard_map/ppermute | solution.py:399
  6.9 2.0 %collective-permute-start.1 = (bf16[2080,256]{1,0:T(8,128)(2,1)S(1)}, bf16[2080,256]{1,0:T(8,128)(2,1)S(1)}, u32[]{:S(2)}, u32[]{:S(2)}) collective-permute-start(bf16[2080,256]{1,0:T(8,128)(2,1)S(1)} %join.1.refs_0_), channel_id=1, source_target_pairs={{0,2},{1,3},{2,0},{3,1},{4,6},{5,7},{6,4},{7,5},{8,10},{9,11},{10,... | collective-permute-start | bytes 3194888 | tf_op jit(solution)/shard_map/ppermute | solution.py:373
  8.8 8.6 %collective-permute-done.2.refs_2_ = bf16[1024,256]{1,0:T(8,128)(2,1)S(1)} collective-permute-done((bf16[1024,256]{1,0:T(8,128)(2,1)S(1)}, bf16[1024,256]{1,0:T(8,128)(2,1)S(1)}, u32[]{:S(2)}, u32[]{:S(2)}) %collective-permute-start.2) | collective-permute-done | bytes 524320 | tf_op jit(solution)/shard_map/ppermute | solution.py:399
  17.5 1.9 %collective-permute-start.3 = (bf16[1024,256]{1,0:T(8,128)(2,1)S(1)}, bf16[1024,256]{1,0:T(8,128)(2,1)S(1)}, u32[]{:S(2)}, u32[]{:S(2)}) collective-permute-start(bf16[1024,256]{1,0:T(8,128)(2,1)S(1)} %collective-permute-done.2.refs_2_), channel_id=1, source_target_pairs={{4,12},{12,20},{20,28},{28,24},{24,16},{16,8},{8,0},{0,4},{5,13},{... | collective-permute-start | bytes 1572872 | tf_op jit(solution)/shard_map/ppermute | solution.py:399
  19.4 0.1 collective-permute-start.6
  19.5 11.1 %collective-permute-done.10.refs_4_ = bf16[1024,256]{1,0:T(8,128)(2,1)S(1)} collective-permute-done((bf16[1024,256]{1,0:T(8,128)(2,1)S(1)}, bf16[1024,256]{1,0:T(8,128)(2,1)S(1)}, u32[]{:S(2)}, u32[]{:S(2)}) %collective-permute-start.10) | collective-permute-done | bytes 524320 | tf_op jit(solution)/shard_map/ppermute | solution.py:399
  30.7 1.9 %collective-permute-start.14 = (bf16[1024,256]{1,0:T(8,128)(2,1)S(1)}, bf16[1024,256]{1,0:T(8,128)(2,1)S(1)}, u32[]{:S(2)}, u32[]{:S(2)}) collective-permute-start(bf16[1024,256]{1,0:T(8,128)(2,1)S(1)} %collective-permute-done.13.refs_5_), channel_id=1, source_target_pairs={{4,12},{12,20},{20,28},{28,24},{24,16},{16,8},{8,0},{0,4},{5,13},{... | collective-permute-start | bytes 1572872 | tf_op jit(solution)/shard_map/ppermute | solution.py:399
  32.6 7.3 %collective-permute-done.3.refs_6_ = bf16[1024,256]{1,0:T(8,128)(2,1)S(1)} collective-permute-done((bf16[1024,256]{1,0:T(8,128)(2,1)S(1)}, bf16[1024,256]{1,0:T(8,128)(2,1)S(1)}, u32[]{:S(2)}, u32[]{:S(2)}) %collective-permute-start.3) | collective-permute-done | bytes 524320 | tf_op jit(solution)/shard_map/ppermute | solution.py:399
  39.9 1.9 %collective-permute-start.4 = (bf16[1024,256]{1,0:T(8,128)(2,1)S(1)}, bf16[1024,256]{1,0:T(8,128)(2,1)S(1)}, u32[]{:S(2)}, u32[]{:S(2)}) collective-permute-start(bf16[1024,256]{1,0:T(8,128)(2,1)S(1)} %collective-permute-done.3.refs_6_), channel_id=1, source_target_pairs={{4,12},{12,20},{20,28},{28,24},{24,16},{16,8},{8,0},{0,4},{5,13},{... | collective-permute-start | bytes 1572872 | tf_op jit(solution)/shard_map/ppermute | solution.py:399
  41.8 0.1 collective-permute-start.7
  42.0 11.1 %collective-permute-done.11.refs_8_ = bf16[1024,256]{1,0:T(8,128)(2,1)S(1)} collective-permute-done((bf16[1024,256]{1,0:T(8,128)(2,1)S(1)}, bf16[1024,256]{1,0:T(8,128)(2,1)S(1)}, u32[]{:S(2)}, u32[]{:S(2)}) %collective-permute-start.11) | collective-permute-done | bytes 524320 | tf_op jit(solution)/shard_map/ppermute | solution.py:399
  53.1 0.1 collective-permute-start.12
  53.2 1.9 %collective-permute-start.15 = (bf16[1024,256]{1,0:T(8,128)(2,1)S(1)}, bf16[1024,256]{1,0:T(8,128)(2,1)S(1)}, u32[]{:S(2)}, u32[]{:S(2)}) collective-permute-start(bf16[1024,256]{1,0:T(8,128)(2,1)S(1)} %collective-permute-done.14.refs_9_), channel_id=1, source_target_pairs={{4,12},{12,20},{20,28},{28,24},{24,16},{16,8},{8,0},{0,4},{5,13},{... | collective-permute-start | bytes 1572872 | tf_op jit(solution)/shard_map/ppermute | solution.py:399
  55.1 7.3 %collective-permute-done.4.refs_0_ = bf16[1024,256]{1,0:T(8,128)(2,1)S(1)} collective-permute-done((bf16[1024,256]{1,0:T(8,128)(2,1)S(1)}, bf16[1024,256]{1,0:T(8,128)(2,1)S(1)}, u32[]{:S(2)}, u32[]{:S(2)}) %collective-permute-start.4) | collective-permute-done | bytes 524320 | tf_op jit(solution)/shard_map/ppermute | solution.py:399
  62.4 1.9 %collective-permute-done.7.refs_1_ = bf16[1024,256]{1,0:T(8,128)(2,1)S(1)} collective-permute-done((bf16[1024,256]{1,0:T(8,128)(2,1)S(1)}, bf16[1024,256]{1,0:T(8,128)(2,1)S(1)}, u32[]{:S(2)}, u32[]{:S(2)}) %collective-permute-start.7) | collective-permute-done | bytes 524320 | tf_op jit(solution)/shard_map/ppermute | solution.py:399
  64.4 1.6 %collective-permute-start.16 = (bf16[640,256]{1,0:T(8,128)(2,1)S(1)}, bf16[640,256]{1,0:T(8,128)(2,1)S(1)}, u32[]{:S(2)}, u32[]{:S(2)}) collective-permute-start(bf16[640,256]{1,0:T(8,128)(2,1)S(1)} %get-tuple-element.26), channel_id=1, source_target_pairs={{4,12},{12,20},{20,28},{28,24},{24,16},{16,8},{8,0},{0,4},{5,13},{... | collective-permute-start | bytes 983048 | tf_op jit(solution)/shard_map/ppermute | solution.py:404
  66.0 0.4 collective-permute-start.17
  66.5 1.6 %collective-permute-start.8 = (bf16[384,256]{1,0:T(8,128)(2,1)S(1)}, bf16[384,256]{1,0:T(8,128)(2,1)S(1)}, u32[]{:S(2)}, u32[]{:S(2)}) collective-permute-start(bf16[384,256]{1,0:T(8,128)(2,1)S(1)} %get-tuple-element.22), channel_id=1, source_target_pairs={{4,12},{12,20},{20,28},{28,24},{24,16},{16,8},{8,0},{0,4},{5,13},{... | collective-permute-start | bytes 589832 | tf_op jit(solution)/shard_map/ppermute | solution.py:404
  68.0 0.7 collect.1
  68.7 6.8 %collective-permute-done.12.refs_2_ = bf16[1024,256]{1,0:T(8,128)(2,1)S(1)} collective-permute-done((bf16[1024,256]{1,0:T(8,128)(2,1)S(1)}, bf16[1024,256]{1,0:T(8,128)(2,1)S(1)}, u32[]{:S(2)}, u32[]{:S(2)}) %collective-permute-start.12) | collective-permute-done | bytes 524320 | tf_op jit(solution)/shard_map/ppermute | solution.py:399
  75.7 2.7 %fold.4.refs_4_ = f32[1024,1536]{1,0:T(8,128)S(1)} custom-call(s32[2,8]{1,0:T(2,128)S(4)} %get-tuple-element.18.codes_ref, bf16[2,8,256,256]{3,2,1,0:T(8,128)(2,1)S(1)} %get-tuple-element.19.ints_ref, bf16[1024,256]{1,0:T(8,128)(2,1)S(1)} %get-tuple-element.20.refs_0_, ...), custom_call_target="tpu_custom_call", output_to_operand_aliasing={{}: (12, {})} | custom-call | flops 2684354560 | bytes 6291456 | tf_op jit(solution)/shard_map/fold/pallas_call | solution.py:340
  78.4 2.0 %fold.5 = (f32[1024,1536]{1,0:T(8,128)S(1)}, f32[1024,1536]{1,0:T(8,128)}) custom-call(s32[2,8]{1,0:T(2,128)S(4)} %get-tuple-element.18.codes_ref, bf16[2,8,256,256]{3,2,1,0:T(8,128)(2,1)S(1)} %get-tuple-element.19.ints_ref, bf16[1024,256]{1,0:T(8,128)(2,1)S(1)} %collective-permute-done.4.refs_0_, ...), custom_call_target="tpu_custom_call", output_to_operand_aliasing={{0}: (6, {})} | custom-call | flops 1073741824 | bytes 6291456 | tf_op jit(solution)/shard_map/fold/pallas_call | solution.py:340
  80.4 0.2 collective-permute-done.16.refs_0_
  80.7 1.9 %collective-permute-done.17.refs_1_ = bf16[640,256]{1,0:T(8,128)(2,1)S(1)} collective-permute-done((bf16[640,256]{1,0:T(8,128)(2,1)S(1)}, bf16[640,256]{1,0:T(8,128)(2,1)S(1)}, u32[]{:S(2)}, u32[]{:S(2)}) %collective-permute-start.17) | collective-permute-done | bytes 327712 | tf_op jit(solution)/shard_map/ppermute | solution.py:404
  82.6 1.6 %fold.6.refs_3_ = f32[1024,1536]{1,0:T(8,128)} custom-call(s32[2,8]{1,0:T(2,128)S(4)} %get-tuple-element.18.codes_ref, bf16[2,8,256,256]{3,2,1,0:T(8,128)(2,1)S(1)} %get-tuple-element.19.ints_ref, bf16[640,256]{1,0:T(8,128)(2,1)S(1)} %collective-permute-done.16.refs_0_, ...), custom_call_target="tpu_custom_call", output_to_operand_aliasing={{}: (5, {})} | custom-call | flops 335544320 | bytes 3932160 | tf_op jit(solution)/shard_map/fold/pallas_call | solution.py:340
  84.2 0.4 collective-permute-done.8.refs_0_
  84.6 1.4 %collective-permute-done.9.refs_1_ = bf16[384,256]{1,0:T(8,128)(2,1)S(1)} collective-permute-done((bf16[384,256]{1,0:T(8,128)(2,1)S(1)}, bf16[384,256]{1,0:T(8,128)(2,1)S(1)}, u32[]{:S(2)}, u32[]{:S(2)}) %collective-permute-start.9) | collective-permute-done | bytes 196640 | tf_op jit(solution)/shard_map/ppermute | solution.py:404
  86.0 1.4 %fold.7 = f32[1024,1536]{1,0:T(8,128)} custom-call(s32[2,8]{1,0:T(2,128)S(4)} %get-tuple-element.18.codes_ref, bf16[2,8,256,256]{3,2,1,0:T(8,128)(2,1)S(1)} %get-tuple-element.19.ints_ref, bf16[384,256]{1,0:T(8,128)(2,1)S(1)} %collective-permute-done.8.refs_0_, bf16[384,256]{1,0:T(8,128)(2,1)S(1)} %collective-permute-done.9.refs_1_, ...), custom_call_target="tpu_custom_call", output_to_operand_aliasing={{}: (5, {})} | custom-call | flops 201326592 | bytes 2359296 | tf_op jit(solution)/shard_map/fold/pallas_call | solution.py:340
  (12 shorter events, 0.6 us)
Async XLA Ops:
  1.5 5.3 %collective-permute-start = (bf16[1040,256]{1,0:T(8,128)(2,1)S(1)}, bf16[1040,256]{1,0:T(8,128)(2,1)S(1)}, u32[]{:S(2)}, u32[]{:S(2)}) collective-permute-start(bf16[1040,256]{1,0:T(8,128)(2,1)S(1)} %get-tuple-element.17.refs_0_), channel_id=1, source_target_pairs={{0,1},{1,0},{2,3},{3,2},{4,5},{5,4},{6,7},{7,6},{8,9},{9,8},{10,11... | collective-permute-start | bytes 1597448 | tf_op jit(solution)/shard_map/ppermute | solution.py:370
  2.0 15.4 %collective-permute-start.2 = (bf16[1024,256]{1,0:T(8,128)(2,1)S(1)}, bf16[1024,256]{1,0:T(8,128)(2,1)S(1)}, u32[]{:S(2)}, u32[]{:S(2)}) collective-permute-start(bf16[1024,256]{1,0:T(8,128)(2,1)S(1)} %get-tuple-element.20.refs_0_), channel_id=1, source_target_pairs={{4,12},{12,20},{20,28},{28,24},{24,16},{16,8},{8,0},{0,4},{5,13},{... | collective-permute-start | bytes 1572872 | tf_op jit(solution)/shard_map/ppermute | solution.py:399
  4.6 14.8 %collective-permute-start.5 = (bf16[1024,256]{1,0:T(8,128)(2,1)S(1)}, bf16[1024,256]{1,0:T(8,128)(2,1)S(1)}, u32[]{:S(2)}, u32[]{:S(2)}) collective-permute-start(bf16[1024,256]{1,0:T(8,128)(2,1)S(1)} %get-tuple-element.21.refs_1_), channel_id=1, source_target_pairs={{12,4},{20,12},{28,20},{24,28},{16,24},{8,16},{0,8},{4,0},{13,5},{... | collective-permute-start | bytes 1572872 | tf_op jit(solution)/shard_map/ppermute | solution.py:399
  4.8 25.8 %collective-permute-start.10 = (bf16[1024,256]{1,0:T(8,128)(2,1)S(1)}, bf16[1024,256]{1,0:T(8,128)(2,1)S(1)}, u32[]{:S(2)}, u32[]{:S(2)}) collective-permute-start(bf16[1024,256]{1,0:T(8,128)(2,1)S(1)} %get-tuple-element.20.refs_0_), channel_id=1, source_target_pairs={{12,4},{20,12},{28,20},{24,28},{16,24},{8,16},{0,8},{4,0},{13,5},{... | collective-permute-start | bytes 1572872 | tf_op jit(solution)/shard_map/ppermute | solution.py:399
  6.7 24.0 %collective-permute-start.13 = (bf16[1024,256]{1,0:T(8,128)(2,1)S(1)}, bf16[1024,256]{1,0:T(8,128)(2,1)S(1)}, u32[]{:S(2)}, u32[]{:S(2)}) collective-permute-start(bf16[1024,256]{1,0:T(8,128)(2,1)S(1)} %get-tuple-element.21.refs_1_), channel_id=1, source_target_pairs={{4,12},{12,20},{20,28},{28,24},{24,16},{16,8},{8,0},{0,4},{5,13},{... | collective-permute-start | bytes 1572872 | tf_op jit(solution)/shard_map/ppermute | solution.py:399
  6.9 59.6 %collective-permute-start.1 = (bf16[2080,256]{1,0:T(8,128)(2,1)S(1)}, bf16[2080,256]{1,0:T(8,128)(2,1)S(1)}, u32[]{:S(2)}, u32[]{:S(2)}) collective-permute-start(bf16[2080,256]{1,0:T(8,128)(2,1)S(1)} %join.1.refs_0_), channel_id=1, source_target_pairs={{0,2},{1,3},{2,0},{3,1},{4,6},{5,7},{6,4},{7,5},{8,10},{9,11},{10,... | collective-permute-start | bytes 3194888 | tf_op jit(solution)/shard_map/ppermute | solution.py:373
  17.5 22.5 %collective-permute-start.3 = (bf16[1024,256]{1,0:T(8,128)(2,1)S(1)}, bf16[1024,256]{1,0:T(8,128)(2,1)S(1)}, u32[]{:S(2)}, u32[]{:S(2)}) collective-permute-start(bf16[1024,256]{1,0:T(8,128)(2,1)S(1)} %collective-permute-done.2.refs_2_), channel_id=1, source_target_pairs={{4,12},{12,20},{20,28},{28,24},{24,16},{16,8},{8,0},{0,4},{5,13},{... | collective-permute-start | bytes 1572872 | tf_op jit(solution)/shard_map/ppermute | solution.py:399
  19.4 22.5 %collective-permute-start.6 = (bf16[1024,256]{1,0:T(8,128)(2,1)S(1)}, bf16[1024,256]{1,0:T(8,128)(2,1)S(1)}, u32[]{:S(2)}, u32[]{:S(2)}) collective-permute-start(bf16[1024,256]{1,0:T(8,128)(2,1)S(1)} %collective-permute-done.5.refs_3_), channel_id=1, source_target_pairs={{12,4},{20,12},{28,20},{24,28},{16,24},{8,16},{0,8},{4,0},{13,5},{... | collective-permute-start | bytes 1572872 | tf_op jit(solution)/shard_map/ppermute | solution.py:399
  30.6 22.5 %collective-permute-start.11 = (bf16[1024,256]{1,0:T(8,128)(2,1)S(1)}, bf16[1024,256]{1,0:T(8,128)(2,1)S(1)}, u32[]{:S(2)}, u32[]{:S(2)}) collective-permute-start(bf16[1024,256]{1,0:T(8,128)(2,1)S(1)} %collective-permute-done.10.refs_4_), channel_id=1, source_target_pairs={{12,4},{20,12},{28,20},{24,28},{16,24},{8,16},{0,8},{4,0},{13,5},{... | collective-permute-start | bytes 1572872 | tf_op jit(solution)/shard_map/ppermute | solution.py:399
  30.7 22.5 %collective-permute-start.14 = (bf16[1024,256]{1,0:T(8,128)(2,1)S(1)}, bf16[1024,256]{1,0:T(8,128)(2,1)S(1)}, u32[]{:S(2)}, u32[]{:S(2)}) collective-permute-start(bf16[1024,256]{1,0:T(8,128)(2,1)S(1)} %collective-permute-done.13.refs_5_), channel_id=1, source_target_pairs={{4,12},{12,20},{20,28},{28,24},{24,16},{16,8},{8,0},{0,4},{5,13},{... | collective-permute-start | bytes 1572872 | tf_op jit(solution)/shard_map/ppermute | solution.py:399
  39.9 22.5 %collective-permute-start.4 = (bf16[1024,256]{1,0:T(8,128)(2,1)S(1)}, bf16[1024,256]{1,0:T(8,128)(2,1)S(1)}, u32[]{:S(2)}, u32[]{:S(2)}) collective-permute-start(bf16[1024,256]{1,0:T(8,128)(2,1)S(1)} %collective-permute-done.3.refs_6_), channel_id=1, source_target_pairs={{4,12},{12,20},{20,28},{28,24},{24,16},{16,8},{8,0},{0,4},{5,13},{... | collective-permute-start | bytes 1572872 | tf_op jit(solution)/shard_map/ppermute | solution.py:399
  41.8 22.5 %collective-permute-start.7 = (bf16[1024,256]{1,0:T(8,128)(2,1)S(1)}, bf16[1024,256]{1,0:T(8,128)(2,1)S(1)}, u32[]{:S(2)}, u32[]{:S(2)}) collective-permute-start(bf16[1024,256]{1,0:T(8,128)(2,1)S(1)} %collective-permute-done.6.refs_7_), channel_id=1, source_target_pairs={{12,4},{20,12},{28,20},{24,28},{16,24},{8,16},{0,8},{4,0},{13,5},{... | collective-permute-start | bytes 1572872 | tf_op jit(solution)/shard_map/ppermute | solution.py:399
  53.1 22.5 %collective-permute-start.12 = (bf16[1024,256]{1,0:T(8,128)(2,1)S(1)}, bf16[1024,256]{1,0:T(8,128)(2,1)S(1)}, u32[]{:S(2)}, u32[]{:S(2)}) collective-permute-start(bf16[1024,256]{1,0:T(8,128)(2,1)S(1)} %collective-permute-done.11.refs_8_), channel_id=1, source_target_pairs={{12,4},{20,12},{28,20},{24,28},{16,24},{8,16},{0,8},{4,0},{13,5},{... | collective-permute-start | bytes 1572872 | tf_op jit(solution)/shard_map/ppermute | solution.py:399
  53.2 25.2 %collective-permute-start.15 = (bf16[1024,256]{1,0:T(8,128)(2,1)S(1)}, bf16[1024,256]{1,0:T(8,128)(2,1)S(1)}, u32[]{:S(2)}, u32[]{:S(2)}) collective-permute-start(bf16[1024,256]{1,0:T(8,128)(2,1)S(1)} %collective-permute-done.14.refs_9_), channel_id=1, source_target_pairs={{4,12},{12,20},{20,28},{28,24},{24,16},{16,8},{8,0},{0,4},{5,13},{... | collective-permute-start | bytes 1572872 | tf_op jit(solution)/shard_map/ppermute | solution.py:399
  64.4 16.3 %collective-permute-start.16 = (bf16[640,256]{1,0:T(8,128)(2,1)S(1)}, bf16[640,256]{1,0:T(8,128)(2,1)S(1)}, u32[]{:S(2)}, u32[]{:S(2)}) collective-permute-start(bf16[640,256]{1,0:T(8,128)(2,1)S(1)} %get-tuple-element.26), channel_id=1, source_target_pairs={{4,12},{12,20},{20,28},{28,24},{24,16},{16,8},{8,0},{0,4},{5,13},{... | collective-permute-start | bytes 983048 | tf_op jit(solution)/shard_map/ppermute | solution.py:404
  66.0 16.6 %collective-permute-start.17 = (bf16[640,256]{1,0:T(8,128)(2,1)S(1)}, bf16[640,256]{1,0:T(8,128)(2,1)S(1)}, u32[]{:S(2)}, u32[]{:S(2)}) collective-permute-start(bf16[640,256]{1,0:T(8,128)(2,1)S(1)} %get-tuple-element.27), channel_id=1, source_target_pairs={{12,4},{20,12},{28,20},{24,28},{16,24},{8,16},{0,8},{4,0},{13,5},{... | collective-permute-start | bytes 983048 | tf_op jit(solution)/shard_map/ppermute | solution.py:404
  66.5 18.2 %collective-permute-start.8 = (bf16[384,256]{1,0:T(8,128)(2,1)S(1)}, bf16[384,256]{1,0:T(8,128)(2,1)S(1)}, u32[]{:S(2)}, u32[]{:S(2)}) collective-permute-start(bf16[384,256]{1,0:T(8,128)(2,1)S(1)} %get-tuple-element.22), channel_id=1, source_target_pairs={{4,12},{12,20},{20,28},{28,24},{24,16},{16,8},{8,0},{0,4},{5,13},{... | collective-permute-start | bytes 589832 | tf_op jit(solution)/shard_map/ppermute | solution.py:404
  75.5 10.5 %collective-permute-start.9 = (bf16[384,256]{1,0:T(8,128)(2,1)S(1)}, bf16[384,256]{1,0:T(8,128)(2,1)S(1)}, u32[]{:S(2)}, u32[]{:S(2)}) collective-permute-start(bf16[384,256]{1,0:T(8,128)(2,1)S(1)} %get-tuple-element.23), channel_id=1, source_target_pairs={{12,4},{20,12},{28,20},{24,28},{16,24},{8,16},{0,8},{4,0},{13,5},{... | collective-permute-start | bytes 589832 | tf_op jit(solution)/shard_map/ppermute | solution.py:404
